TPU v7x, 32 devices: a whole 2x2x4 slice. The times are simulated.
32 devices in a mesh: row: 4 (over y, x), col: 8 (over z, core).
Axes of the slice: x: 2, y: 2, z: 4, core: 2. Of those that a mesh axis runs over, the one named last changes fastest.
Arguments:
- ray_feat: bfloat16 [6144, 256], P(('row', 'col'))
- ray_pos: int32 [6144], P(('row', 'col')), may hold values from 0 to 6143, as said below
- target_index: int32 [6144], P(('row', 'col')), may hold values from 0 to 8191
- target_map: bfloat16 [8192, 256], replicated, may hold values from -6 to 6
Outputs:
- feature_grad: float32 [6144, 256], P(('row', 'col'))
Inputs may be any that keep to these rules, and one draw needn't show every extreme that they name: `ray_pos`: each position appears once. Cut positions into cells of 192 in order and rays into shards of 192 in order, both numbered row-major over the mesh (row, col); the ray shard of device (r, c) holds exactly 24 positions of every cell of row r and none of other rows.
All inputs are finite; a program needn't handle non-finite values.
Results may differ from a plain program's by a relative error of at most 0.0095.
Values may be sent and summed in bfloat16 or wider, within the bound.
No kernel may reach another device: no remote copies, remote signals or barrier semaphores. Data moves between devices by JAX's collectives and lax.ppermute only.
A program may use at most 64 MiB of HBM per device.

v0:
```python
import math

import jax
import jax.numpy as jnp
from jax import lax
from jax.sharding import PartitionSpec as P

normalized_exponent_heat = 0.25
epsilon = 1e-06


def normalize(values):
    as_float = values.astype(jnp.float32)
    norms = jnp.sqrt(jnp.sum(as_float * as_float, axis=1, keepdims=True) + epsilon)
    return ((as_float / norms).astype(jnp.bfloat16), norms)


def reduce_leading_dims(left, right):
    return lax.dot_general(
        left, right, (((1,), (1,)), ((), ())), preferred_element_type=jnp.float32
    )


def weight_tile(
    drawn_kinship, goal_kinship, render_sum, target_sum, blend_component, couple_multiplier
):
    likelihood_leading = drawn_kinship / render_sum
    likelihood_trailing = goal_kinship / target_sum
    return (
        couple_multiplier
        * likelihood_leading
        * (likelihood_leading - likelihood_trailing - blend_component)
        / normalized_exponent_heat
    ).astype(jnp.bfloat16)


def body(ray_feat, ray_pos, target_index, target_map):
    per_device, channels = ray_feat.shape
    col_count = lax.axis_size("col")
    row_count = lax.axis_size("row")
    send_col = ray_pos // per_device % col_count
    ordering = jnp.argsort(send_col, stable=True)
    outgoing = jnp.take(ray_feat, ordering, axis=0)
    offsets = jnp.take(ray_pos % per_device, ordering).astype(jnp.float32).astype(jnp.bfloat16)
    incoming, in_offsets = (
        lax.all_to_all(outgoing, "col", split_axis=0, concat_axis=0, tiled=True),
        lax.all_to_all(offsets, "col", split_axis=0, concat_axis=0, tiled=True),
    )
    slot_grid = lax.broadcasted_iota(jnp.float32, (per_device, per_device), 0)
    placement = (slot_grid == in_offsets.astype(jnp.float32)[None, :]).astype(jnp.bfloat16)
    cell_feats = jnp.dot(placement, incoming, preferred_element_type=jnp.float32).astype(
        jnp.bfloat16
    )
    unit_cell, cell_norm = normalize(cell_feats)
    target_cell, _ = normalize(jnp.take(target_map, target_index, axis=0))
    query_unit, query_target = (
        lax.all_gather(unit_cell, "col", axis=0, tiled=True),
        lax.all_gather(target_cell, "col", axis=0, tiled=True),
    )
    lookup_normed_directions, lookup_goal_kinship = (
        lax.all_gather(unit_cell, "row", axis=0, tiled=True),
        lax.all_gather(target_cell, "row", axis=0, tiled=True),
    )
    query_count = query_unit.shape[0]
    key_count = lookup_normed_directions.shape[0]
    block_rows = math.gcd(query_count, 512)
    block_count = query_count // block_rows
    x_blocks = query_unit.reshape(block_count, block_rows, channels)
    y_blocks = query_target.reshape(block_count, block_rows, channels)

    def affinities(leading_tile_part, trailing_tile_part):
        drawn_kinship = jnp.exp(
            reduce_leading_dims(leading_tile_part, lookup_normed_directions)
            / normalized_exponent_heat
        )
        goal_kinship = jnp.exp(
            reduce_leading_dims(trailing_tile_part, lookup_goal_kinship) / normalized_exponent_heat
        )
        return (drawn_kinship, goal_kinship)

    empty = jnp.zeros((key_count,), jnp.float32)

    def stat_pass(totals, pieces):
        drawn_kinship, goal_kinship = affinities(pieces[0], pieces[1])
        return (
            (
                totals[0] + jnp.sum(drawn_kinship, 0),
                totals[1] + jnp.sum(goal_kinship, 0),
                totals[2] + jnp.sum(drawn_kinship * drawn_kinship, 0),
                totals[3] + jnp.sum(drawn_kinship * goal_kinship, 0),
            ),
            None,
        )

    stats, _ = lax.scan(stat_pass, (empty, empty, empty, empty), (x_blocks, y_blocks))
    render_sum, target_sum, render_sq, cross_sum = lax.psum(
        (stats[0], stats[1], stats[2], stats[3]), "row"
    )
    blend_component = render_sq / (render_sum * render_sum) - cross_sum / (render_sum * target_sum)
    couple_multiplier = float(query_count * row_count) ** 2

    def grad_pass(key_part, pieces):
        drawn_kinship, goal_kinship = affinities(pieces[0], pieces[1])
        penalty_factor = weight_tile(
            drawn_kinship, goal_kinship, render_sum, target_sum, blend_component, couple_multiplier
        )
        query_piece = jnp.dot(
            penalty_factor, lookup_normed_directions, preferred_element_type=jnp.float32
        )
        key_part = key_part + lax.dot_general(
            penalty_factor, pieces[0], (((0,), (0,)), ((), ())), preferred_element_type=jnp.float32
        )
        return (key_part, query_piece)

    key_part, query_pieces = lax.scan(
        grad_pass, jnp.zeros((key_count, channels), jnp.float32), (x_blocks, y_blocks)
    )
    query_part = query_pieces.reshape(query_count, channels)
    query_total = lax.psum_scatter(query_part, "col", scatter_dimension=0, tiled=True)
    key_total = lax.psum_scatter(key_part, "row", scatter_dimension=0, tiled=True)
    gradient = query_total + key_total
    unit_float = unit_cell.astype(jnp.float32)
    return (
        gradient - unit_float * jnp.sum(unit_float * gradient, axis=1, keepdims=True)
    ) / cell_norm


def solution(mesh):
    return jax.shard_map(
        body,
        mesh=mesh,
        in_specs=(P(("row", "col"), None), P(("row", "col")), P(("row", "col")), P()),
        out_specs=P(("row", "col"), None),
        check_vma=False,
    )
```

profile of v0, /device:TPU:0, one launch (start us, length us, event | category | flops | bytes accessed | tf_op | source)
XLA Modules:
  0.0 183.2 jit_solution(3478789795324501876)
XLA Ops:
  7.3 3.2 %sort.17 = (s32[192]{0:T(256)}, s32[192]{0:T(256)S(1)}) sort(s32[192]{0:T(256)S(1)} %get-tuple-element.234, s32[192]{0:T(256)S(1)} %iota.10), dimensions={0}, to_apply=%region_0.1 | sort | flops 1536 | bytes 3072 | tf_op jit(solution)/shard_map/jit(argsort)/sort | solution.py:42
  10.5 1.6 gather_fusion
  12.8 6.3 %all-to-all-start = ((bf16[8,24,1]{1,2,0:T(2,128)(2,1)}), bf16[8,24,1]{1,2,0:T(2,128)(2,1)S(1)}, u32[]{:S(2)}, u32[]{:S(2)}) async-start(bf16[8,24,1]{1,2,0:T(2,128)(2,1)} %convert_element_type.69), calls=%async_computation | async-start | bytes 8192 | tf_op jit(solution)/shard_map/all_to_all | solution.py:47
  20.6 3.6 %gather_fusion.2 = bf16[192,256]{1,0:T(8,128)(2,1)S(1)} fusion(bf16[8192,256]{1,0:T(8,128)(2,1)} %param.11, s32[1024]{0:T(1024)S(1)} %pad_clamp_fusion), kind=kCustom, calls=%fused_computation.2 | custom fusion | bytes 197376 | tf_op jit(solution)/shard_map/jit(_take)/gather | solution.py:55
  24.5 1.0 gather_fusion.1
  25.5 16.0 %all_gather.14 = bf16[1536,256]{1,0:T(8,128)(2,1)S(1)} all-gather(bf16[192,256]{1,0:T(8,128)(2,1)S(1)} %fusion.19), channel_id=1, replica_groups=mesh['row'=4,'col'=8] {'col'}, dimensions={0}, use_global_device_ids=true | all-gather | bytes 884736 | tf_op jit(solution)/shard_map/all_gather | solution.py:58
  42.2 5.2 %all-to-all-start.1 = ((bf16[8,24,256]{2,1,0:T(8,128)(2,1)}), bf16[8,24,256]{2,1,0:T(8,128)(2,1)S(1)}, u32[]{:S(2)}, u32[]{:S(2)}) async-start(bf16[8,24,256]{2,1,0:T(8,128)(2,1)} %broadcast_select_fusion.1), calls=%async_computation.1 | async-start | bytes 196608 | tf_op jit(solution)/shard_map/all_to_all | solution.py:46
  47.5 9.6 %all_gather.15 = bf16[768,256]{1,0:T(8,128)(2,1)S(1)} all-gather(bf16[192,256]{1,0:T(8,128)(2,1)S(1)} %fusion.19), channel_id=1, replica_groups=mesh['row'=4,'col'=8] {'row'}, dimensions={0}, use_global_device_ids=true | all-gather | bytes 491520 | tf_op jit(solution)/shard_map/all_gather | solution.py:62
  57.6 10.0 %all_gather.13 = bf16[768,256]{1,0:T(8,128)(2,1)S(1)} all-gather(bf16[192,256]{1,0:T(8,128)(2,1)S(1)} %divide_convert_fusion), channel_id=1, replica_groups=mesh['row'=4,'col'=8] {'row'}, dimensions={0}, use_global_device_ids=true | all-gather | bytes 491520 | tf_op jit(solution)/shard_map/all_gather | solution.py:61
  67.6 15.9 %all_gather.12 = bf16[1536,256]{1,0:T(8,128)(2,1)S(1)} all-gather(bf16[192,256]{1,0:T(8,128)(2,1)S(1)} %divide_convert_fusion), channel_id=1, replica_groups=mesh['row'=4,'col'=8] {'col'}, dimensions={0}, use_global_device_ids=true | all-gather | bytes 884736 | tf_op jit(solution)/shard_map/all_gather | solution.py:57
  83.6 3.5 %while.30 = (s32[]{:T(128)}, f32[768]{0:T(1024)S(1)}, f32[768]{0:T(1024)S(1)}, f32[768]{0:T(1024)S(1)}, f32[768]{0:T(1024)S(1)}, /*index=5*/bf16[3,512,256]{2,1,...) while((s32[]{:T(128)}, f32[768]{0:T(1024)S(1)}, ...), condition=%wide.region_8.9_spmd.clone, body=%wide.region_3.8_spmd.clone.sunk | while | flops 405801984 | bytes 4505736 | solution.py:95
  87.1 15.0 %all-reduce = (f32[768]{0:T(1024)S(1)}, f32[768]{0:T(1024)S(1)}, f32[768]{0:T(1024)S(1)}, f32[768]{0:T(1024)S(1)}) all-reduce(f32[768]{0:T(1024)S(1)} %get-tuple-element.110, f32[768]{0:T(1024)S(1)} %get-tuple-element.111, f32[768]{0:T(1024)S(1)} %get-tuple-element.113, ...), channel_id=1, replica_groups=mesh['row'=4,'col'=8] {'row'}, use_global_device_ids=true, to_apply=%region_9.10 | all-reduce | flops 3072 | bytes 24576 | tf_op jit(solution)/shard_map/psum | solution.py:96
  102.1 9.3 %while.31 = (s32[]{:T(128)}, f32[768,256]{1,0:T(8,128)S(1)}, f32[3,512,256]{2,1,0:T(8,128)}, bf16[3,512,256]{2,1,0:T(8,128)(2,1)S(1)}, bf16[768,256]{1,0:T(8,128...) while((s32[]{:T(128)}, f32[768,256]{1,0:T(8,128)S(1)}, ...), condition=%wide.region_14.15_spmd.clone, body=%wide.region_13.14_spmd.clone.sunk | while | flops 809631744 | bytes 9580695 | solution.py:115
  102.5 0.9 multiply_convert_fusion.2
  104.0 1.2 fusion.58
  105.6 0.9 multiply_convert_fusion.2
  107.1 1.2 fusion.58
  108.6 0.9 multiply_convert_fusion.2
  110.1 1.2 fusion.58
  111.3 0.9 copy-done.1
  113.0 24.7 %reduce-scatter.5.cloned.1.call-done = f32[192,256]{1,0:T(8,128)} async-done(((f32[768,256]{1,0:T(8,128)}), f32[192,256]{1,0:T(8,128)}) %reduce-scatter.5.cloned.1.call-update) | async-done | bytes 196624 | tf_op jit(solution)/shard_map/reduce_scatter | solution.py:120
  137.7 36.6 %reduce-scatter.3.cloned.1.call-done = f32[192,256]{1,0:T(8,128)} async-done(((f32[1536,256]{1,0:T(8,128)}), f32[192,256]{1,0:T(8,128)}) %reduce-scatter.3.cloned.1.call-update) | async-done | bytes 196624 | tf_op jit(solution)/shard_map/reduce_scatter | solution.py:119
  174.3 1.2 fusion.20
  175.6 0.8 fusion.22
  (53 shorter events, 11.7 us)
Async XLA Ops:
  6.5 18.0 %copy-start = (bf16[192,256]{1,0:T(8,128)(2,1)S(1)}, bf16[192,256]{1,0:T(8,128)(2,1)}, u32[]{:S(2)}) copy-start(bf16[192,256]{1,0:T(8,128)(2,1)} %param.8) | copy-start | bytes 294916
  12.8 29.5 %all-to-all-start = ((bf16[8,24,1]{1,2,0:T(2,128)(2,1)}), bf16[8,24,1]{1,2,0:T(2,128)(2,1)S(1)}, u32[]{:S(2)}, u32[]{:S(2)}) async-start(bf16[8,24,1]{1,2,0:T(2,128)(2,1)} %convert_element_type.69), calls=%async_computation | async-start | bytes 8192 | tf_op jit(solution)/shard_map/all_to_all | solution.py:47
  42.2 15.0 %all-to-all-start.1 = ((bf16[8,24,256]{2,1,0:T(8,128)(2,1)}), bf16[8,24,256]{2,1,0:T(8,128)(2,1)S(1)}, u32[]{:S(2)}, u32[]{:S(2)}) async-start(bf16[8,24,256]{2,1,0:T(8,128)(2,1)} %broadcast_select_fusion.1), calls=%async_computation.1 | async-start | bytes 196608 | tf_op jit(solution)/shard_map/all_to_all | solution.py:46
  47.5 90.2 %reduce-scatter.5.cloned.1.call-start = ((), (), s32[]{:S(2)}) async-start(), calls=%async_computation.5 | async-start | bytes 983040 | tf_op jit(solution)/shard_map/reduce_scatter | solution.py:120
  111.3 0.9 copy-start.1
  112.2 62.1 %reduce-scatter.3.cloned.1.call-start = ((), (), s32[]{:S(2)}) async-start(), calls=%async_computation.4 | async-start | bytes 1769472 | tf_op jit(solution)/shard_map/reduce_scatter | solution.py:119
Sparse Core Ops, SparseCore 0:
  112.4 25.3 reduce-scatter.4
  140.0 34.2 reduce-scatter.2
where the time goes:
time: 184 us; the launch traced here: 183 us
  blocking collectives  66.5 us (36%)
  waiting for transfers between devices  62.1 us (34%)
  between operations  13.5 us (7%)
  matrix products  12.8 us (7%)
  starting transfers between devices  11.6 us (6%)
  other arithmetic  8.56 us (5%)
  local copies, waits for them, and re-layouts  7.94 us (4%)
    reduce_scatter x1, waiting for transfers between devices, body(): lax.psum_scatter(query_part, 'col', scatter_dimension=0, tiled=True)  36.6 us
    reduce_scatter x1, waiting for transfers between devices, body(): lax.psum_scatter(key_part, 'row', scatter_dimension=0, tiled=True)  24.7 us
    all_gather x1, blocking collectives, body(): lax.all_gather(target_cell, 'col', axis=0, tiled=True)  16 us
    all_gather x1, blocking collectives, body(): lax.all_gather(unit_cell, 'col', axis=0, tiled=True)  15.9 us
    psum x1, blocking collectives, body(): lax.psum((stats[0], stats[1], stats[2], stats[3]), 'row')  15 us
    all_gather x1, blocking collectives, body(): lax.all_gather(unit_cell, 'row', axis=0, tiled=True)  10 us
    all_gather x1, blocking collectives, body(): lax.all_gather(target_cell, 'row', axis=0, tiled=True)  9.56 us
    dot_general x12, matrix products, reduce_leading_dims(): lax.dot_general(left, right, (((1,), (1,)), ((), ())), preferred_element_...  7.08 us
  transfers between devices with their start and end apart: 4, of which 2 were waited for; matrix products, arithmetic and copies ran while one was open for 4% of the time, Pallas kernels for 0%

commit v1 on v0

v1 whole, which is shorter than its diff:
```python
import functools
import math

import jax
import jax.numpy as jnp
from jax import lax
from jax.experimental import pallas as pl
from jax.experimental.pallas import tpu as pltpu
from jax.sharding import PartitionSpec as P

HEAT = 0.25
EPSILON = 1e-06
EXTRA = 16
BASE = 128
F32 = jnp.float32
BF16 = jnp.bfloat16
VMEM = pl.BlockSpec(memory_space=pltpu.VMEM)
SMEM = pl.BlockSpec(memory_space=pltpu.SMEM)
HIGH = lax.Precision.HIGHEST


def params(mib):
    return pltpu.CompilerParams(vmem_limit_bytes=mib * 2**20)


def unit_rows(values):
    as_float = values.astype(F32)
    norms = jnp.sqrt(jnp.sum(as_float * as_float, axis=1, keepdims=True) + EPSILON)
    return (as_float * (1.0 / norms)).astype(BF16), norms


def widen(table_ref, wide_ref):
    step = math.gcd(table_ref.shape[0], 256)

    @pl.loop(0, table_ref.shape[0] // step)
    def _(i):
        rows = pl.ds(pl.multiple_of(i * step, step), step)
        wide_ref[rows, :] = table_ref[rows, :].astype(F32)


def own_target_kernel(index_ref, table_ref, out_ref, wide_ref, rows_ref):
    widen(table_ref, wide_ref)

    @pl.loop(0, out_ref.shape[0] // 8)
    def _(i):
        rows = [wide_ref[pl.ds(index_ref[i * 8 + j], 1), :] for j in range(8)]
        rows_ref[pl.ds(pl.multiple_of(i * 8, 8), 8), :] = jnp.concatenate(rows, axis=0)

    out_ref[...] = unit_rows(rows_ref[...])[0]


def pick_kernel(count, col_ref, *refs):
    blocks = refs[:count]
    unit_ref, place_ref, target_ref, cell_ref, norm_ref = refs[count:]
    per_device, channels = cell_ref.shape
    me = col_ref[0]
    slot = lax.broadcasted_iota(jnp.int32, (per_device, per_device), 0)
    cell = jnp.zeros((per_device, channels), F32)
    for i, block in enumerate(blocks):
        feats = block[0:per_device, :]
        digits = block[per_device : per_device + EXTRA, :].astype(F32).astype(jnp.int32)
        column, offset, high, low = (digits[k : k + 1, :] for k in range(4))
        place_ref[i : i + 1, :] = (column ^ me) * channels + offset
        target_ref[i : i + 1, :] = high * BASE + low
        wanted = jnp.where(column == me, offset, -1)[:, :per_device]
        chosen = jnp.where(slot == wanted, 1.0, 0.0).astype(BF16)
        cell = cell + jnp.dot(chosen, feats, preferred_element_type=F32)
        unit_ref[i * per_device : (i + 1) * per_device, :] = unit_rows(feats)[0]
    unit, norms = unit_rows(cell.astype(BF16))
    cell_ref[...] = unit
    norm_ref[...] = jnp.broadcast_to(norms, norm_ref.shape)


def query_target_kernel(place_ref, target_ref, table_ref, out_ref, wide_ref, rows_ref):
    widen(table_ref, wide_ref)
    count, channels = place_ref.shape
    per_device = out_ref.shape[0] // count
    shift = channels.bit_length() - 1

    @pl.loop(0, count)
    def _(block):
        @pl.loop(0, per_device // 8)
        def _(i):
            rows = []
            for j in range(8):
                place = place_ref[block, i * 8 + j]
                target = target_ref[place >> shift, place & (channels - 1)]
                rows.append(wide_ref[pl.ds(target, 1), :])
            start = pl.multiple_of(block * per_device + i * 8, 8)
            rows_ref[pl.ds(start, 8), :] = jnp.concatenate(rows, axis=0)

    @pl.loop(0, count)
    def _(block):
        span = pl.ds(pl.multiple_of(block * per_device, 16), per_device)
        out_ref[span, :] = unit_rows(rows_ref[span, :])[0]


def affinity(left, right):
    product = lax.dot_general(
        left, right, (((1,), (1,)), ((), ())), preferred_element_type=F32
    )
    return jnp.exp2(product * (math.log2(math.e) / HEAT))


def lanes_of(length):
    return math.gcd(length, 256)


def fold(values):
    total = values[:, :128]
    for start in range(128, values.shape[1], 128):
        total = total + values[:, start : start + 128]
    return total


def gather_keys(blocks, whole_ref):
    per_device = blocks[0].shape[0]
    for i, block in enumerate(blocks):
        whole_ref[i * per_device : (i + 1) * per_device, :] = block[...]


def stat_kernel(count, qx_ref, qy_ref, *refs):
    kx_blocks, ky_blocks = refs[:count], refs[count : 2 * count]
    key_ref, query_ref, kx_ref, ky_ref, sums_ref = refs[2 * count :]
    gather_keys(kx_blocks, kx_ref)
    gather_keys(ky_blocks, ky_ref)
    sums_ref[...] = jnp.zeros_like(sums_ref)
    lanes = lanes_of(qx_ref.shape[0])

    @pl.loop(0, qx_ref.shape[0] // lanes)
    def _(i):
        span = pl.ds(pl.multiple_of(i * lanes, lanes), lanes)
        render = affinity(kx_ref[...], qx_ref[span, :])
        target = affinity(ky_ref[...], qy_ref[span, :])
        for k, values in enumerate((render, target, render * render, render * target)):
            sums_ref[k] += fold(values)
            query_ref[k : k + 1, span] = jnp.sum(values, axis=0, keepdims=True)

    ones = jnp.ones((8, 128), F32)
    for k in range(4):
        totals = lax.dot_general(
            ones,
            sums_ref[k],
            (((1,), (1,)), ((), ())),
            precision=HIGH,
            preferred_element_type=F32,
        )
        key_ref[k : k + 1, :] = totals[0:1, :]


def factors(sums, scale):
    render, target, square, cross = (sums[k : k + 1, :] for k in range(4))
    by_render, by_target = scale / render, scale / target
    mix = (square * by_render * by_render - cross * by_render * by_target) / scale
    return by_render * by_render, by_render * by_target, by_render * mix


def reorder(values, size, flip):
    blocks = values.shape[1] // size
    return jnp.concatenate(
        [values[:, (i ^ flip) * size : ((i ^ flip) + 1) * size] for i in range(blocks)], axis=1
    )


def sum_pair_kernel(size, own_ref, other_ref, out_ref):
    out_ref[...] = own_ref[...] + reorder(other_ref[...], size, 1)


def grad_kernel(count, parts, scale, qx_ref, qy_ref, *refs):
    kx_blocks, ky_blocks = refs[:count], refs[count : 2 * count]
    refs = refs[2 * count :]
    key_sums, query_sums = refs[:count], refs[count : count + parts]
    outs = refs[count + parts : 2 * count + parts]
    kx_ref, ky_ref, key_ref, query_ref, total_ref = refs[2 * count + parts :]
    per_device = kx_blocks[0].shape[0]
    gather_keys(kx_blocks, kx_ref)
    gather_keys(ky_blocks, ky_ref)

    sums = query_sums[0][...]
    for k in range(1, parts):
        sums = sums + reorder(query_sums[k][...], 2 * per_device, k)
    for k, row in enumerate(factors(sums, scale)):
        query_ref[k : k + 1, :] = row
    sums = key_sums[0][...]
    for k in range(1, count):
        sums = sums + reorder(key_sums[k][...], per_device, k)
    for k, row in enumerate(factors(sums, scale)):
        key_ref[k] = jnp.broadcast_to(row, (128, row.shape[1])).T

    total_ref[...] = jnp.zeros_like(total_ref)
    lanes = lanes_of(qx_ref.shape[0])

    @pl.loop(0, qx_ref.shape[0] // lanes)
    def _(i):
        span = pl.ds(pl.multiple_of(i * lanes, lanes), lanes)
        queries = qx_ref[span, :]
        render = affinity(kx_ref[...], queries)
        target = affinity(ky_ref[...], qy_ref[span, :])
        weights = []
        for start in range(0, lanes, 128):
            part = slice(start, start + 128)
            at = pl.ds(pl.multiple_of(i * lanes + start, 128), 128)
            square, cross, single = (key_ref[k] + query_ref[k : k + 1, at] for k in range(3))
            a, b = render[:, part], target[:, part]
            weights.append((a * (a * square - b * cross - single)).astype(BF16))
        total_ref[...] += jnp.dot(
            jnp.concatenate(weights, axis=1), queries, preferred_element_type=F32
        )

    for k, out in enumerate(outs):
        out[...] = total_ref[k * per_device : (k + 1) * per_device, :].astype(out.dtype)


def last_kernel(unit_ref, norm_ref, *refs):
    parts, out_ref = refs[:-1], refs[-1]
    gradient = parts[0][...]
    for part in parts[1:]:
        gradient = gradient + part[...].astype(F32)
    unit = unit_ref[...].astype(F32)
    along = jnp.sum(unit * gradient, axis=1, keepdims=True)
    out_ref[...] = (gradient - unit * along) / norm_ref[:, :1]


def call(kernel, out_shape, args, in_specs=None, scratch=(), mib=16, flops=0, nbytes=0):
    many = isinstance(out_shape, (tuple, list))
    return pl.pallas_call(
        kernel,
        out_shape=out_shape,
        in_specs=in_specs or [VMEM] * len(args),
        out_specs=[VMEM] * len(out_shape) if many else VMEM,
        scratch_shapes=scratch,
        compiler_params=params(mib),
        cost_estimate=pl.CostEstimate(flops=flops, bytes_accessed=nbytes, transcendentals=0),
    )(*args)


def body(ray_feat, ray_pos, target_index, target_map):
    per_device, channels = ray_feat.shape
    col_count = lax.axis_size("col")
    row_count = lax.axis_size("row")
    shape = jax.ShapeDtypeStruct
    queries, keys = col_count * per_device, row_count * per_device

    def flip(values, axis, bits):
        pairs = [(i, i ^ bits) for i in range(lax.axis_size(axis))]
        return lax.ppermute(values, axis, pairs)

    digits = jnp.stack(
        [
            ray_pos // per_device % col_count,
            ray_pos % per_device,
            target_index // BASE,
            target_index % BASE,
        ]
    )
    digits = jnp.pad(digits, ((0, EXTRA - 4), (0, channels - per_device)))
    sent = jnp.concatenate([ray_feat, digits.astype(F32).astype(BF16)], axis=0)
    blocks = []
    for k in range(col_count // 2):
        block = flip(sent, "col", 2 * k) if k else sent
        blocks += [block, flip(block, "col", 1)]

    own_target = call(
        own_target_kernel,
        shape((per_device, channels), BF16),
        (target_index, target_map),
        in_specs=[SMEM, VMEM],
        scratch=[pltpu.VMEM(target_map.shape, F32), pltpu.VMEM((per_device, channels), F32)],
        mib=24,
        nbytes=target_map.size * 2,
    )
    key_targets = [own_target] + [flip(own_target, "row", k) for k in range(1, row_count)]

    me = lax.axis_index("col").astype(jnp.int32).reshape(1)
    query_unit, places, targets, own_unit, own_norm = call(
        functools.partial(pick_kernel, col_count),
        (
            shape((queries, channels), BF16),
            shape((col_count, channels), jnp.int32),
            shape((col_count, channels), jnp.int32),
            shape((per_device, channels), BF16),
            shape((per_device, 128), F32),
        ),
        (me, *blocks),
        in_specs=[SMEM] + [VMEM] * col_count,
        nbytes=queries * channels * 4,
    )
    key_units = [own_unit] + [flip(own_unit, "row", k) for k in range(1, row_count)]
    query_target = call(
        query_target_kernel,
        shape((queries, channels), BF16),
        (places, targets, target_map),
        in_specs=[SMEM, SMEM, VMEM],
        scratch=[pltpu.VMEM(target_map.shape, F32), pltpu.VMEM((queries, channels), F32)],
        mib=24,
        nbytes=target_map.size * 4,
    )

    flops = 2 * queries * keys * channels
    key_scratch = [pltpu.VMEM((keys, channels), BF16)] * 2
    key_sums, query_sums = call(
        functools.partial(stat_kernel, row_count),
        (shape((4, keys), F32), shape((4, queries), F32)),
        (query_unit, query_target, *key_units, *key_targets),
        scratch=key_scratch + [pltpu.VMEM((4, keys, 128), F32)],
        mib=32,
        flops=2 * flops,
    )
    key_parts = [key_sums] + [flip(key_sums, "row", k) for k in range(1, row_count)]
    query_sums = call(
        functools.partial(sum_pair_kernel, per_device),
        shape((4, queries), F32),
        (query_sums, flip(query_sums, "col", 1)),
    )
    query_parts = [query_sums] + [
        flip(query_sums, "col", 2 * k) for k in range(1, col_count // 2)
    ]
    scale = float(queries * row_count) / math.sqrt(HEAT)
    partials = call(
        functools.partial(grad_kernel, row_count, len(query_parts), scale),
        [shape((per_device, channels), F32 if k == 0 else BF16) for k in range(row_count)],
        (query_unit, query_target, *key_units, *key_targets, *key_parts, *query_parts),
        scratch=key_scratch
        + [
            pltpu.VMEM((3, keys, 128), F32),
            pltpu.VMEM((3, queries), F32),
            pltpu.VMEM((keys, channels), F32),
        ],
        mib=32,
        flops=3 * flops,
    )
    partials = [partials[0]] + [flip(partials[k], "row", k) for k in range(1, row_count)]
    return call(
        last_kernel,
        shape((per_device, channels), F32),
        (own_unit, own_norm, *partials),
    )


def solution(mesh):
    return jax.shard_map(
        body,
        mesh=mesh,
        in_specs=(P(("row", "col"), None), P(("row", "col")), P(("row", "col")), P()),
        out_specs=P(("row", "col"), None),
        check_vma=False,
    )
```

time: 184 us -> 77.2 us (0.42)
  blocking collectives: 66.5 us -> 0 us
  waiting for transfers between devices: 62.1 us -> 15.1 us
  Pallas kernels: 0 us -> 28.8 us
  starting transfers between devices: 11.6 us -> 25.5 us
  between operations: 13.5 us -> 0.12 us
  matrix products: 12.8 us -> 0 us
  other arithmetic: 8.56 us -> 2.31 us
  local copies, waits for them, and re-layouts: 7.94 us -> 5.05 us
    reduce_scatter x2 -> x0, waiting for transfers between devices: 61.3 us -> none  [the longest x1 36.6 us: body(): lax.psum_scatter(query_part, 'col', scatter_dimension=0, tiled=True)]
    all_gather x4 -> x0, blocking collectives: 51.5 us -> none  [the longest x1 16 us: body(): lax.all_gather(target_cell, 'col', axis=0, tiled=True)]
    pallas_call x0 -> x7, Pallas kernels: none -> 28.8 us  [call(): pl.pallas_call(kernel, out_shape=out_shape, in_specs=in_specs or [VMEM] *...]
    ppermute x0 -> x23, starting transfers between devices: none -> 25.5 us  [flip(): return lax.ppermute(values, axis, pairs)]
    ppermute x0 -> x23, waiting for transfers between devices: none -> 15.1 us  [flip(): return lax.ppermute(values, axis, pairs)]
    psum x1 -> x0, blocking collectives: 15 us -> none  [body(): lax.psum((stats[0], stats[1], stats[2], stats[3]), 'row')]
    dot_general x19 -> x0, matrix products: 12.8 us -> none  [the longest x12 7.08 us: reduce_leading_dims(): lax.dot_general(left, right, (((1,), (1,)), ((), ())), preferred_element_...]
    all_to_all x2 -> x0, starting transfers between devices: 11.6 us -> none  [the longest x1 6.33 us: body(): lax.all_to_all(offsets, 'col', split_axis=0, concat_axis=0, tiled=True)]
  transfers between devices with their start and end apart: 4 -> 23, of which waited for: 2 -> 7; matrix products, arithmetic and copies ran while one was open for 4% -> 0% of each run, Pallas kernels for 0% -> 23%
where the time goes in v1:
time: 77.2 us; the launch traced here: 77 us
  Pallas kernels  28.8 us (37%)
  starting transfers between devices  25.5 us (33%)
  waiting for transfers between devices  15.1 us (20%)
  local copies, waits for them, and re-layouts  5.05 us (7%)
  other arithmetic  2.31 us (3%)
    pallas_call x7, Pallas kernels, call(): pl.pallas_call(kernel, out_shape=out_shape, in_specs=in_specs or [VMEM] *...  28.8 us
    ppermute x23, starting transfers between devices, flip(): return lax.ppermute(values, axis, pairs)  25.5 us
    ppermute x23, waiting for transfers between devices, flip(): return lax.ppermute(values, axis, pairs)  15.1 us
    unnamed x6, local copies, waits for them, and re-layouts  5.05 us
  transfers between devices with their start and end apart: 23, of which 7 were waited for; matrix products, arithmetic and copies ran while one was open for 0% of the time, Pallas kernels for 23%

profile of v1, /device:TPU:0, one launch (start us, length us, event | category | flops | bytes accessed | tf_op | source)
XLA Modules:
  0.0 77.0 jit_solution(7681520490950875576)
XLA Ops:
  1.4 0.9 %pad_maximum_fusion.refs_0_ = bf16[208,256]{1,0:T(8,128)(2,1)S(1)} fusion(bf16[16,256]{1,0:T(8,128)(2,1)S(1)} %convert_convert_fusion, bf16[192,256]{1,0:T(8,128)(2,1)} %param.4), kind=kLoop, calls=%fused_computation | loop fusion | flops 212992 | bytes 212992 | tf_op jit(solution)/shard_map/concatenate | solution.py:257
  2.3 5.0 %collective-permute-start.5 = (bf16[208,256]{1,0:T(8,128)(2,1)S(1)}, bf16[208,256]{1,0:T(8,128)(2,1)S(1)}, u32[]{:S(2)}, u32[]{:S(2)}) collective-permute-start(bf16[208,256]{1,0:T(8,128)(2,1)S(1)} %pad_maximum_fusion.refs_0_), channel_id=1, source_target_pairs={{0,6},{1,7},{2,4},{3,5},{4,2},{5,3},{6,0},{7,1},{8,14},{9,15},{10,... | collective-permute-start | bytes 319496 | tf_op jit(solution)/shard_map/ppermute | solution.py:246
  8.0 3.3 %collective-permute-done.5.refs_6_ = bf16[208,256]{1,0:T(8,128)(2,1)S(1)} collective-permute-done((bf16[208,256]{1,0:T(8,128)(2,1)S(1)}, bf16[208,256]{1,0:T(8,128)(2,1)S(1)}, u32[]{:S(2)}, u32[]{:S(2)}) %collective-permute-start.5) | collective-permute-done | bytes 106528 | tf_op jit(solution)/shard_map/ppermute | solution.py:246
  11.3 5.1 %collective-permute-done.3.refs_4_ = bf16[208,256]{1,0:T(8,128)(2,1)S(1)} collective-permute-done((bf16[208,256]{1,0:T(8,128)(2,1)S(1)}, bf16[208,256]{1,0:T(8,128)(2,1)S(1)}, u32[]{:S(2)}, u32[]{:S(2)}) %collective-permute-start.3) | collective-permute-done | bytes 106528 | tf_op jit(solution)/shard_map/ppermute | solution.py:246
  16.9 2.2 %copy-done = bf16[8192,256]{1,0:T(8,128)(2,1)S(1)} copy-done((bf16[8192,256]{1,0:T(8,128)(2,1)S(1)}, bf16[8192,256]{1,0:T(8,128)(2,1)}, u32[]{:S(2)}) %copy-start) | copy-done | bytes 4194328
  19.7 1.8 %shard_map.48.refs_4_ = bf16[192,256]{1,0:T(8,128)(2,1)S(1)} custom-call(s32[192]{0:T(256)S(1)} %copy-done.2, bf16[8192,256]{1,0:T(8,128)(2,1)S(1)} %copy-done), custom_call_target="tpu_custom_call" | custom-call | bytes 4194304 | tf_op jit(solution)/shard_map/pallas_call | solution.py:226
  21.5 2.5 %collective-permute-start.12 = (bf16[192,256]{1,0:T(8,128)(2,1)S(1)}, bf16[192,256]{1,0:T(8,128)(2,1)S(1)}, u32[]{:S(2)}, u32[]{:S(2)}) collective-permute-start(bf16[192,256]{1,0:T(8,128)(2,1)S(1)} %shard_map.48.refs_4_), channel_id=1, source_target_pairs={{0,24},{8,16},{16,8},{24,0},{1,25},{9,17},{17,9},{25,1},{2,26},{10... | collective-permute-start | bytes 294920 | tf_op jit(solution)/shard_map/ppermute | solution.py:246
  25.1 0.8 %shard_map.46 = (bf16[1536,256]{1,0:T(8,128)(2,1)S(1)}, s32[8,256]{1,0:T(8,128)S(1)}, s32[8,256]{1,0:T(8,128)S(1)}, bf16[192,256]{1,0:T(8,128)(2,1)S(1)}, f32[192,128]{1,0:T(8,128)S(1)}) custom-call(s32[1]{0:T(128)} %bitcast.col_ref, bf16[208,256]{1,0:T(8,128)(2,1)S(1)} %pad_maximum_fusion.refs_0_, bf16[208,256]{1,0:T(8,128)(2,1)S(1)} %collective-permute-done.refs_1_, ...), custom_call_target="tpu_custom_call" | custom-call | bytes 1572864 | tf_op jit(solution)/shard_map/pallas_call | solution.py:226
  25.9 2.5 %collective-permute-start.9 = (bf16[192,256]{1,0:T(8,128)(2,1)S(1)}, bf16[192,256]{1,0:T(8,128)(2,1)S(1)}, u32[]{:S(2)}, u32[]{:S(2)}) collective-permute-start(bf16[192,256]{1,0:T(8,128)(2,1)S(1)} %get-tuple-element.16.refs_0_.unit_ref), channel_id=1, source_target_pairs={{0,24},{8,16},{16,8},{24,0},{1,25},{9,17},{17,9},{25,1},{2,26},{10... | collective-permute-start | bytes 294920 | tf_op jit(solution)/shard_map/ppermute | solution.py:246
  29.5 2.2 %copy-done.1 = bf16[8192,256]{1,0:T(8,128)(2,1)S(1)} copy-done((bf16[8192,256]{1,0:T(8,128)(2,1)S(1)}, bf16[8192,256]{1,0:T(8,128)(2,1)}, u32[]{:S(2)}) %copy-start.1) | copy-done | bytes 4194328
  31.7 15.1 %shard_map.47.qy_ref = bf16[1536,256]{1,0:T(8,128)(2,1)S(1)} custom-call(s32[8,256]{1,0:T(8,128)S(1)} %get-tuple-element.19.place_ref, s32[8,256]{1,0:T(8,128)S(1)} %get-tuple-element.20.target_ref, bf16[8192,256]{1,0:T(8,128)(2,1)S(1)} %copy-done.1), custom_call_target="tpu_custom_call" | custom-call | bytes 8388608 | tf_op jit(solution)/shard_map/pallas_call | solution.py:226
  46.8 5.5 %shard_map.49 = (f32[4,768]{1,0:T(4,128)S(1)}, f32[4,1536]{1,0:T(4,128)S(1)}) custom-call(bf16[1536,256]{1,0:T(8,128)(2,1)S(1)} %get-tuple-element.18.qx_ref, bf16[1536,256]{1,0:T(8,128)(2,1)S(1)} %shard_map.47.qy_ref, bf16[192,256]{1,0:T(8,128)(2,1)S(1)} %get-tuple-element.16.refs_0_.unit_ref, bf16[192,256]{1,0:T(8,128)(2,1)S(1)} %collective-permute-done.7.refs_1_, ...), custom_call_target="tpu_custom_call" | custom-call | flops 1207959552 | tf_op jit(solution)/shard_map/pallas_call | solution.py:226
  52.3 2.5 %collective-permute-start.15 = (f32[4,768]{1,0:T(4,128)S(1)}, f32[4,768]{1,0:T(4,128)S(1)}, u32[]{:S(2)}, u32[]{:S(2)}) collective-permute-start(f32[4,768]{1,0:T(4,128)S(1)} %get-tuple-element.21.refs_8_), channel_id=1, source_target_pairs={{0,24},{8,16},{16,8},{24,0},{1,25},{9,17},{17,9},{25,1},{2,26},{10... | collective-permute-start | bytes 36872 | tf_op jit(solution)/shard_map/ppermute | solution.py:246
  54.9 2.5 %collective-permute-start.19 = (f32[4,1536]{1,0:T(4,128)S(1)}, f32[4,1536]{1,0:T(4,128)S(1)}, u32[]{:S(2)}, u32[]{:S(2)}) collective-permute-start(f32[4,1536]{1,0:T(4,128)S(1)} %shard_map.50.refs_12_), channel_id=1, source_target_pairs={{0,6},{1,7},{2,4},{3,5},{4,2},{5,3},{6,0},{7,1},{8,14},{9,15},{10,... | collective-permute-start | bytes 73736 | tf_op jit(solution)/shard_map/ppermute | solution.py:246
  57.4 1.9 %collective-permute-start.17 = (f32[4,1536]{1,0:T(4,128)S(1)}, f32[4,1536]{1,0:T(4,128)S(1)}, u32[]{:S(2)}, u32[]{:S(2)}) collective-permute-start(f32[4,1536]{1,0:T(4,128)S(1)} %shard_map.50.refs_12_), channel_id=1, source_target_pairs={{0,2},{1,3},{2,0},{3,1},{4,6},{5,7},{6,4},{7,5},{8,10},{9,11},{10,... | collective-permute-start | bytes 73736 | tf_op jit(solution)/shard_map/ppermute | solution.py:246
  59.8 1.2 %collective-permute-start.13 = (f32[4,768]{1,0:T(4,128)S(1)}, f32[4,768]{1,0:T(4,128)S(1)}, u32[]{:S(2)}, u32[]{:S(2)}) collective-permute-start(f32[4,768]{1,0:T(4,128)S(1)} %get-tuple-element.21.refs_8_), channel_id=1, source_target_pairs={{0,8},{8,0},{16,24},{24,16},{1,9},{9,1},{17,25},{25,17},{2,10},{10... | collective-permute-start | bytes 36872 | tf_op jit(solution)/shard_map/ppermute | solution.py:246
  61.0 2.0 %collective-permute-done.14.refs_10_ = f32[4,768]{1,0:T(4,128)S(1)} collective-permute-done((f32[4,768]{1,0:T(4,128)S(1)}, f32[4,768]{1,0:T(4,128)S(1)}, u32[]{:S(2)}, u32[]{:S(2)}) %collective-permute-start.14) | collective-permute-done | bytes 12320 | tf_op jit(solution)/shard_map/ppermute | solution.py:246
  63.5 4.7 %shard_map.51 = (f32[192,256]{1,0:T(8,128)S(1)}, bf16[192,256]{1,0:T(8,128)(2,1)S(1)}, bf16[192,256]{1,0:T(8,128)(2,1)S(1)}, bf16[192,256]{1,0:T(8,128)(2,1)S(1)}) custom-call(bf16[1536,256]{1,0:T(8,128)(2,1)S(1)} %get-tuple-element.18.qx_ref, bf16[1536,256]{1,0:T(8,128)(2,1)S(1)} %shard_map.47.qy_ref, ...), custom_call_target="tpu_custom_call" | custom-call | flops 1811939328 | tf_op jit(solution)/shard_map/pallas_call | solution.py:226
  68.3 1.3 %collective-permute-start.20 = (bf16[192,256]{1,0:T(8,128)(2,1)S(1)}, bf16[192,256]{1,0:T(8,128)(2,1)S(1)}, u32[]{:S(2)}, u32[]{:S(2)}) collective-permute-start(bf16[192,256]{1,0:T(8,128)(2,1)S(1)} %get-tuple-element.24), channel_id=1, source_target_pairs={{0,8},{8,0},{16,24},{24,16},{1,9},{9,1},{17,25},{25,17},{2,10},{10... | collective-permute-start | bytes 294920 | tf_op jit(solution)/shard_map/ppermute | solution.py:246
  69.5 1.1 %collective-permute-start.21 = (bf16[192,256]{1,0:T(8,128)(2,1)S(1)}, bf16[192,256]{1,0:T(8,128)(2,1)S(1)}, u32[]{:S(2)}, u32[]{:S(2)}) collective-permute-start(bf16[192,256]{1,0:T(8,128)(2,1)S(1)} %get-tuple-element.25), channel_id=1, source_target_pairs={{0,16},{8,24},{16,0},{24,8},{1,17},{9,25},{17,1},{25,9},{2,18},{10... | collective-permute-start | bytes 294920 | tf_op jit(solution)/shard_map/ppermute | solution.py:246
  70.6 1.2 %collective-permute-start.22 = (bf16[192,256]{1,0:T(8,128)(2,1)S(1)}, bf16[192,256]{1,0:T(8,128)(2,1)S(1)}, u32[]{:S(2)}, u32[]{:S(2)}) collective-permute-start(bf16[192,256]{1,0:T(8,128)(2,1)S(1)} %get-tuple-element.26), channel_id=1, source_target_pairs={{0,24},{8,16},{16,8},{24,0},{1,25},{9,17},{17,9},{25,1},{2,26},{10... | collective-permute-start | bytes 294920 | tf_op jit(solution)/shard_map/ppermute | solution.py:246
  71.8 1.5 %collective-permute-done.20.refs_1_ = bf16[192,256]{1,0:T(8,128)(2,1)S(1)} collective-permute-done((bf16[192,256]{1,0:T(8,128)(2,1)S(1)}, bf16[192,256]{1,0:T(8,128)(2,1)S(1)}, u32[]{:S(2)}, u32[]{:S(2)}) %collective-permute-start.20) | collective-permute-done | bytes 98336 | tf_op jit(solution)/shard_map/ppermute | solution.py:246
  74.2 2.0 %collective-permute-done.22.refs_3_ = bf16[192,256]{1,0:T(8,128)(2,1)S(1)} collective-permute-done((bf16[192,256]{1,0:T(8,128)(2,1)S(1)}, bf16[192,256]{1,0:T(8,128)(2,1)S(1)}, u32[]{:S(2)}, u32[]{:S(2)}) %collective-permute-start.22) | collective-permute-done | bytes 98336 | tf_op jit(solution)/shard_map/ppermute | solution.py:246
  76.1 0.9 %shard_map.52 = f32[192,256]{1,0:T(8,128)} custom-call(bf16[192,256]{1,0:T(8,128)(2,1)S(1)} %get-tuple-element.16.refs_0_.unit_ref, f32[192,128]{1,0:T(8,128)S(1)} %get-tuple-element.17.norm_ref, f32[192,256]{1,0:T(8,128)S(1)} %get-tuple-element.23.refs_0_, bf16[192,256]{1,0:T(8,128)(2,1)S(1)} %collective-permute-done.20.refs_1_, ...), custom_call_target="tpu_custom_call" | custom-call | tf_op jit(solution)/shard_map/pallas_call | solution.py:226
  (40 shorter events, 7.3 us)
Async XLA Ops:
  2.3 8.9 %collective-permute-start.5 = (bf16[208,256]{1,0:T(8,128)(2,1)S(1)}, bf16[208,256]{1,0:T(8,128)(2,1)S(1)}, u32[]{:S(2)}, u32[]{:S(2)}) collective-permute-start(bf16[208,256]{1,0:T(8,128)(2,1)S(1)} %pad_maximum_fusion.refs_0_), channel_id=1, source_target_pairs={{0,6},{1,7},{2,4},{3,5},{4,2},{5,3},{6,0},{7,1},{8,14},{9,15},{10,... | collective-permute-start | bytes 319496 | tf_op jit(solution)/shard_map/ppermute | solution.py:246
  7.4 9.0 %collective-permute-start.3 = (bf16[208,256]{1,0:T(8,128)(2,1)S(1)}, bf16[208,256]{1,0:T(8,128)(2,1)S(1)}, u32[]{:S(2)}, u32[]{:S(2)}) collective-permute-start(bf16[208,256]{1,0:T(8,128)(2,1)S(1)} %pad_maximum_fusion.refs_0_), channel_id=1, source_target_pairs={{0,4},{1,5},{2,6},{3,7},{4,0},{5,1},{6,2},{7,3},{8,12},{9,13},{10,... | collective-permute-start | bytes 319496 | tf_op jit(solution)/shard_map/ppermute | solution.py:246
  7.4 9.0 %collective-permute-start.1 = (bf16[208,256]{1,0:T(8,128)(2,1)S(1)}, bf16[208,256]{1,0:T(8,128)(2,1)S(1)}, u32[]{:S(2)}, u32[]{:S(2)}) collective-permute-start(bf16[208,256]{1,0:T(8,128)(2,1)S(1)} %pad_maximum_fusion.refs_0_), channel_id=1, source_target_pairs={{0,2},{1,3},{2,0},{3,1},{4,6},{5,7},{6,4},{7,5},{8,10},{9,11},{10,... | collective-permute-start | bytes 319496 | tf_op jit(solution)/shard_map/ppermute | solution.py:246
  8.0 16.0 %collective-permute-start = (bf16[208,256]{1,0:T(8,128)(2,1)S(1)}, bf16[208,256]{1,0:T(8,128)(2,1)S(1)}, u32[]{:S(2)}, u32[]{:S(2)}) collective-permute-start(bf16[208,256]{1,0:T(8,128)(2,1)S(1)} %pad_maximum_fusion.refs_0_), channel_id=1, source_target_pairs={{0,1},{1,0},{2,3},{3,2},{4,5},{5,4},{6,7},{7,6},{8,9},{9,8},{10,11... | collective-permute-start | bytes 319496 | tf_op jit(solution)/shard_map/ppermute | solution.py:246
  11.3 13.3 %collective-permute-start.6 = (bf16[208,256]{1,0:T(8,128)(2,1)S(1)}, bf16[208,256]{1,0:T(8,128)(2,1)S(1)}, u32[]{:S(2)}, u32[]{:S(2)}) collective-permute-start(bf16[208,256]{1,0:T(8,128)(2,1)S(1)} %collective-permute-done.5.refs_6_), channel_id=1, source_target_pairs={{0,1},{1,0},{2,3},{3,2},{4,5},{5,4},{6,7},{7,6},{8,9},{9,8},{10,11... | collective-permute-start | bytes 319496 | tf_op jit(solution)/shard_map/ppermute | solution.py:246
  16.3 8.8 %collective-permute-start.4 = (bf16[208,256]{1,0:T(8,128)(2,1)S(1)}, bf16[208,256]{1,0:T(8,128)(2,1)S(1)}, u32[]{:S(2)}, u32[]{:S(2)}) collective-permute-start(bf16[208,256]{1,0:T(8,128)(2,1)S(1)} %collective-permute-done.3.refs_4_), channel_id=1, source_target_pairs={{0,1},{1,0},{2,3},{3,2},{4,5},{5,4},{6,7},{7,6},{8,9},{9,8},{10,11... | collective-permute-start | bytes 319496 | tf_op jit(solution)/shard_map/ppermute | solution.py:246
  16.3 8.7 %collective-permute-start.2 = (bf16[208,256]{1,0:T(8,128)(2,1)S(1)}, bf16[208,256]{1,0:T(8,128)(2,1)S(1)}, u32[]{:S(2)}, u32[]{:S(2)}) collective-permute-start(bf16[208,256]{1,0:T(8,128)(2,1)S(1)} %collective-permute-done.1.refs_2_), channel_id=1, source_target_pairs={{0,1},{1,0},{2,3},{3,2},{4,5},{5,4},{6,7},{7,6},{8,9},{9,8},{10,11... | collective-permute-start | bytes 319496 | tf_op jit(solution)/shard_map/ppermute | solution.py:246
  21.5 7.4 %collective-permute-start.12 = (bf16[192,256]{1,0:T(8,128)(2,1)S(1)}, bf16[192,256]{1,0:T(8,128)(2,1)S(1)}, u32[]{:S(2)}, u32[]{:S(2)}) collective-permute-start(bf16[192,256]{1,0:T(8,128)(2,1)S(1)} %shard_map.48.refs_4_), channel_id=1, source_target_pairs={{0,24},{8,16},{16,8},{24,0},{1,25},{9,17},{17,9},{25,1},{2,26},{10... | collective-permute-start | bytes 294920 | tf_op jit(solution)/shard_map/ppermute | solution.py:246
  24.0 22.7 %collective-permute-start.11 = (bf16[192,256]{1,0:T(8,128)(2,1)S(1)}, bf16[192,256]{1,0:T(8,128)(2,1)S(1)}, u32[]{:S(2)}, u32[]{:S(2)}) collective-permute-start(bf16[192,256]{1,0:T(8,128)(2,1)S(1)} %shard_map.48.refs_4_), channel_id=1, source_target_pairs={{0,16},{8,24},{16,0},{24,8},{1,17},{9,25},{17,1},{25,9},{2,18},{10... | collective-permute-start | bytes 294920 | tf_op jit(solution)/shard_map/ppermute | solution.py:246
  24.5 22.2 %collective-permute-start.10 = (bf16[192,256]{1,0:T(8,128)(2,1)S(1)}, bf16[192,256]{1,0:T(8,128)(2,1)S(1)}, u32[]{:S(2)}, u32[]{:S(2)}) collective-permute-start(bf16[192,256]{1,0:T(8,128)(2,1)S(1)} %shard_map.48.refs_4_), channel_id=1, source_target_pairs={{0,8},{8,0},{16,24},{24,16},{1,9},{9,1},{17,25},{25,17},{2,10},{10... | collective-permute-start | bytes 294920 | tf_op jit(solution)/shard_map/ppermute | solution.py:246
  25.9 20.8 %collective-permute-start.9 = (bf16[192,256]{1,0:T(8,128)(2,1)S(1)}, bf16[192,256]{1,0:T(8,128)(2,1)S(1)}, u32[]{:S(2)}, u32[]{:S(2)}) collective-permute-start(bf16[192,256]{1,0:T(8,128)(2,1)S(1)} %get-tuple-element.16.refs_0_.unit_ref), channel_id=1, source_target_pairs={{0,24},{8,16},{16,8},{24,0},{1,25},{9,17},{17,9},{25,1},{2,26},{10... | collective-permute-start | bytes 294920 | tf_op jit(solution)/shard_map/ppermute | solution.py:246
  28.4 18.3 %collective-permute-start.8 = (bf16[192,256]{1,0:T(8,128)(2,1)S(1)}, bf16[192,256]{1,0:T(8,128)(2,1)S(1)}, u32[]{:S(2)}, u32[]{:S(2)}) collective-permute-start(bf16[192,256]{1,0:T(8,128)(2,1)S(1)} %get-tuple-element.16.refs_0_.unit_ref), channel_id=1, source_target_pairs={{0,16},{8,24},{16,0},{24,8},{1,17},{9,25},{17,1},{25,9},{2,18},{10... | collective-permute-start | bytes 294920 | tf_op jit(solution)/shard_map/ppermute | solution.py:246
  28.9 17.8 %collective-permute-start.7 = (bf16[192,256]{1,0:T(8,128)(2,1)S(1)}, bf16[192,256]{1,0:T(8,128)(2,1)S(1)}, u32[]{:S(2)}, u32[]{:S(2)}) collective-permute-start(bf16[192,256]{1,0:T(8,128)(2,1)S(1)} %get-tuple-element.16.refs_0_.unit_ref), channel_id=1, source_target_pairs={{0,8},{8,0},{16,24},{24,16},{1,9},{9,1},{17,25},{25,17},{2,10},{10... | collective-permute-start | bytes 294920 | tf_op jit(solution)/shard_map/ppermute | solution.py:246
  29.5 2.2 %copy-start.1 = (bf16[8192,256]{1,0:T(8,128)(2,1)S(1)}, bf16[8192,256]{1,0:T(8,128)(2,1)}, u32[]{:S(2)}) copy-start(bf16[8192,256]{1,0:T(8,128)(2,1)} %table_ref.3) | copy-start | bytes 12582916
  52.2 2.5 %collective-permute-start.16 = (f32[4,1536]{1,0:T(4,128)S(1)}, f32[4,1536]{1,0:T(4,128)S(1)}, u32[]{:S(2)}, u32[]{:S(2)}) collective-permute-start(f32[4,1536]{1,0:T(4,128)S(1)} %get-tuple-element.22.own_ref), channel_id=1, source_target_pairs={{0,1},{1,0},{2,3},{3,2},{4,5},{5,4},{6,7},{7,6},{8,9},{9,8},{10,11... | collective-permute-start | bytes 73736 | tf_op jit(solution)/shard_map/ppermute | solution.py:246
  52.3 7.6 %collective-permute-start.15 = (f32[4,768]{1,0:T(4,128)S(1)}, f32[4,768]{1,0:T(4,128)S(1)}, u32[]{:S(2)}, u32[]{:S(2)}) collective-permute-start(f32[4,768]{1,0:T(4,128)S(1)} %get-tuple-element.21.refs_8_), channel_id=1, source_target_pairs={{0,24},{8,16},{16,8},{24,0},{1,25},{9,17},{17,9},{25,1},{2,26},{10... | collective-permute-start | bytes 36872 | tf_op jit(solution)/shard_map/ppermute | solution.py:246
  54.9 8.7 %collective-permute-start.19 = (f32[4,1536]{1,0:T(4,128)S(1)}, f32[4,1536]{1,0:T(4,128)S(1)}, u32[]{:S(2)}, u32[]{:S(2)}) collective-permute-start(f32[4,1536]{1,0:T(4,128)S(1)} %shard_map.50.refs_12_), channel_id=1, source_target_pairs={{0,6},{1,7},{2,4},{3,5},{4,2},{5,3},{6,0},{7,1},{8,14},{9,15},{10,... | collective-permute-start | bytes 73736 | tf_op jit(solution)/shard_map/ppermute | solution.py:246
  57.4 6.1 %collective-permute-start.18 = (f32[4,1536]{1,0:T(4,128)S(1)}, f32[4,1536]{1,0:T(4,128)S(1)}, u32[]{:S(2)}, u32[]{:S(2)}) collective-permute-start(f32[4,1536]{1,0:T(4,128)S(1)} %shard_map.50.refs_12_), channel_id=1, source_target_pairs={{0,4},{1,5},{2,6},{3,7},{4,0},{5,1},{6,2},{7,3},{8,12},{9,13},{10,... | collective-permute-start | bytes 73736 | tf_op jit(solution)/shard_map/ppermute | solution.py:246
  57.4 6.1 %collective-permute-start.17 = (f32[4,1536]{1,0:T(4,128)S(1)}, f32[4,1536]{1,0:T(4,128)S(1)}, u32[]{:S(2)}, u32[]{:S(2)}) collective-permute-start(f32[4,1536]{1,0:T(4,128)S(1)} %shard_map.50.refs_12_), channel_id=1, source_target_pairs={{0,2},{1,3},{2,0},{3,1},{4,6},{5,7},{6,4},{7,5},{8,10},{9,11},{10,... | collective-permute-start | bytes 73736 | tf_op jit(solution)/shard_map/ppermute | solution.py:246
  59.3 3.7 %collective-permute-start.14 = (f32[4,768]{1,0:T(4,128)S(1)}, f32[4,768]{1,0:T(4,128)S(1)}, u32[]{:S(2)}, u32[]{:S(2)}) collective-permute-start(f32[4,768]{1,0:T(4,128)S(1)} %get-tuple-element.21.refs_8_), channel_id=1, source_target_pairs={{0,16},{8,24},{16,0},{24,8},{1,17},{9,25},{17,1},{25,9},{2,18},{10... | collective-permute-start | bytes 36872 | tf_op jit(solution)/shard_map/ppermute | solution.py:246
  59.8 3.7 %collective-permute-start.13 = (f32[4,768]{1,0:T(4,128)S(1)}, f32[4,768]{1,0:T(4,128)S(1)}, u32[]{:S(2)}, u32[]{:S(2)}) collective-permute-start(f32[4,768]{1,0:T(4,128)S(1)} %get-tuple-element.21.refs_8_), channel_id=1, source_target_pairs={{0,8},{8,0},{16,24},{24,16},{1,9},{9,1},{17,25},{25,17},{2,10},{10... | collective-permute-start | bytes 36872 | tf_op jit(solution)/shard_map/ppermute | solution.py:246
  68.3 5.0 %collective-permute-start.20 = (bf16[192,256]{1,0:T(8,128)(2,1)S(1)}, bf16[192,256]{1,0:T(8,128)(2,1)S(1)}, u32[]{:S(2)}, u32[]{:S(2)}) collective-permute-start(bf16[192,256]{1,0:T(8,128)(2,1)S(1)} %get-tuple-element.24), channel_id=1, source_target_pairs={{0,8},{8,0},{16,24},{24,16},{1,9},{9,1},{17,25},{25,17},{2,10},{10... | collective-permute-start | bytes 294920 | tf_op jit(solution)/shard_map/ppermute | solution.py:246
  69.5 4.6 %collective-permute-start.21 = (bf16[192,256]{1,0:T(8,128)(2,1)S(1)}, bf16[192,256]{1,0:T(8,128)(2,1)S(1)}, u32[]{:S(2)}, u32[]{:S(2)}) collective-permute-start(bf16[192,256]{1,0:T(8,128)(2,1)S(1)} %get-tuple-element.25), channel_id=1, source_target_pairs={{0,16},{8,24},{16,0},{24,8},{1,17},{9,25},{17,1},{25,9},{2,18},{10... | collective-permute-start | bytes 294920 | tf_op jit(solution)/shard_map/ppermute | solution.py:246
  70.6 5.5 %collective-permute-start.22 = (bf16[192,256]{1,0:T(8,128)(2,1)S(1)}, bf16[192,256]{1,0:T(8,128)(2,1)S(1)}, u32[]{:S(2)}, u32[]{:S(2)}) collective-permute-start(bf16[192,256]{1,0:T(8,128)(2,1)S(1)} %get-tuple-element.26), channel_id=1, source_target_pairs={{0,24},{8,16},{16,8},{24,0},{1,25},{9,17},{17,9},{25,1},{2,26},{10... | collective-permute-start | bytes 294920 | tf_op jit(solution)/shard_map/ppermute | solution.py:246
  (2 other events, 2.9 us)

commit v2 on v1

--- a/solution.py
+++ b/solution.py
@@ -11,11 +11,15 @@
 HEAT = 0.25
 EPSILON = 1e-06
 EXTRA = 16
-BASE = 128
+BASE_BITS = 7
+BASE = 1 << BASE_BITS
 F32 = jnp.float32
 BF16 = jnp.bfloat16
 VMEM = pl.BlockSpec(memory_space=pltpu.VMEM)
 SMEM = pl.BlockSpec(memory_space=pltpu.SMEM)
+HBM = pl.BlockSpec(memory_space=pltpu.HBM)
+FULL = 60
+PIECES = 8
 HIGH = lax.Precision.HIGHEST
 
 
@@ -29,70 +33,124 @@
     return (as_float * (1.0 / norms)).astype(BF16), norms
 
 
-def widen(table_ref, wide_ref):
-    step = math.gcd(table_ref.shape[0], 256)
-
-    @pl.loop(0, table_ref.shape[0] // step)
+def table_scratch(table, rows):
+    half = table.shape[1] // 2
+    return [
+        pltpu.VMEM(table.shape, BF16),
+        pltpu.VMEM((2 * table.shape[0], half), F32),
+        pltpu.VMEM((2 * rows, half), F32),
+        pltpu.SemaphoreType.DMA((PIECES,)),
+    ]
+
+
+def load_table(table_ref, narrow_ref, wide_ref, sems):
+    size = table_ref.shape[0] // PIECES
+    half = table_ref.shape[1] // 2
+
+    def copy(i):
+        rows = pl.ds(i * size, size)
+        return pltpu.make_async_copy(table_ref.at[rows, :], narrow_ref.at[rows, :], sems.at[i])
+
+    for i in range(PIECES):
+        copy(i).start()
+    step = math.gcd(size, 256)
+    for i in range(PIECES):
+        copy(i).wait()
+
+        @pl.loop(i * (size // step), (i + 1) * (size // step))
+        def _(j):
+            start = pl.multiple_of(j * step, step)
+            values = narrow_ref[pl.ds(start, step), :].astype(F32)
+            wide_ref[pl.ds(start * 2, step, 2), :] = values[:, :half]
+            wide_ref[pl.ds(start * 2 + 1, step, 2), :] = values[:, half:]
+
+
+def take_rows(index, start, count, wide_ref, rows_ref):
+    @pl.loop(0, count // 32)
     def _(i):
-        rows = pl.ds(pl.multiple_of(i * step, step), step)
-        wide_ref[rows, :] = table_ref[rows, :].astype(F32)
-
-
-def own_target_kernel(index_ref, table_ref, out_ref, wide_ref, rows_ref):
-    widen(table_ref, wide_ref)
-
-    @pl.loop(0, out_ref.shape[0] // 8)
-    def _(i):
-        rows = [wide_ref[pl.ds(index_ref[i * 8 + j], 1), :] for j in range(8)]
-        rows_ref[pl.ds(pl.multiple_of(i * 8, 8), 8), :] = jnp.concatenate(rows, axis=0)
-
-    out_ref[...] = unit_rows(rows_ref[...])[0]
-
-
-def pick_kernel(count, col_ref, *refs):
+        for group in range(8):
+            first = i * 32 + group * 4
+            rows = [wide_ref[pl.ds(index(first + j) * 2, 2), :] for j in range(4)]
+            at = pl.multiple_of(start * 2 + first * 2, 8)
+            rows_ref[pl.ds(at, 8), :] = jnp.concatenate(rows, axis=0)
+
+
+def unit_taken(rows_ref, out_ref):
+    rows, half = out_ref.shape[0], out_ref.shape[1] // 2
+    step = math.gcd(rows, 64)
+    for start in range(0, rows, step):
+        left = rows_ref[pl.ds(2 * start, step, 2), :]
+        right = rows_ref[pl.ds(2 * start + 1, step, 2), :]
+        square = jnp.sum(left * left + right * right, axis=1, keepdims=True)
+        inverse = 1.0 / jnp.sqrt(square + EPSILON)
+        out_ref[start : start + step, :half] = (left * inverse).astype(BF16)
+        out_ref[start : start + step, half:] = (right * inverse).astype(BF16)
+
+
+def own_target_kernel(index_ref, table_ref, out_ref, narrow_ref, wide_ref, rows_ref, sems):
+    load_table(table_ref, narrow_ref, wide_ref, sems)
+    take_rows(lambda i: index_ref[i], 0, out_ref.shape[0], wide_ref, rows_ref)
+    unit_taken(rows_ref, out_ref)
+
+
+def query_target_kernel(per_device, target_ref, table_ref, out_ref, narrow_ref, wide_ref, rows_ref, sems):
+    load_table(table_ref, narrow_ref, wide_ref, sems)
+    stride = table_ref.shape[1]
+    for block in range(out_ref.shape[0] // per_device):
+        start = block * stride
+        take_rows(lambda i: target_ref[0, start + i], block * per_device, per_device, wide_ref, rows_ref)
+    unit_taken(rows_ref, out_ref)
+
+
+def send_kernel(columns, row_ref, feat_ref, pos_ref, index_ref, out_ref, pos_own, index_own, sems):
+    per_device, channels = feat_ref.shape
+    copies = [
+        pltpu.make_async_copy(pos_ref, pos_own, sems.at[0]),
+        pltpu.make_async_copy(index_ref, index_own, sems.at[1]),
+        pltpu.make_async_copy(feat_ref, out_ref.at[pl.ds(0, per_device), :], sems.at[2]),
+    ]
+    for copy in copies:
+        copy.start()
+    for copy in copies[:2]:
+        copy.wait()
+    pos, index = pos_own[...] - row_ref[0] * (columns * per_device), index_own[...]
+    cell = jnp.zeros_like(pos)
+    for k in range(1, columns):
+        cell = cell + (pos >= k * per_device).astype(jnp.int32)
+    rows = [cell, pos - cell * per_device, index >> BASE_BITS, index & (BASE - 1)]
+    digits = jnp.concatenate(rows + [jnp.zeros((EXTRA - 4, per_device), jnp.int32)], axis=0)
+    pad = jnp.zeros((EXTRA, channels - per_device), jnp.int32)
+    digits = jnp.concatenate([digits, pad], axis=1) if channels > per_device else digits
+    out_ref[per_device : per_device + EXTRA, :] = digits.astype(F32).astype(BF16)
+    copies[2].wait()
+
+
+def pick_kernel(count, col_ref, own_ref, *refs):
     blocks = refs[:count]
-    unit_ref, place_ref, target_ref, cell_ref, norm_ref = refs[count:]
-    per_device, channels = cell_ref.shape
+    unit_ref, target_ref, cell_ref, norm_ref = refs[count:]
+    per_device, channels = own_ref.shape
     me = col_ref[0]
     slot = lax.broadcasted_iota(jnp.int32, (per_device, per_device), 0)
     cell = jnp.zeros((per_device, channels), F32)
+    digits = [block[per_device : per_device + EXTRA, :] for block in blocks]
+    table = jnp.concatenate([d[2:4, :per_device].astype(F32) for d in digits], axis=0).astype(BF16)
     for i, block in enumerate(blocks):
         feats = block[0:per_device, :]
-        digits = block[per_device : per_device + EXTRA, :].astype(F32).astype(jnp.int32)
-        column, offset, high, low = (digits[k : k + 1, :] for k in range(4))
-        place_ref[i : i + 1, :] = (column ^ me) * channels + offset
-        target_ref[i : i + 1, :] = high * BASE + low
-        wanted = jnp.where(column == me, offset, -1)[:, :per_device]
-        chosen = jnp.where(slot == wanted, 1.0, 0.0).astype(BF16)
+        column, offset = (digits[i][k : k + 1, :per_device].astype(F32).astype(jnp.int32) for k in range(2))
+        at_slot = jnp.where(slot == offset, 1.0, 0.0)
+        found = jnp.dot(table, at_slot.astype(BF16), preferred_element_type=F32)
+        target = jnp.zeros((1, per_device), F32)
+        for j in range(count):
+            value = found[2 * j : 2 * j + 1, :] * BASE + found[2 * j + 1 : 2 * j + 2, :]
+            target = target + jnp.where((column ^ me) == j, value, 0.0)
+        target_ref[:, i * channels : i * channels + per_device] = target.astype(jnp.int32)
+        chosen = jnp.where(column == me, at_slot, 0.0).astype(BF16)
         cell = cell + jnp.dot(chosen, feats, preferred_element_type=F32)
         unit_ref[i * per_device : (i + 1) * per_device, :] = unit_rows(feats)[0]
     unit, norms = unit_rows(cell.astype(BF16))
-    cell_ref[...] = unit
+    cell_ref[0:per_device, :] = unit
+    cell_ref[per_device:, :] = own_ref[...]
     norm_ref[...] = jnp.broadcast_to(norms, norm_ref.shape)
-
-
-def query_target_kernel(place_ref, target_ref, table_ref, out_ref, wide_ref, rows_ref):
-    widen(table_ref, wide_ref)
-    count, channels = place_ref.shape
-    per_device = out_ref.shape[0] // count
-    shift = channels.bit_length() - 1
-
-    @pl.loop(0, count)
-    def _(block):
-        @pl.loop(0, per_device // 8)
-        def _(i):
-            rows = []
-            for j in range(8):
-                place = place_ref[block, i * 8 + j]
-                target = target_ref[place >> shift, place & (channels - 1)]
-                rows.append(wide_ref[pl.ds(target, 1), :])
-            start = pl.multiple_of(block * per_device + i * 8, 8)
-            rows_ref[pl.ds(start, 8), :] = jnp.concatenate(rows, axis=0)
-
-    @pl.loop(0, count)
-    def _(block):
-        span = pl.ds(pl.multiple_of(block * per_device, 16), per_device)
-        out_ref[span, :] = unit_rows(rows_ref[span, :])[0]
 
 
 def affinity(left, right):
@@ -113,17 +171,16 @@
     return total
 
 
-def gather_keys(blocks, whole_ref):
-    per_device = blocks[0].shape[0]
+def gather_keys(blocks, whole_refs):
+    per_device = blocks[0].shape[0] // 2
     for i, block in enumerate(blocks):
-        whole_ref[i * per_device : (i + 1) * per_device, :] = block[...]
+        for k, whole_ref in enumerate(whole_refs):
+            whole_ref[i * per_device : (i + 1) * per_device, :] = block[k * per_device : (k + 1) * per_device, :]
 
 
 def stat_kernel(count, qx_ref, qy_ref, *refs):
-    kx_blocks, ky_blocks = refs[:count], refs[count : 2 * count]
-    key_ref, query_ref, kx_ref, ky_ref, sums_ref = refs[2 * count :]
-    gather_keys(kx_blocks, kx_ref)
-    gather_keys(ky_blocks, ky_ref)
+    key_ref, query_ref, kx_ref, ky_ref, sums_ref = refs[count:]
+    gather_keys(refs[:count], (kx_ref, ky_ref))
     sums_ref[...] = jnp.zeros_like(sums_ref)
     lanes = lanes_of(qx_ref.shape[0])
 
@@ -167,14 +224,12 @@
 
 
 def grad_kernel(count, parts, scale, qx_ref, qy_ref, *refs):
-    kx_blocks, ky_blocks = refs[:count], refs[count : 2 * count]
-    refs = refs[2 * count :]
+    blocks, refs = refs[:count], refs[count:]
     key_sums, query_sums = refs[:count], refs[count : count + parts]
     outs = refs[count + parts : 2 * count + parts]
     kx_ref, ky_ref, key_ref, query_ref, total_ref = refs[2 * count + parts :]
-    per_device = kx_blocks[0].shape[0]
-    gather_keys(kx_blocks, kx_ref)
-    gather_keys(ky_blocks, ky_ref)
+    per_device = blocks[0].shape[0] // 2
+    gather_keys(blocks, (kx_ref, ky_ref))
 
     sums = query_sums[0][...]
     for k in range(1, parts):
@@ -216,7 +271,7 @@
     gradient = parts[0][...]
     for part in parts[1:]:
         gradient = gradient + part[...].astype(F32)
-    unit = unit_ref[...].astype(F32)
+    unit = unit_ref[0 : gradient.shape[0], :].astype(F32)
     along = jnp.sum(unit * gradient, axis=1, keepdims=True)
     out_ref[...] = (gradient - unit * along) / norm_ref[:, :1]
 
@@ -245,55 +300,54 @@
         pairs = [(i, i ^ bits) for i in range(lax.axis_size(axis))]
         return lax.ppermute(values, axis, pairs)
 
-    digits = jnp.stack(
-        [
-            ray_pos // per_device % col_count,
-            ray_pos % per_device,
-            target_index // BASE,
-            target_index % BASE,
-        ]
-    )
-    digits = jnp.pad(digits, ((0, EXTRA - 4), (0, channels - per_device)))
-    sent = jnp.concatenate([ray_feat, digits.astype(F32).astype(BF16)], axis=0)
-    blocks = []
-    for k in range(col_count // 2):
-        block = flip(sent, "col", 2 * k) if k else sent
-        blocks += [block, flip(block, "col", 1)]
-
+    me = lax.axis_index("col").astype(jnp.int32).reshape(1)
+    sent = call(
+        functools.partial(send_kernel, col_count),
+        shape((per_device + EXTRA, channels), BF16),
+        (
+            lax.axis_index("row").astype(jnp.int32).reshape(1),
+            ray_feat,
+            ray_pos.reshape(1, -1),
+            target_index.reshape(1, -1),
+        ),
+        in_specs=[SMEM, HBM, HBM, HBM],
+        scratch=[pltpu.VMEM((1, per_device), jnp.int32)] * 2 + [pltpu.SemaphoreType.DMA((3,))],
+        mib=FULL,
+    )
     own_target = call(
         own_target_kernel,
         shape((per_device, channels), BF16),
         (target_index, target_map),
-        in_specs=[SMEM, VMEM],
-        scratch=[pltpu.VMEM(target_map.shape, F32), pltpu.VMEM((per_device, channels), F32)],
+        in_specs=[SMEM, HBM],
+        scratch=table_scratch(target_map, per_device),
         mib=24,
         nbytes=target_map.size * 2,
     )
-    key_targets = [own_target] + [flip(own_target, "row", k) for k in range(1, row_count)]
-
-    me = lax.axis_index("col").astype(jnp.int32).reshape(1)
-    query_unit, places, targets, own_unit, own_norm = call(
+    blocks = [sent, flip(sent, "col", 1)]
+    for k in range(2, col_count, 2):
+        block, own_target = lax.optimization_barrier((flip(sent, "col", k), own_target))
+        blocks += [block, flip(block, "col", 1)]
+    query_unit, targets, own_block, own_norm = call(
         functools.partial(pick_kernel, col_count),
         (
             shape((queries, channels), BF16),
-            shape((col_count, channels), jnp.int32),
-            shape((col_count, channels), jnp.int32),
-            shape((per_device, channels), BF16),
+            shape((1, col_count * channels), jnp.int32),
+            shape((2 * per_device, channels), BF16),
             shape((per_device, 128), F32),
         ),
-        (me, *blocks),
-        in_specs=[SMEM] + [VMEM] * col_count,
+        (me, own_target, *blocks),
+        in_specs=[SMEM] + [VMEM] * (col_count + 1),
         nbytes=queries * channels * 4,
     )
-    key_units = [own_unit] + [flip(own_unit, "row", k) for k in range(1, row_count)]
+    key_blocks = [own_block] + [flip(own_block, "row", k) for k in range(1, row_count)]
     query_target = call(
-        query_target_kernel,
+        functools.partial(query_target_kernel, per_device),
         shape((queries, channels), BF16),
-        (places, targets, target_map),
-        in_specs=[SMEM, SMEM, VMEM],
-        scratch=[pltpu.VMEM(target_map.shape, F32), pltpu.VMEM((queries, channels), F32)],
+        (targets, target_map),
+        in_specs=[SMEM, HBM],
+        scratch=table_scratch(target_map, queries),
         mib=24,
-        nbytes=target_map.size * 4,
+        nbytes=target_map.size * 2,
     )
 
     flops = 2 * queries * keys * channels
@@ -301,7 +355,7 @@
     key_sums, query_sums = call(
         functools.partial(stat_kernel, row_count),
         (shape((4, keys), F32), shape((4, queries), F32)),
-        (query_unit, query_target, *key_units, *key_targets),
+        (query_unit, query_target, *key_blocks),
         scratch=key_scratch + [pltpu.VMEM((4, keys, 128), F32)],
         mib=32,
         flops=2 * flops,
@@ -319,7 +373,7 @@
     partials = call(
         functools.partial(grad_kernel, row_count, len(query_parts), scale),
         [shape((per_device, channels), F32 if k == 0 else BF16) for k in range(row_count)],
-        (query_unit, query_target, *key_units, *key_targets, *key_parts, *query_parts),
+        (query_unit, query_target, *key_blocks, *key_parts, *query_parts),
         scratch=key_scratch
         + [
             pltpu.VMEM((3, keys, 128), F32),
@@ -333,7 +387,7 @@
     return call(
         last_kernel,
         shape((per_device, channels), F32),
-        (own_unit, own_norm, *partials),
+        (own_block, own_norm, *partials),
     )
 
 

time: 77.2 us -> 61 us (0.79)
  Pallas kernels: 28.8 us -> 19.8 us
  starting transfers between devices: 25.5 us -> 21.9 us
  other arithmetic: 2.31 us -> 0 us
  waiting for transfers between devices: 15.1 us -> 14 us
    pallas_call x7 -> x8, Pallas kernels: 28.8 us -> 19.8 us  [call(): pl.pallas_call(kernel, out_shape=out_shape, in_specs=in_specs or [VMEM] *...]
    ppermute x23 -> x20, starting transfers between devices: 25.5 us -> 21.9 us  [flip(): return lax.ppermute(values, axis, pairs)]
    select_n x2 -> x0, other arithmetic: 1.39 us -> none  [the longest x1 0.7 us: body(): ray_pos // per_device % col_count]
    ppermute x23 -> x20, waiting for transfers between devices: 15.1 us -> 14 us  [flip(): return lax.ppermute(values, axis, pairs)]
    concatenate x1 -> x0, other arithmetic: 0.9 us -> none  [body(): sent = jnp.concatenate([ray_feat, digits.astype(F32).astype(BF16)], axis=0)]
    unnamed x6 -> x8, local copies, waits for them, and re-layouts: 5.05 us -> 5.06 us
  transfers between devices with their start and end apart: 23 -> 20, of which waited for: 7 -> 10; matrix products, arithmetic and copies ran while one was open for 0% -> 0% of each run, Pallas kernels for 23% -> 10%
where the time goes in v2:
time: 61 us; the launch traced here: 60.8 us
  starting transfers between devices  21.9 us (36%)
  Pallas kernels  19.8 us (32%)
  waiting for transfers between devices  14 us (23%)
  local copies, waits for them, and re-layouts  5.06 us (8%)
    ppermute x20, starting transfers between devices, flip(): return lax.ppermute(values, axis, pairs)  21.9 us
    pallas_call x8, Pallas kernels, call(): pl.pallas_call(kernel, out_shape=out_shape, in_specs=in_specs or [VMEM] *...  19.8 us
    ppermute x20, waiting for transfers between devices, flip(): return lax.ppermute(values, axis, pairs)  14 us
    unnamed x8, local copies, waits for them, and re-layouts  5.06 us
  transfers between devices with their start and end apart: 20, of which 10 were waited for; matrix products, arithmetic and copies ran while one was open for 0% of the time, Pallas kernels for 10%

profile of v2, /device:TPU:0, one launch (start us, length us, event | category | flops | bytes accessed | tf_op | source)
XLA Modules:
  0.0 60.8 jit_solution(8346709335980215465)
XLA Ops:
  0.0 1.6 %shard_map.46.refs_0_ = bf16[208,256]{1,0:T(8,128)(2,1)} custom-call(s32[1]{0:T(128)} %bitcast.1.row_ref, bf16[192,256]{1,0:T(8,128)(2,1)} %feat_ref.1, s32[1,192]{1,0:T(1,128)} %bitcast.5, s32[1,192]{1,0:T(1,128)} %bitcast.4), custom_call_target="tpu_custom_call" | custom-call | tf_op jit(solution)/shard_map/pallas_call | solution.py:281
  1.6 3.1 %collective-permute-start.2 = (bf16[208,256]{1,0:T(8,128)(2,1)}, bf16[208,256]{1,0:T(8,128)(2,1)S(1)}, u32[]{:S(2)}, u32[]{:S(2)}) collective-permute-start(bf16[208,256]{1,0:T(8,128)(2,1)} %shard_map.46.refs_0_), channel_id=1, source_target_pairs={{0,2},{1,3},{2,0},{3,1},{4,6},{5,7},{6,4},{7,5},{8,10},{9,11},{10,... | collective-permute-start | bytes 319496 | tf_op jit(solution)/shard_map/ppermute | solution.py:301
  4.7 2.6 %collective-permute-start.1 = (bf16[208,256]{1,0:T(8,128)(2,1)}, bf16[208,256]{1,0:T(8,128)(2,1)S(1)}, u32[]{:S(2)}, u32[]{:S(2)}) collective-permute-start(bf16[208,256]{1,0:T(8,128)(2,1)} %shard_map.46.refs_0_), channel_id=1, source_target_pairs={{0,4},{1,5},{2,6},{3,7},{4,0},{5,1},{6,2},{7,3},{8,12},{9,13},{10,... | collective-permute-start | bytes 319496 | tf_op jit(solution)/shard_map/ppermute | solution.py:301
  7.3 2.2 %copy-done = bf16[8192,256]{1,0:T(8,128)(2,1)S(1)} copy-done((bf16[8192,256]{1,0:T(8,128)(2,1)S(1)}, bf16[8192,256]{1,0:T(8,128)(2,1)}, u32[]{:S(2)}) %copy-start) | copy-done | bytes 4194328
  10.2 2.0 %shard_map.47.own_ref = bf16[192,256]{1,0:T(8,128)(2,1)S(1)} custom-call(s32[192]{0:T(256)S(1)} %copy-done.3, bf16[8192,256]{1,0:T(8,128)(2,1)S(1)} %copy-done), custom_call_target="tpu_custom_call" | custom-call | bytes 4194304 | tf_op jit(solution)/shard_map/pallas_call | solution.py:281
  12.7 3.3 %collective-permute-done.1.refs_4_ = bf16[208,256]{1,0:T(8,128)(2,1)S(1)} collective-permute-done((bf16[208,256]{1,0:T(8,128)(2,1)}, bf16[208,256]{1,0:T(8,128)(2,1)S(1)}, u32[]{:S(2)}, u32[]{:S(2)}) %collective-permute-start.1) | collective-permute-done | bytes 106528 | tf_op jit(solution)/shard_map/ppermute | solution.py:301
  17.4 1.0 %shard_map.48 = (bf16[1536,256]{1,0:T(8,128)(2,1)S(1)}, s32[1,2048]{1,0:T(1,128)S(1)}, bf16[384,256]{1,0:T(8,128)(2,1)S(1)}, f32[192,128]{1,0:T(8,128)S(1)}) custom-call(s32[1]{0:T(128)} %bitcast.col_ref, bf16[192,256]{1,0:T(8,128)(2,1)S(1)} %shard_map.47.own_ref, bf16[208,256]{1,0:T(8,128)(2,1)S(1)} %copy-done.2, ...), custom_call_target="tpu_custom_call" | custom-call | bytes 1572864 | tf_op jit(solution)/shard_map/pallas_call | solution.py:281
  18.5 2.5 %collective-permute-start.9 = (bf16[384,256]{1,0:T(8,128)(2,1)S(1)}, bf16[384,256]{1,0:T(8,128)(2,1)S(1)}, u32[]{:S(2)}, u32[]{:S(2)}) collective-permute-start(bf16[384,256]{1,0:T(8,128)(2,1)S(1)} %get-tuple-element.27.refs_0_.unit_ref), channel_id=1, source_target_pairs={{0,24},{8,16},{16,8},{24,0},{1,25},{9,17},{17,9},{25,1},{2,26},{10... | collective-permute-start | bytes 589832 | tf_op jit(solution)/shard_map/ppermute | solution.py:301
  22.0 2.2 %copy-done.1 = bf16[8192,256]{1,0:T(8,128)(2,1)S(1)} copy-done((bf16[8192,256]{1,0:T(8,128)(2,1)S(1)}, bf16[8192,256]{1,0:T(8,128)(2,1)}, u32[]{:S(2)}) %copy-start.1) | copy-done | bytes 4194328
  24.2 4.1 %shard_map.49.qy_ref = bf16[1536,256]{1,0:T(8,128)(2,1)S(1)} custom-call(s32[1,2048]{1,0:T(1,128)S(1)} %get-tuple-element.30.target_ref, bf16[8192,256]{1,0:T(8,128)(2,1)S(1)} %copy-done.1), custom_call_target="tpu_custom_call" | custom-call | bytes 4194304 | tf_op jit(solution)/shard_map/pallas_call | solution.py:281
  28.3 2.5 %collective-permute-done.8.refs_2_ = bf16[384,256]{1,0:T(8,128)(2,1)S(1)} collective-permute-done((bf16[384,256]{1,0:T(8,128)(2,1)S(1)}, bf16[384,256]{1,0:T(8,128)(2,1)S(1)}, u32[]{:S(2)}, u32[]{:S(2)}) %collective-permute-start.8) | collective-permute-done | bytes 196640 | tf_op jit(solution)/shard_map/ppermute | solution.py:301
  30.9 5.5 %shard_map.50 = (f32[4,768]{1,0:T(4,128)S(1)}, f32[4,1536]{1,0:T(4,128)S(1)}) custom-call(bf16[1536,256]{1,0:T(8,128)(2,1)S(1)} %get-tuple-element.29.qx_ref, bf16[1536,256]{1,0:T(8,128)(2,1)S(1)} %shard_map.49.qy_ref, bf16[384,256]{1,0:T(8,128)(2,1)S(1)} %get-tuple-element.27.refs_0_.unit_ref, bf16[384,256]{1,0:T(8,128)(2,1)S(1)} %collective-permute-done.7.refs_1_, ...), custom_call_target="tpu_custom_call" | custom-call | flops 1207959552 | tf_op jit(solution)/shard_map/pallas_call | solution.py:281
  36.4 1.7 %collective-permute-start.12 = (f32[4,768]{1,0:T(4,128)S(1)}, f32[4,768]{1,0:T(4,128)S(1)}, u32[]{:S(2)}, u32[]{:S(2)}) collective-permute-start(f32[4,768]{1,0:T(4,128)S(1)} %get-tuple-element.31.refs_4_), channel_id=1, source_target_pairs={{0,24},{8,16},{16,8},{24,0},{1,25},{9,17},{17,9},{25,1},{2,26},{10... | collective-permute-start | bytes 36872 | tf_op jit(solution)/shard_map/ppermute | solution.py:301
  38.2 2.5 %collective-permute-start.16 = (f32[4,1536]{1,0:T(4,128)S(1)}, f32[4,1536]{1,0:T(4,128)S(1)}, u32[]{:S(2)}, u32[]{:S(2)}) collective-permute-start(f32[4,1536]{1,0:T(4,128)S(1)} %shard_map.51.refs_8_), channel_id=1, source_target_pairs={{0,6},{1,7},{2,4},{3,5},{4,2},{5,3},{6,0},{7,1},{8,14},{9,15},{10,... | collective-permute-start | bytes 73736 | tf_op jit(solution)/shard_map/ppermute | solution.py:301
  41.1 1.6 %collective-permute-start.14 = (f32[4,1536]{1,0:T(4,128)S(1)}, f32[4,1536]{1,0:T(4,128)S(1)}, u32[]{:S(2)}, u32[]{:S(2)}) collective-permute-start(f32[4,1536]{1,0:T(4,128)S(1)} %shard_map.51.refs_8_), channel_id=1, source_target_pairs={{0,2},{1,3},{2,0},{3,1},{4,6},{5,7},{6,4},{7,5},{8,10},{9,11},{10,... | collective-permute-start | bytes 73736 | tf_op jit(solution)/shard_map/ppermute | solution.py:301
  42.7 1.3 %collective-permute-start.11 = (f32[4,768]{1,0:T(4,128)S(1)}, f32[4,768]{1,0:T(4,128)S(1)}, u32[]{:S(2)}, u32[]{:S(2)}) collective-permute-start(f32[4,768]{1,0:T(4,128)S(1)} %get-tuple-element.31.refs_4_), channel_id=1, source_target_pairs={{0,16},{8,24},{16,0},{24,8},{1,17},{9,25},{17,1},{25,9},{2,18},{10... | collective-permute-start | bytes 36872 | tf_op jit(solution)/shard_map/ppermute | solution.py:301
  44.5 1.8 %collective-permute-done.11.refs_6_ = f32[4,768]{1,0:T(4,128)S(1)} collective-permute-done((f32[4,768]{1,0:T(4,128)S(1)}, f32[4,768]{1,0:T(4,128)S(1)}, u32[]{:S(2)}, u32[]{:S(2)}) %collective-permute-start.11) | collective-permute-done | bytes 12320 | tf_op jit(solution)/shard_map/ppermute | solution.py:301
  46.3 1.3 %collective-permute-done.10.refs_5_ = f32[4,768]{1,0:T(4,128)S(1)} collective-permute-done((f32[4,768]{1,0:T(4,128)S(1)}, f32[4,768]{1,0:T(4,128)S(1)}, u32[]{:S(2)}, u32[]{:S(2)}) %collective-permute-start.10) | collective-permute-done | bytes 12320 | tf_op jit(solution)/shard_map/ppermute | solution.py:301
  47.7 4.7 %shard_map.52 = (f32[192,256]{1,0:T(8,128)S(1)}, bf16[192,256]{1,0:T(8,128)(2,1)S(1)}, bf16[192,256]{1,0:T(8,128)(2,1)S(1)}, bf16[192,256]{1,0:T(8,128)(2,1)S(1)}) custom-call(bf16[1536,256]{1,0:T(8,128)(2,1)S(1)} %get-tuple-element.29.qx_ref, bf16[1536,256]{1,0:T(8,128)(2,1)S(1)} %shard_map.49.qy_ref, ...), custom_call_target="tpu_custom_call" | custom-call | flops 1811939328 | tf_op jit(solution)/shard_map/pallas_call | solution.py:281
  53.0 1.4 %collective-permute-start.18 = (bf16[192,256]{1,0:T(8,128)(2,1)S(1)}, bf16[192,256]{1,0:T(8,128)(2,1)S(1)}, u32[]{:S(2)}, u32[]{:S(2)}) collective-permute-start(bf16[192,256]{1,0:T(8,128)(2,1)S(1)} %get-tuple-element.35), channel_id=1, source_target_pairs={{0,16},{8,24},{16,0},{24,8},{1,17},{9,25},{17,1},{25,9},{2,18},{10... | collective-permute-start | bytes 294920 | tf_op jit(solution)/shard_map/ppermute | solution.py:301
  54.4 1.5 %collective-permute-start.19 = (bf16[192,256]{1,0:T(8,128)(2,1)S(1)}, bf16[192,256]{1,0:T(8,128)(2,1)S(1)}, u32[]{:S(2)}, u32[]{:S(2)}) collective-permute-start(bf16[192,256]{1,0:T(8,128)(2,1)S(1)} %get-tuple-element.36), channel_id=1, source_target_pairs={{0,24},{8,16},{16,8},{24,0},{1,25},{9,17},{17,9},{25,1},{2,26},{10... | collective-permute-start | bytes 294920 | tf_op jit(solution)/shard_map/ppermute | solution.py:301
  56.0 1.1 %collective-permute-done.17.refs_1_ = bf16[192,256]{1,0:T(8,128)(2,1)S(1)} collective-permute-done((bf16[192,256]{1,0:T(8,128)(2,1)S(1)}, bf16[192,256]{1,0:T(8,128)(2,1)S(1)}, u32[]{:S(2)}, u32[]{:S(2)}) %collective-permute-start.17) | collective-permute-done | bytes 98336 | tf_op jit(solution)/shard_map/ppermute | solution.py:301
  57.6 2.3 %collective-permute-done.19.refs_3_ = bf16[192,256]{1,0:T(8,128)(2,1)S(1)} collective-permute-done((bf16[192,256]{1,0:T(8,128)(2,1)S(1)}, bf16[192,256]{1,0:T(8,128)(2,1)S(1)}, u32[]{:S(2)}, u32[]{:S(2)}) %collective-permute-start.19) | collective-permute-done | bytes 98336 | tf_op jit(solution)/shard_map/ppermute | solution.py:301
  59.9 0.9 %shard_map.53 = f32[192,256]{1,0:T(8,128)} custom-call(bf16[384,256]{1,0:T(8,128)(2,1)S(1)} %get-tuple-element.27.refs_0_.unit_ref, f32[192,128]{1,0:T(8,128)S(1)} %get-tuple-element.28.norm_ref, f32[192,256]{1,0:T(8,128)S(1)} %get-tuple-element.33.refs_0_, bf16[192,256]{1,0:T(8,128)(2,1)S(1)} %collective-permute-done.17.refs_1_, ...), custom_call_target="tpu_custom_call" | custom-call | tf_op jit(solution)/shard_map/pallas_call | solution.py:281
  (32 shorter events, 5.9 us)
Async XLA Ops:
  1.6 10.5 %collective-permute-start.2 = (bf16[208,256]{1,0:T(8,128)(2,1)}, bf16[208,256]{1,0:T(8,128)(2,1)S(1)}, u32[]{:S(2)}, u32[]{:S(2)}) collective-permute-start(bf16[208,256]{1,0:T(8,128)(2,1)} %shard_map.46.refs_0_), channel_id=1, source_target_pairs={{0,2},{1,3},{2,0},{3,1},{4,6},{5,7},{6,4},{7,5},{8,10},{9,11},{10,... | collective-permute-start | bytes 319496 | tf_op jit(solution)/shard_map/ppermute | solution.py:301
  4.7 11.3 %collective-permute-start.1 = (bf16[208,256]{1,0:T(8,128)(2,1)}, bf16[208,256]{1,0:T(8,128)(2,1)S(1)}, u32[]{:S(2)}, u32[]{:S(2)}) collective-permute-start(bf16[208,256]{1,0:T(8,128)(2,1)} %shard_map.46.refs_0_), channel_id=1, source_target_pairs={{0,4},{1,5},{2,6},{3,7},{4,0},{5,1},{6,2},{7,3},{8,12},{9,13},{10,... | collective-permute-start | bytes 319496 | tf_op jit(solution)/shard_map/ppermute | solution.py:301
  7.3 8.7 %collective-permute-start = (bf16[208,256]{1,0:T(8,128)(2,1)}, bf16[208,256]{1,0:T(8,128)(2,1)S(1)}, u32[]{:S(2)}, u32[]{:S(2)}) collective-permute-start(bf16[208,256]{1,0:T(8,128)(2,1)} %shard_map.46.refs_0_), channel_id=1, source_target_pairs={{0,6},{1,7},{2,4},{3,5},{4,2},{5,3},{6,0},{7,1},{8,14},{9,15},{10,... | collective-permute-start | bytes 319496 | tf_op jit(solution)/shard_map/ppermute | solution.py:301
  7.3 9.2 %collective-permute-start.3 = (bf16[208,256]{1,0:T(8,128)(2,1)}, bf16[208,256]{1,0:T(8,128)(2,1)S(1)}, u32[]{:S(2)}, u32[]{:S(2)}) collective-permute-start(bf16[208,256]{1,0:T(8,128)(2,1)} %shard_map.46.refs_0_), channel_id=1, source_target_pairs={{0,1},{1,0},{2,3},{3,2},{4,5},{5,4},{6,7},{7,6},{8,9},{9,8},{10,11... | collective-permute-start | bytes 319496 | tf_op jit(solution)/shard_map/ppermute | solution.py:301
  7.3 2.2 %copy-start = (bf16[8192,256]{1,0:T(8,128)(2,1)S(1)}, bf16[8192,256]{1,0:T(8,128)(2,1)}, u32[]{:S(2)}) copy-start(bf16[8192,256]{1,0:T(8,128)(2,1)} %table_ref.3) | copy-start | bytes 12582916
  9.5 0.7 %copy-start.3 = (s32[192]{0:T(256)S(1)}, s32[192]{0:T(256)}, u32[]{:S(2)}) copy-start(s32[192]{0:T(256)} %index_ref.1) | copy-start | bytes 2308
  10.2 7.3 %copy-start.2 = (bf16[208,256]{1,0:T(8,128)(2,1)S(1)}, bf16[208,256]{1,0:T(8,128)(2,1)}, u32[]{:S(2)}) copy-start(bf16[208,256]{1,0:T(8,128)(2,1)} %shard_map.46.refs_0_) | copy-start | bytes 319492
  12.1 4.3 %collective-permute-start.4 = (bf16[208,256]{1,0:T(8,128)(2,1)S(1)}, bf16[208,256]{1,0:T(8,128)(2,1)S(1)}, u32[]{:S(2)}, u32[]{:S(2)}) collective-permute-start(bf16[208,256]{1,0:T(8,128)(2,1)S(1)} %collective-permute-done.2.refs_2_), channel_id=1, source_target_pairs={{0,1},{1,0},{2,3},{3,2},{4,5},{5,4},{6,7},{7,6},{8,9},{9,8},{10,11... | collective-permute-start | bytes 319496 | tf_op jit(solution)/shard_map/ppermute | solution.py:301
  16.0 1.3 %collective-permute-start.5 = (bf16[208,256]{1,0:T(8,128)(2,1)S(1)}, bf16[208,256]{1,0:T(8,128)(2,1)S(1)}, u32[]{:S(2)}, u32[]{:S(2)}) collective-permute-start(bf16[208,256]{1,0:T(8,128)(2,1)S(1)} %collective-permute-done.1.refs_4_), channel_id=1, source_target_pairs={{0,1},{1,0},{2,3},{3,2},{4,5},{5,4},{6,7},{7,6},{8,9},{9,8},{10,11... | collective-permute-start | bytes 319496 | tf_op jit(solution)/shard_map/ppermute | solution.py:301
  16.0 1.5 %collective-permute-start.6 = (bf16[208,256]{1,0:T(8,128)(2,1)S(1)}, bf16[208,256]{1,0:T(8,128)(2,1)S(1)}, u32[]{:S(2)}, u32[]{:S(2)}) collective-permute-start(bf16[208,256]{1,0:T(8,128)(2,1)S(1)} %collective-permute-done.refs_6_), channel_id=1, source_target_pairs={{0,1},{1,0},{2,3},{3,2},{4,5},{5,4},{6,7},{7,6},{8,9},{9,8},{10,11... | collective-permute-start | bytes 319496 | tf_op jit(solution)/shard_map/ppermute | solution.py:301
  18.5 9.8 %collective-permute-start.9 = (bf16[384,256]{1,0:T(8,128)(2,1)S(1)}, bf16[384,256]{1,0:T(8,128)(2,1)S(1)}, u32[]{:S(2)}, u32[]{:S(2)}) collective-permute-start(bf16[384,256]{1,0:T(8,128)(2,1)S(1)} %get-tuple-element.27.refs_0_.unit_ref), channel_id=1, source_target_pairs={{0,24},{8,16},{16,8},{24,0},{1,25},{9,17},{17,9},{25,1},{2,26},{10... | collective-permute-start | bytes 589832 | tf_op jit(solution)/shard_map/ppermute | solution.py:301
  21.0 9.8 %collective-permute-start.8 = (bf16[384,256]{1,0:T(8,128)(2,1)S(1)}, bf16[384,256]{1,0:T(8,128)(2,1)S(1)}, u32[]{:S(2)}, u32[]{:S(2)}) collective-permute-start(bf16[384,256]{1,0:T(8,128)(2,1)S(1)} %get-tuple-element.27.refs_0_.unit_ref), channel_id=1, source_target_pairs={{0,16},{8,24},{16,0},{24,8},{1,17},{9,25},{17,1},{25,9},{2,18},{10... | collective-permute-start | bytes 589832 | tf_op jit(solution)/shard_map/ppermute | solution.py:301
  21.5 9.4 %collective-permute-start.7 = (bf16[384,256]{1,0:T(8,128)(2,1)S(1)}, bf16[384,256]{1,0:T(8,128)(2,1)S(1)}, u32[]{:S(2)}, u32[]{:S(2)}) collective-permute-start(bf16[384,256]{1,0:T(8,128)(2,1)S(1)} %get-tuple-element.27.refs_0_.unit_ref), channel_id=1, source_target_pairs={{0,8},{8,0},{16,24},{24,16},{1,9},{9,1},{17,25},{25,17},{2,10},{10... | collective-permute-start | bytes 589832 | tf_op jit(solution)/shard_map/ppermute | solution.py:301
  22.0 2.2 %copy-start.1 = (bf16[8192,256]{1,0:T(8,128)(2,1)S(1)}, bf16[8192,256]{1,0:T(8,128)(2,1)}, u32[]{:S(2)}) copy-start(bf16[8192,256]{1,0:T(8,128)(2,1)} %table_ref.3) | copy-start | bytes 12582916
  36.4 1.7 %collective-permute-start.13 = (f32[4,1536]{1,0:T(4,128)S(1)}, f32[4,1536]{1,0:T(4,128)S(1)}, u32[]{:S(2)}, u32[]{:S(2)}) collective-permute-start(f32[4,1536]{1,0:T(4,128)S(1)} %get-tuple-element.32.own_ref), channel_id=1, source_target_pairs={{0,1},{1,0},{2,3},{3,2},{4,5},{5,4},{6,7},{7,6},{8,9},{9,8},{10,11... | collective-permute-start | bytes 73736 | tf_op jit(solution)/shard_map/ppermute | solution.py:301
  36.4 7.6 %collective-permute-start.12 = (f32[4,768]{1,0:T(4,128)S(1)}, f32[4,768]{1,0:T(4,128)S(1)}, u32[]{:S(2)}, u32[]{:S(2)}) collective-permute-start(f32[4,768]{1,0:T(4,128)S(1)} %get-tuple-element.31.refs_4_), channel_id=1, source_target_pairs={{0,24},{8,16},{16,8},{24,0},{1,25},{9,17},{17,9},{25,1},{2,26},{10... | collective-permute-start | bytes 36872 | tf_op jit(solution)/shard_map/ppermute | solution.py:301
  38.2 9.5 %collective-permute-start.16 = (f32[4,1536]{1,0:T(4,128)S(1)}, f32[4,1536]{1,0:T(4,128)S(1)}, u32[]{:S(2)}, u32[]{:S(2)}) collective-permute-start(f32[4,1536]{1,0:T(4,128)S(1)} %shard_map.51.refs_8_), channel_id=1, source_target_pairs={{0,6},{1,7},{2,4},{3,5},{4,2},{5,3},{6,0},{7,1},{8,14},{9,15},{10,... | collective-permute-start | bytes 73736 | tf_op jit(solution)/shard_map/ppermute | solution.py:301
  40.7 6.9 %collective-permute-start.15 = (f32[4,1536]{1,0:T(4,128)S(1)}, f32[4,1536]{1,0:T(4,128)S(1)}, u32[]{:S(2)}, u32[]{:S(2)}) collective-permute-start(f32[4,1536]{1,0:T(4,128)S(1)} %shard_map.51.refs_8_), channel_id=1, source_target_pairs={{0,4},{1,5},{2,6},{3,7},{4,0},{5,1},{6,2},{7,3},{8,12},{9,13},{10,... | collective-permute-start | bytes 73736 | tf_op jit(solution)/shard_map/ppermute | solution.py:301
  41.1 6.6 %collective-permute-start.14 = (f32[4,1536]{1,0:T(4,128)S(1)}, f32[4,1536]{1,0:T(4,128)S(1)}, u32[]{:S(2)}, u32[]{:S(2)}) collective-permute-start(f32[4,1536]{1,0:T(4,128)S(1)} %shard_map.51.refs_8_), channel_id=1, source_target_pairs={{0,2},{1,3},{2,0},{3,1},{4,6},{5,7},{6,4},{7,5},{8,10},{9,11},{10,... | collective-permute-start | bytes 73736 | tf_op jit(solution)/shard_map/ppermute | solution.py:301
  42.7 3.7 %collective-permute-start.11 = (f32[4,768]{1,0:T(4,128)S(1)}, f32[4,768]{1,0:T(4,128)S(1)}, u32[]{:S(2)}, u32[]{:S(2)}) collective-permute-start(f32[4,768]{1,0:T(4,128)S(1)} %get-tuple-element.31.refs_4_), channel_id=1, source_target_pairs={{0,16},{8,24},{16,0},{24,8},{1,17},{9,25},{17,1},{25,9},{2,18},{10... | collective-permute-start | bytes 36872 | tf_op jit(solution)/shard_map/ppermute | solution.py:301
  44.0 3.7 %collective-permute-start.10 = (f32[4,768]{1,0:T(4,128)S(1)}, f32[4,768]{1,0:T(4,128)S(1)}, u32[]{:S(2)}, u32[]{:S(2)}) collective-permute-start(f32[4,768]{1,0:T(4,128)S(1)} %get-tuple-element.31.refs_4_), channel_id=1, source_target_pairs={{0,8},{8,0},{16,24},{24,16},{1,9},{9,1},{17,25},{25,17},{2,10},{10... | collective-permute-start | bytes 36872 | tf_op jit(solution)/shard_map/ppermute | solution.py:301
  52.4 4.7 %collective-permute-start.17 = (bf16[192,256]{1,0:T(8,128)(2,1)S(1)}, bf16[192,256]{1,0:T(8,128)(2,1)S(1)}, u32[]{:S(2)}, u32[]{:S(2)}) collective-permute-start(bf16[192,256]{1,0:T(8,128)(2,1)S(1)} %get-tuple-element.34), channel_id=1, source_target_pairs={{0,8},{8,0},{16,24},{24,16},{1,9},{9,1},{17,25},{25,17},{2,10},{10... | collective-permute-start | bytes 294920 | tf_op jit(solution)/shard_map/ppermute | solution.py:301
  53.0 4.6 %collective-permute-start.18 = (bf16[192,256]{1,0:T(8,128)(2,1)S(1)}, bf16[192,256]{1,0:T(8,128)(2,1)S(1)}, u32[]{:S(2)}, u32[]{:S(2)}) collective-permute-start(bf16[192,256]{1,0:T(8,128)(2,1)S(1)} %get-tuple-element.35), channel_id=1, source_target_pairs={{0,16},{8,24},{16,0},{24,8},{1,17},{9,25},{17,1},{25,9},{2,18},{10... | collective-permute-start | bytes 294920 | tf_op jit(solution)/shard_map/ppermute | solution.py:301
  54.4 5.5 %collective-permute-start.19 = (bf16[192,256]{1,0:T(8,128)(2,1)S(1)}, bf16[192,256]{1,0:T(8,128)(2,1)S(1)}, u32[]{:S(2)}, u32[]{:S(2)}) collective-permute-start(bf16[192,256]{1,0:T(8,128)(2,1)S(1)} %get-tuple-element.36), channel_id=1, source_target_pairs={{0,24},{8,16},{16,8},{24,0},{1,25},{9,17},{17,9},{25,1},{2,26},{10... | collective-permute-start | bytes 294920 | tf_op jit(solution)/shard_map/ppermute | solution.py:301

commit v3 on v2

--- a/solution.py
+++ b/solution.py
@@ -153,22 +153,32 @@
     norm_ref[...] = jnp.broadcast_to(norms, norm_ref.shape)
 
 
-def affinity(left, right):
-    product = lax.dot_general(
-        left, right, (((1,), (1,)), ((), ())), preferred_element_type=F32
-    )
+def products(left, right):
+    return lax.dot_general(left, right, (((1,), (1,)), ((), ())), preferred_element_type=F32)
+
+
+def affinity(product):
     return jnp.exp2(product * (math.log2(math.e) / HEAT))
 
 
 def lanes_of(length):
-    return math.gcd(length, 256)
-
-
-def fold(values):
-    total = values[:, :128]
-    for start in range(128, values.shape[1], 128):
-        total = total + values[:, start : start + 128]
-    return total
+    return math.gcd(length, 512)
+
+
+def each_part(length, body):
+    size = math.gcd(length, 768)
+    if size == length:
+        body(0, size)
+    else:
+        pl.loop(0, length // size)(lambda i: body(pl.multiple_of(i * size, size), size))
+
+
+def tiles(rows, lanes):
+    for strip in range(0, rows, 16):
+        yield strip, [
+            [(slice(row, row + 8), slice(lane, lane + 128)) for row in range(strip, strip + 16, 8)]
+            for lane in range(0, lanes, 128)
+        ]
 
 
 def gather_keys(blocks, whole_refs):
@@ -181,28 +191,40 @@
 def stat_kernel(count, qx_ref, qy_ref, *refs):
     key_ref, query_ref, kx_ref, ky_ref, sums_ref = refs[count:]
     gather_keys(refs[:count], (kx_ref, ky_ref))
-    sums_ref[...] = jnp.zeros_like(sums_ref)
-    lanes = lanes_of(qx_ref.shape[0])
-
-    @pl.loop(0, qx_ref.shape[0] // lanes)
-    def _(i):
-        span = pl.ds(pl.multiple_of(i * lanes, lanes), lanes)
-        render = affinity(kx_ref[...], qx_ref[span, :])
-        target = affinity(ky_ref[...], qy_ref[span, :])
-        for k, values in enumerate((render, target, render * render, render * target)):
-            sums_ref[k] += fold(values)
-            query_ref[k : k + 1, span] = jnp.sum(values, axis=0, keepdims=True)
-
-    ones = jnp.ones((8, 128), F32)
+    keys, lanes = kx_ref.shape[0], lanes_of(qx_ref.shape[0])
+    query_ref[...] = jnp.zeros_like(query_ref)
+
+    def part(base, size):
+        for start in range(0, qx_ref.shape[0], lanes):
+            span = slice(start, start + lanes)
+            x = products(kx_ref[pl.ds(base, size), :], qx_ref[span, :])
+            y = products(ky_ref[pl.ds(base, size), :], qy_ref[span, :])
+            query = [[0.0] * (lanes // 128) for _ in range(4)]
+            for strip, columns in tiles(size, lanes):
+                key = [[0.0] * 2 for _ in range(4)]
+                for i, column in enumerate(columns):
+                    for j, at in enumerate(column):
+                        a, b = affinity(x[at]), affinity(y[at])
+                        for k, value in enumerate((a, b, a * a, a * b)):
+                            key[k][j] = key[k][j] + value
+                            query[k][i] = query[k][i] + value
+                for k in range(4):
+                    for j in range(2):
+                        rows = pl.ds(base + strip + 8 * j, 8)
+                        if start:
+                            sums_ref[k, rows, :] += key[k][j]
+                        else:
+                            sums_ref[k, rows, :] = key[k][j]
+            for k in range(4):
+                for i, value in enumerate(query[k]):
+                    at = slice(start + i * 128, start + i * 128 + 128)
+                    query_ref[k : k + 1, at] += jnp.sum(value, axis=0, keepdims=True)
+
+    each_part(keys, part)
     for k in range(4):
-        totals = lax.dot_general(
-            ones,
-            sums_ref[k],
-            (((1,), (1,)), ((), ())),
-            precision=HIGH,
-            preferred_element_type=F32,
-        )
-        key_ref[k : k + 1, :] = totals[0:1, :]
+        for row in range(0, keys, 128):
+            at = slice(row, row + 128)
+            key_ref[k : k + 1, at] = jnp.sum(sums_ref[k, at, :].T, axis=0, keepdims=True)
 
 
 def factors(sums, scale):
@@ -242,26 +264,40 @@
     for k, row in enumerate(factors(sums, scale)):
         key_ref[k] = jnp.broadcast_to(row, (128, row.shape[1])).T
 
-    total_ref[...] = jnp.zeros_like(total_ref)
     lanes = lanes_of(qx_ref.shape[0])
 
-    @pl.loop(0, qx_ref.shape[0] // lanes)
-    def _(i):
-        span = pl.ds(pl.multiple_of(i * lanes, lanes), lanes)
-        queries = qx_ref[span, :]
-        render = affinity(kx_ref[...], queries)
-        target = affinity(ky_ref[...], qy_ref[span, :])
-        weights = []
-        for start in range(0, lanes, 128):
-            part = slice(start, start + 128)
-            at = pl.ds(pl.multiple_of(i * lanes + start, 128), 128)
-            square, cross, single = (key_ref[k] + query_ref[k : k + 1, at] for k in range(3))
-            a, b = render[:, part], target[:, part]
-            weights.append((a * (a * square - b * cross - single)).astype(BF16))
-        total_ref[...] += jnp.dot(
-            jnp.concatenate(weights, axis=1), queries, preferred_element_type=F32
-        )
-
+    def part(base, size):
+        rows = pl.ds(base, size)
+        for start in range(0, qx_ref.shape[0], lanes):
+            span = slice(start, start + lanes)
+            queries = qx_ref[span, :]
+            x = products(kx_ref[rows, :], queries)
+            y = products(ky_ref[rows, :], qy_ref[span, :])
+            query = [
+                [jnp.broadcast_to(query_ref[k : k + 1, i : i + 128], (8, 128)) for k in range(3)]
+                for i in range(start, start + lanes, 128)
+            ]
+            weights = []
+            for strip, columns in tiles(size, lanes):
+                row = []
+                for i, column in enumerate(columns):
+                    pair = []
+                    for j, at in enumerate(column):
+                        a, b = affinity(x[at]), affinity(y[at])
+                        group = pl.ds(base + strip + 8 * j, 8)
+                        square, cross, single = (key_ref[k, group, :] + query[i][k] for k in range(3))
+                        pair.append(a * (a * square - b * cross - single))
+                    row.append(jnp.concatenate(pair, axis=0).astype(BF16))
+                weights.append(jnp.concatenate(row, axis=1))
+            share = jnp.dot(
+                jnp.concatenate(weights, axis=0), queries, preferred_element_type=F32
+            )
+            if start:
+                total_ref[rows, :] += share
+            else:
+                total_ref[rows, :] = share
+
+    each_part(kx_ref.shape[0], part)
     for k, out in enumerate(outs):
         out[...] = total_ref[k * per_device : (k + 1) * per_device, :].astype(out.dtype)
 

time: 61 us -> 56.3 us (0.923)
  Pallas kernels: 19.8 us -> 15 us
    pallas_call x8, Pallas kernels: 19.8 us -> 15 us  [call(): pl.pallas_call(kernel, out_shape=out_shape, in_specs=in_specs or [VMEM] *...]
  transfers between devices with their start and end apart: 20 -> 20, of which waited for: 10 -> 10; matrix products, arithmetic and copies ran while one was open for 0% -> 0% of each run, Pallas kernels for 10% -> 11%
where the time goes in v3:
time: 56.3 us; the launch traced here: 56.1 us
  starting transfers between devices  22 us (39%)
  Pallas kernels  15 us (27%)
  waiting for transfers between devices  14 us (25%)
  local copies, waits for them, and re-layouts  5.06 us (9%)
    ppermute x20, starting transfers between devices, flip(): return lax.ppermute(values, axis, pairs)  22 us
    pallas_call x8, Pallas kernels, call(): pl.pallas_call(kernel, out_shape=out_shape, in_specs=in_specs or [VMEM] *...  15 us
    ppermute x20, waiting for transfers between devices, flip(): return lax.ppermute(values, axis, pairs)  14 us
    unnamed x8, local copies, waits for them, and re-layouts  5.06 us
  transfers between devices with their start and end apart: 20, of which 10 were waited for; matrix products, arithmetic and copies ran while one was open for 0% of the time, Pallas kernels for 11%

profile of v3, /device:TPU:0, one launch (start us, length us, event | category | flops | bytes accessed | tf_op | source)
XLA Modules:
  0.0 56.1 jit_solution(935984874130678129)
XLA Ops:
  0.0 1.6 %shard_map.46.refs_0_ = bf16[208,256]{1,0:T(8,128)(2,1)} custom-call(s32[1]{0:T(128)} %bitcast.1.row_ref, bf16[192,256]{1,0:T(8,128)(2,1)} %feat_ref.1, s32[1,192]{1,0:T(1,128)} %bitcast.5, s32[1,192]{1,0:T(1,128)} %bitcast.4), custom_call_target="tpu_custom_call" | custom-call | tf_op jit(solution)/shard_map/pallas_call | solution.py:317
  1.6 3.1 %collective-permute-start.2 = (bf16[208,256]{1,0:T(8,128)(2,1)}, bf16[208,256]{1,0:T(8,128)(2,1)S(1)}, u32[]{:S(2)}, u32[]{:S(2)}) collective-permute-start(bf16[208,256]{1,0:T(8,128)(2,1)} %shard_map.46.refs_0_), channel_id=1, source_target_pairs={{0,2},{1,3},{2,0},{3,1},{4,6},{5,7},{6,4},{7,5},{8,10},{9,11},{10,... | collective-permute-start | bytes 319496 | tf_op jit(solution)/shard_map/ppermute | solution.py:337
  4.7 2.6 %collective-permute-start.1 = (bf16[208,256]{1,0:T(8,128)(2,1)}, bf16[208,256]{1,0:T(8,128)(2,1)S(1)}, u32[]{:S(2)}, u32[]{:S(2)}) collective-permute-start(bf16[208,256]{1,0:T(8,128)(2,1)} %shard_map.46.refs_0_), channel_id=1, source_target_pairs={{0,4},{1,5},{2,6},{3,7},{4,0},{5,1},{6,2},{7,3},{8,12},{9,13},{10,... | collective-permute-start | bytes 319496 | tf_op jit(solution)/shard_map/ppermute | solution.py:337
  7.3 2.2 %copy-done = bf16[8192,256]{1,0:T(8,128)(2,1)S(1)} copy-done((bf16[8192,256]{1,0:T(8,128)(2,1)S(1)}, bf16[8192,256]{1,0:T(8,128)(2,1)}, u32[]{:S(2)}) %copy-start) | copy-done | bytes 4194328
  10.2 2.0 %shard_map.47.own_ref = bf16[192,256]{1,0:T(8,128)(2,1)S(1)} custom-call(s32[192]{0:T(256)S(1)} %copy-done.3, bf16[8192,256]{1,0:T(8,128)(2,1)S(1)} %copy-done), custom_call_target="tpu_custom_call" | custom-call | bytes 4194304 | tf_op jit(solution)/shard_map/pallas_call | solution.py:317
  12.7 3.3 %collective-permute-done.1.refs_4_ = bf16[208,256]{1,0:T(8,128)(2,1)S(1)} collective-permute-done((bf16[208,256]{1,0:T(8,128)(2,1)}, bf16[208,256]{1,0:T(8,128)(2,1)S(1)}, u32[]{:S(2)}, u32[]{:S(2)}) %collective-permute-start.1) | collective-permute-done | bytes 106528 | tf_op jit(solution)/shard_map/ppermute | solution.py:337
  17.4 1.0 %shard_map.48 = (bf16[1536,256]{1,0:T(8,128)(2,1)S(1)}, s32[1,2048]{1,0:T(1,128)S(1)}, bf16[384,256]{1,0:T(8,128)(2,1)S(1)}, f32[192,128]{1,0:T(8,128)S(1)}) custom-call(s32[1]{0:T(128)} %bitcast.col_ref, bf16[192,256]{1,0:T(8,128)(2,1)S(1)} %shard_map.47.own_ref, bf16[208,256]{1,0:T(8,128)(2,1)S(1)} %copy-done.2, ...), custom_call_target="tpu_custom_call" | custom-call | bytes 1572864 | tf_op jit(solution)/shard_map/pallas_call | solution.py:317
  18.5 2.5 %collective-permute-start.9 = (bf16[384,256]{1,0:T(8,128)(2,1)S(1)}, bf16[384,256]{1,0:T(8,128)(2,1)S(1)}, u32[]{:S(2)}, u32[]{:S(2)}) collective-permute-start(bf16[384,256]{1,0:T(8,128)(2,1)S(1)} %get-tuple-element.27.refs_0_.unit_ref), channel_id=1, source_target_pairs={{0,24},{8,16},{16,8},{24,0},{1,25},{9,17},{17,9},{25,1},{2,26},{10... | collective-permute-start | bytes 589832 | tf_op jit(solution)/shard_map/ppermute | solution.py:337
  22.0 2.2 %copy-done.1 = bf16[8192,256]{1,0:T(8,128)(2,1)S(1)} copy-done((bf16[8192,256]{1,0:T(8,128)(2,1)S(1)}, bf16[8192,256]{1,0:T(8,128)(2,1)}, u32[]{:S(2)}) %copy-start.1) | copy-done | bytes 4194328
  24.2 4.1 %shard_map.49.qy_ref = bf16[1536,256]{1,0:T(8,128)(2,1)S(1)} custom-call(s32[1,2048]{1,0:T(1,128)S(1)} %get-tuple-element.30.target_ref, bf16[8192,256]{1,0:T(8,128)(2,1)S(1)} %copy-done.1), custom_call_target="tpu_custom_call" | custom-call | bytes 4194304 | tf_op jit(solution)/shard_map/pallas_call | solution.py:317
  28.3 2.5 %collective-permute-done.8.refs_2_ = bf16[384,256]{1,0:T(8,128)(2,1)S(1)} collective-permute-done((bf16[384,256]{1,0:T(8,128)(2,1)S(1)}, bf16[384,256]{1,0:T(8,128)(2,1)S(1)}, u32[]{:S(2)}, u32[]{:S(2)}) %collective-permute-start.8) | collective-permute-done | bytes 196640 | tf_op jit(solution)/shard_map/ppermute | solution.py:337
  30.9 2.6 %shard_map.50 = (f32[4,768]{1,0:T(4,128)S(1)}, f32[4,1536]{1,0:T(4,128)S(1)}) custom-call(bf16[1536,256]{1,0:T(8,128)(2,1)S(1)} %get-tuple-element.29.qx_ref, bf16[1536,256]{1,0:T(8,128)(2,1)S(1)} %shard_map.49.qy_ref, bf16[384,256]{1,0:T(8,128)(2,1)S(1)} %get-tuple-element.27.refs_0_.unit_ref, bf16[384,256]{1,0:T(8,128)(2,1)S(1)} %collective-permute-done.7.refs_1_, ...), custom_call_target="tpu_custom_call" | custom-call | flops 1207959552 | tf_op jit(solution)/shard_map/pallas_call | solution.py:317
  33.6 1.7 %collective-permute-start.12 = (f32[4,768]{1,0:T(4,128)S(1)}, f32[4,768]{1,0:T(4,128)S(1)}, u32[]{:S(2)}, u32[]{:S(2)}) collective-permute-start(f32[4,768]{1,0:T(4,128)S(1)} %get-tuple-element.31.refs_4_), channel_id=1, source_target_pairs={{0,24},{8,16},{16,8},{24,0},{1,25},{9,17},{17,9},{25,1},{2,26},{10... | collective-permute-start | bytes 36872 | tf_op jit(solution)/shard_map/ppermute | solution.py:337
  35.4 2.5 %collective-permute-start.16 = (f32[4,1536]{1,0:T(4,128)S(1)}, f32[4,1536]{1,0:T(4,128)S(1)}, u32[]{:S(2)}, u32[]{:S(2)}) collective-permute-start(f32[4,1536]{1,0:T(4,128)S(1)} %shard_map.51.refs_8_), channel_id=1, source_target_pairs={{0,6},{1,7},{2,4},{3,5},{4,2},{5,3},{6,0},{7,1},{8,14},{9,15},{10,... | collective-permute-start | bytes 73736 | tf_op jit(solution)/shard_map/ppermute | solution.py:337
  38.2 1.6 %collective-permute-start.14 = (f32[4,1536]{1,0:T(4,128)S(1)}, f32[4,1536]{1,0:T(4,128)S(1)}, u32[]{:S(2)}, u32[]{:S(2)}) collective-permute-start(f32[4,1536]{1,0:T(4,128)S(1)} %shard_map.51.refs_8_), channel_id=1, source_target_pairs={{0,2},{1,3},{2,0},{3,1},{4,6},{5,7},{6,4},{7,5},{8,10},{9,11},{10,... | collective-permute-start | bytes 73736 | tf_op jit(solution)/shard_map/ppermute | solution.py:337
  39.8 1.3 %collective-permute-start.11 = (f32[4,768]{1,0:T(4,128)S(1)}, f32[4,768]{1,0:T(4,128)S(1)}, u32[]{:S(2)}, u32[]{:S(2)}) collective-permute-start(f32[4,768]{1,0:T(4,128)S(1)} %get-tuple-element.31.refs_4_), channel_id=1, source_target_pairs={{0,16},{8,24},{16,0},{24,8},{1,17},{9,25},{17,1},{25,9},{2,18},{10... | collective-permute-start | bytes 36872 | tf_op jit(solution)/shard_map/ppermute | solution.py:337
  41.7 1.9 %collective-permute-done.11.refs_6_ = f32[4,768]{1,0:T(4,128)S(1)} collective-permute-done((f32[4,768]{1,0:T(4,128)S(1)}, f32[4,768]{1,0:T(4,128)S(1)}, u32[]{:S(2)}, u32[]{:S(2)}) %collective-permute-start.11) | collective-permute-done | bytes 12320 | tf_op jit(solution)/shard_map/ppermute | solution.py:337
  43.5 1.3 %collective-permute-done.10.refs_5_ = f32[4,768]{1,0:T(4,128)S(1)} collective-permute-done((f32[4,768]{1,0:T(4,128)S(1)}, f32[4,768]{1,0:T(4,128)S(1)}, u32[]{:S(2)}, u32[]{:S(2)}) %collective-permute-start.10) | collective-permute-done | bytes 12320 | tf_op jit(solution)/shard_map/ppermute | solution.py:337
  44.9 2.9 %shard_map.52 = (f32[192,256]{1,0:T(8,128)S(1)}, bf16[192,256]{1,0:T(8,128)(2,1)S(1)}, bf16[192,256]{1,0:T(8,128)(2,1)S(1)}, bf16[192,256]{1,0:T(8,128)(2,1)S(1)}) custom-call(bf16[1536,256]{1,0:T(8,128)(2,1)S(1)} %get-tuple-element.29.qx_ref, bf16[1536,256]{1,0:T(8,128)(2,1)S(1)} %shard_map.49.qy_ref, ...), custom_call_target="tpu_custom_call" | custom-call | flops 1811939328 | tf_op jit(solution)/shard_map/pallas_call | solution.py:317
  48.3 1.4 %collective-permute-start.18 = (bf16[192,256]{1,0:T(8,128)(2,1)S(1)}, bf16[192,256]{1,0:T(8,128)(2,1)S(1)}, u32[]{:S(2)}, u32[]{:S(2)}) collective-permute-start(bf16[192,256]{1,0:T(8,128)(2,1)S(1)} %get-tuple-element.35), channel_id=1, source_target_pairs={{0,16},{8,24},{16,0},{24,8},{1,17},{9,25},{17,1},{25,9},{2,18},{10... | collective-permute-start | bytes 294920 | tf_op jit(solution)/shard_map/ppermute | solution.py:337
  49.7 1.5 %collective-permute-start.19 = (bf16[192,256]{1,0:T(8,128)(2,1)S(1)}, bf16[192,256]{1,0:T(8,128)(2,1)S(1)}, u32[]{:S(2)}, u32[]{:S(2)}) collective-permute-start(bf16[192,256]{1,0:T(8,128)(2,1)S(1)} %get-tuple-element.36), channel_id=1, source_target_pairs={{0,24},{8,16},{16,8},{24,0},{1,25},{9,17},{17,9},{25,1},{2,26},{10... | collective-permute-start | bytes 294920 | tf_op jit(solution)/shard_map/ppermute | solution.py:337
  51.3 1.1 %collective-permute-done.17.refs_1_ = bf16[192,256]{1,0:T(8,128)(2,1)S(1)} collective-permute-done((bf16[192,256]{1,0:T(8,128)(2,1)S(1)}, bf16[192,256]{1,0:T(8,128)(2,1)S(1)}, u32[]{:S(2)}, u32[]{:S(2)}) %collective-permute-start.17) | collective-permute-done | bytes 98336 | tf_op jit(solution)/shard_map/ppermute | solution.py:337
  52.9 2.3 %collective-permute-done.19.refs_3_ = bf16[192,256]{1,0:T(8,128)(2,1)S(1)} collective-permute-done((bf16[192,256]{1,0:T(8,128)(2,1)S(1)}, bf16[192,256]{1,0:T(8,128)(2,1)S(1)}, u32[]{:S(2)}, u32[]{:S(2)}) %collective-permute-start.19) | collective-permute-done | bytes 98336 | tf_op jit(solution)/shard_map/ppermute | solution.py:337
  55.3 0.9 %shard_map.53 = f32[192,256]{1,0:T(8,128)} custom-call(bf16[384,256]{1,0:T(8,128)(2,1)S(1)} %get-tuple-element.27.refs_0_.unit_ref, f32[192,128]{1,0:T(8,128)S(1)} %get-tuple-element.28.norm_ref, f32[192,256]{1,0:T(8,128)S(1)} %get-tuple-element.33.refs_0_, bf16[192,256]{1,0:T(8,128)(2,1)S(1)} %collective-permute-done.17.refs_1_, ...), custom_call_target="tpu_custom_call" | custom-call | tf_op jit(solution)/shard_map/pallas_call | solution.py:317
  (32 shorter events, 6.0 us)
Async XLA Ops:
  1.6 10.5 %collective-permute-start.2 = (bf16[208,256]{1,0:T(8,128)(2,1)}, bf16[208,256]{1,0:T(8,128)(2,1)S(1)}, u32[]{:S(2)}, u32[]{:S(2)}) collective-permute-start(bf16[208,256]{1,0:T(8,128)(2,1)} %shard_map.46.refs_0_), channel_id=1, source_target_pairs={{0,2},{1,3},{2,0},{3,1},{4,6},{5,7},{6,4},{7,5},{8,10},{9,11},{10,... | collective-permute-start | bytes 319496 | tf_op jit(solution)/shard_map/ppermute | solution.py:337
  4.7 11.3 %collective-permute-start.1 = (bf16[208,256]{1,0:T(8,128)(2,1)}, bf16[208,256]{1,0:T(8,128)(2,1)S(1)}, u32[]{:S(2)}, u32[]{:S(2)}) collective-permute-start(bf16[208,256]{1,0:T(8,128)(2,1)} %shard_map.46.refs_0_), channel_id=1, source_target_pairs={{0,4},{1,5},{2,6},{3,7},{4,0},{5,1},{6,2},{7,3},{8,12},{9,13},{10,... | collective-permute-start | bytes 319496 | tf_op jit(solution)/shard_map/ppermute | solution.py:337
  7.3 8.7 %collective-permute-start = (bf16[208,256]{1,0:T(8,128)(2,1)}, bf16[208,256]{1,0:T(8,128)(2,1)S(1)}, u32[]{:S(2)}, u32[]{:S(2)}) collective-permute-start(bf16[208,256]{1,0:T(8,128)(2,1)} %shard_map.46.refs_0_), channel_id=1, source_target_pairs={{0,6},{1,7},{2,4},{3,5},{4,2},{5,3},{6,0},{7,1},{8,14},{9,15},{10,... | collective-permute-start | bytes 319496 | tf_op jit(solution)/shard_map/ppermute | solution.py:337
  7.3 9.2 %collective-permute-start.3 = (bf16[208,256]{1,0:T(8,128)(2,1)}, bf16[208,256]{1,0:T(8,128)(2,1)S(1)}, u32[]{:S(2)}, u32[]{:S(2)}) collective-permute-start(bf16[208,256]{1,0:T(8,128)(2,1)} %shard_map.46.refs_0_), channel_id=1, source_target_pairs={{0,1},{1,0},{2,3},{3,2},{4,5},{5,4},{6,7},{7,6},{8,9},{9,8},{10,11... | collective-permute-start | bytes 319496 | tf_op jit(solution)/shard_map/ppermute | solution.py:337
  7.3 2.2 %copy-start = (bf16[8192,256]{1,0:T(8,128)(2,1)S(1)}, bf16[8192,256]{1,0:T(8,128)(2,1)}, u32[]{:S(2)}) copy-start(bf16[8192,256]{1,0:T(8,128)(2,1)} %table_ref.3) | copy-start | bytes 12582916
  9.5 0.7 %copy-start.3 = (s32[192]{0:T(256)S(1)}, s32[192]{0:T(256)}, u32[]{:S(2)}) copy-start(s32[192]{0:T(256)} %index_ref.1) | copy-start | bytes 2308
  10.2 7.3 %copy-start.2 = (bf16[208,256]{1,0:T(8,128)(2,1)S(1)}, bf16[208,256]{1,0:T(8,128)(2,1)}, u32[]{:S(2)}) copy-start(bf16[208,256]{1,0:T(8,128)(2,1)} %shard_map.46.refs_0_) | copy-start | bytes 319492
  12.1 4.3 %collective-permute-start.4 = (bf16[208,256]{1,0:T(8,128)(2,1)S(1)}, bf16[208,256]{1,0:T(8,128)(2,1)S(1)}, u32[]{:S(2)}, u32[]{:S(2)}) collective-permute-start(bf16[208,256]{1,0:T(8,128)(2,1)S(1)} %collective-permute-done.2.refs_2_), channel_id=1, source_target_pairs={{0,1},{1,0},{2,3},{3,2},{4,5},{5,4},{6,7},{7,6},{8,9},{9,8},{10,11... | collective-permute-start | bytes 319496 | tf_op jit(solution)/shard_map/ppermute | solution.py:337
  16.0 1.3 %collective-permute-start.5 = (bf16[208,256]{1,0:T(8,128)(2,1)S(1)}, bf16[208,256]{1,0:T(8,128)(2,1)S(1)}, u32[]{:S(2)}, u32[]{:S(2)}) collective-permute-start(bf16[208,256]{1,0:T(8,128)(2,1)S(1)} %collective-permute-done.1.refs_4_), channel_id=1, source_target_pairs={{0,1},{1,0},{2,3},{3,2},{4,5},{5,4},{6,7},{7,6},{8,9},{9,8},{10,11... | collective-permute-start | bytes 319496 | tf_op jit(solution)/shard_map/ppermute | solution.py:337
  16.0 1.5 %collective-permute-start.6 = (bf16[208,256]{1,0:T(8,128)(2,1)S(1)}, bf16[208,256]{1,0:T(8,128)(2,1)S(1)}, u32[]{:S(2)}, u32[]{:S(2)}) collective-permute-start(bf16[208,256]{1,0:T(8,128)(2,1)S(1)} %collective-permute-done.refs_6_), channel_id=1, source_target_pairs={{0,1},{1,0},{2,3},{3,2},{4,5},{5,4},{6,7},{7,6},{8,9},{9,8},{10,11... | collective-permute-start | bytes 319496 | tf_op jit(solution)/shard_map/ppermute | solution.py:337
  18.5 9.8 %collective-permute-start.9 = (bf16[384,256]{1,0:T(8,128)(2,1)S(1)}, bf16[384,256]{1,0:T(8,128)(2,1)S(1)}, u32[]{:S(2)}, u32[]{:S(2)}) collective-permute-start(bf16[384,256]{1,0:T(8,128)(2,1)S(1)} %get-tuple-element.27.refs_0_.unit_ref), channel_id=1, source_target_pairs={{0,24},{8,16},{16,8},{24,0},{1,25},{9,17},{17,9},{25,1},{2,26},{10... | collective-permute-start | bytes 589832 | tf_op jit(solution)/shard_map/ppermute | solution.py:337
  21.0 9.8 %collective-permute-start.8 = (bf16[384,256]{1,0:T(8,128)(2,1)S(1)}, bf16[384,256]{1,0:T(8,128)(2,1)S(1)}, u32[]{:S(2)}, u32[]{:S(2)}) collective-permute-start(bf16[384,256]{1,0:T(8,128)(2,1)S(1)} %get-tuple-element.27.refs_0_.unit_ref), channel_id=1, source_target_pairs={{0,16},{8,24},{16,0},{24,8},{1,17},{9,25},{17,1},{25,9},{2,18},{10... | collective-permute-start | bytes 589832 | tf_op jit(solution)/shard_map/ppermute | solution.py:337
  21.5 9.4 %collective-permute-start.7 = (bf16[384,256]{1,0:T(8,128)(2,1)S(1)}, bf16[384,256]{1,0:T(8,128)(2,1)S(1)}, u32[]{:S(2)}, u32[]{:S(2)}) collective-permute-start(bf16[384,256]{1,0:T(8,128)(2,1)S(1)} %get-tuple-element.27.refs_0_.unit_ref), channel_id=1, source_target_pairs={{0,8},{8,0},{16,24},{24,16},{1,9},{9,1},{17,25},{25,17},{2,10},{10... | collective-permute-start | bytes 589832 | tf_op jit(solution)/shard_map/ppermute | solution.py:337
  22.0 2.2 %copy-start.1 = (bf16[8192,256]{1,0:T(8,128)(2,1)S(1)}, bf16[8192,256]{1,0:T(8,128)(2,1)}, u32[]{:S(2)}) copy-start(bf16[8192,256]{1,0:T(8,128)(2,1)} %table_ref.3) | copy-start | bytes 12582916
  33.5 1.8 %collective-permute-start.13 = (f32[4,1536]{1,0:T(4,128)S(1)}, f32[4,1536]{1,0:T(4,128)S(1)}, u32[]{:S(2)}, u32[]{:S(2)}) collective-permute-start(f32[4,1536]{1,0:T(4,128)S(1)} %get-tuple-element.32.own_ref), channel_id=1, source_target_pairs={{0,1},{1,0},{2,3},{3,2},{4,5},{5,4},{6,7},{7,6},{8,9},{9,8},{10,11... | collective-permute-start | bytes 73736 | tf_op jit(solution)/shard_map/ppermute | solution.py:337
  33.6 7.6 %collective-permute-start.12 = (f32[4,768]{1,0:T(4,128)S(1)}, f32[4,768]{1,0:T(4,128)S(1)}, u32[]{:S(2)}, u32[]{:S(2)}) collective-permute-start(f32[4,768]{1,0:T(4,128)S(1)} %get-tuple-element.31.refs_4_), channel_id=1, source_target_pairs={{0,24},{8,16},{16,8},{24,0},{1,25},{9,17},{17,9},{25,1},{2,26},{10... | collective-permute-start | bytes 36872 | tf_op jit(solution)/shard_map/ppermute | solution.py:337
  35.4 9.5 %collective-permute-start.16 = (f32[4,1536]{1,0:T(4,128)S(1)}, f32[4,1536]{1,0:T(4,128)S(1)}, u32[]{:S(2)}, u32[]{:S(2)}) collective-permute-start(f32[4,1536]{1,0:T(4,128)S(1)} %shard_map.51.refs_8_), channel_id=1, source_target_pairs={{0,6},{1,7},{2,4},{3,5},{4,2},{5,3},{6,0},{7,1},{8,14},{9,15},{10,... | collective-permute-start | bytes 73736 | tf_op jit(solution)/shard_map/ppermute | solution.py:337
  37.9 6.9 %collective-permute-start.15 = (f32[4,1536]{1,0:T(4,128)S(1)}, f32[4,1536]{1,0:T(4,128)S(1)}, u32[]{:S(2)}, u32[]{:S(2)}) collective-permute-start(f32[4,1536]{1,0:T(4,128)S(1)} %shard_map.51.refs_8_), channel_id=1, source_target_pairs={{0,4},{1,5},{2,6},{3,7},{4,0},{5,1},{6,2},{7,3},{8,12},{9,13},{10,... | collective-permute-start | bytes 73736 | tf_op jit(solution)/shard_map/ppermute | solution.py:337
  38.2 6.6 %collective-permute-start.14 = (f32[4,1536]{1,0:T(4,128)S(1)}, f32[4,1536]{1,0:T(4,128)S(1)}, u32[]{:S(2)}, u32[]{:S(2)}) collective-permute-start(f32[4,1536]{1,0:T(4,128)S(1)} %shard_map.51.refs_8_), channel_id=1, source_target_pairs={{0,2},{1,3},{2,0},{3,1},{4,6},{5,7},{6,4},{7,5},{8,10},{9,11},{10,... | collective-permute-start | bytes 73736 | tf_op jit(solution)/shard_map/ppermute | solution.py:337
  39.8 3.7 %collective-permute-start.11 = (f32[4,768]{1,0:T(4,128)S(1)}, f32[4,768]{1,0:T(4,128)S(1)}, u32[]{:S(2)}, u32[]{:S(2)}) collective-permute-start(f32[4,768]{1,0:T(4,128)S(1)} %get-tuple-element.31.refs_4_), channel_id=1, source_target_pairs={{0,16},{8,24},{16,0},{24,8},{1,17},{9,25},{17,1},{25,9},{2,18},{10... | collective-permute-start | bytes 36872 | tf_op jit(solution)/shard_map/ppermute | solution.py:337
  41.1 3.7 %collective-permute-start.10 = (f32[4,768]{1,0:T(4,128)S(1)}, f32[4,768]{1,0:T(4,128)S(1)}, u32[]{:S(2)}, u32[]{:S(2)}) collective-permute-start(f32[4,768]{1,0:T(4,128)S(1)} %get-tuple-element.31.refs_4_), channel_id=1, source_target_pairs={{0,8},{8,0},{16,24},{24,16},{1,9},{9,1},{17,25},{25,17},{2,10},{10... | collective-permute-start | bytes 36872 | tf_op jit(solution)/shard_map/ppermute | solution.py:337
  47.7 4.7 %collective-permute-start.17 = (bf16[192,256]{1,0:T(8,128)(2,1)S(1)}, bf16[192,256]{1,0:T(8,128)(2,1)S(1)}, u32[]{:S(2)}, u32[]{:S(2)}) collective-permute-start(bf16[192,256]{1,0:T(8,128)(2,1)S(1)} %get-tuple-element.34), channel_id=1, source_target_pairs={{0,8},{8,0},{16,24},{24,16},{1,9},{9,1},{17,25},{25,17},{2,10},{10... | collective-permute-start | bytes 294920 | tf_op jit(solution)/shard_map/ppermute | solution.py:337
  48.3 4.6 %collective-permute-start.18 = (bf16[192,256]{1,0:T(8,128)(2,1)S(1)}, bf16[192,256]{1,0:T(8,128)(2,1)S(1)}, u32[]{:S(2)}, u32[]{:S(2)}) collective-permute-start(bf16[192,256]{1,0:T(8,128)(2,1)S(1)} %get-tuple-element.35), channel_id=1, source_target_pairs={{0,16},{8,24},{16,0},{24,8},{1,17},{9,25},{17,1},{25,9},{2,18},{10... | collective-permute-start | bytes 294920 | tf_op jit(solution)/shard_map/ppermute | solution.py:337
  49.7 5.5 %collective-permute-start.19 = (bf16[192,256]{1,0:T(8,128)(2,1)S(1)}, bf16[192,256]{1,0:T(8,128)(2,1)S(1)}, u32[]{:S(2)}, u32[]{:S(2)}) collective-permute-start(bf16[192,256]{1,0:T(8,128)(2,1)S(1)} %get-tuple-element.36), channel_id=1, source_target_pairs={{0,24},{8,16},{16,8},{24,0},{1,25},{9,17},{17,9},{25,1},{2,26},{10... | collective-permute-start | bytes 294920 | tf_op jit(solution)/shard_map/ppermute | solution.py:337

commit v4 on v3

--- a/solution.py
+++ b/solution.py
@@ -20,7 +20,7 @@
 HBM = pl.BlockSpec(memory_space=pltpu.HBM)
 FULL = 60
 PIECES = 8
-HIGH = lax.Precision.HIGHEST
+KEY_ROWS = 8
 
 
 def params(mib):
@@ -43,7 +43,7 @@
     ]
 
 
-def load_table(table_ref, narrow_ref, wide_ref, sems):
+def load_table(table_ref, narrow_ref, wide_ref, sems, meanwhile=lambda: None):
     size = table_ref.shape[0] // PIECES
     half = table_ref.shape[1] // 2
 
@@ -53,6 +53,7 @@
 
     for i in range(PIECES):
         copy(i).start()
+    meanwhile()
     step = math.gcd(size, 256)
     for i in range(PIECES):
         copy(i).wait()
@@ -93,12 +94,20 @@
     unit_taken(rows_ref, out_ref)
 
 
-def query_target_kernel(per_device, target_ref, table_ref, out_ref, narrow_ref, wide_ref, rows_ref, sems):
-    load_table(table_ref, narrow_ref, wide_ref, sems)
+def query_kernel(count, target_ref, table_ref, *refs):
+    blocks = refs[:count]
+    unit_ref, out_ref, narrow_ref, wide_ref, rows_ref, sems = refs[count:]
+    per_device = out_ref.shape[0] // count
     stride = table_ref.shape[1]
-    for block in range(out_ref.shape[0] // per_device):
-        start = block * stride
-        take_rows(lambda i: target_ref[0, start + i], block * per_device, per_device, wide_ref, rows_ref)
+
+    def meanwhile():
+        for i, block in enumerate(blocks):
+            unit_ref[i * per_device : (i + 1) * per_device, :] = unit_rows(block[:per_device, :])[0]
+
+    load_table(table_ref, narrow_ref, wide_ref, sems, meanwhile)
+    for i in range(count):
+        start = i * stride
+        take_rows(lambda j: target_ref[0, start + j], i * per_device, per_device, wide_ref, rows_ref)
     unit_taken(rows_ref, out_ref)
 
 
@@ -125,10 +134,10 @@
     copies[2].wait()
 
 
-def pick_kernel(count, col_ref, own_ref, *refs):
+def pick_kernel(count, col_ref, *refs):
     blocks = refs[:count]
-    unit_ref, target_ref, cell_ref, norm_ref = refs[count:]
-    per_device, channels = own_ref.shape
+    target_ref, cell_ref, norm_ref = refs[count:]
+    per_device, channels = cell_ref.shape
     me = col_ref[0]
     slot = lax.broadcasted_iota(jnp.int32, (per_device, per_device), 0)
     cell = jnp.zeros((per_device, channels), F32)
@@ -146,10 +155,8 @@
         target_ref[:, i * channels : i * channels + per_device] = target.astype(jnp.int32)
         chosen = jnp.where(column == me, at_slot, 0.0).astype(BF16)
         cell = cell + jnp.dot(chosen, feats, preferred_element_type=F32)
-        unit_ref[i * per_device : (i + 1) * per_device, :] = unit_rows(feats)[0]
     unit, norms = unit_rows(cell.astype(BF16))
-    cell_ref[0:per_device, :] = unit
-    cell_ref[per_device:, :] = own_ref[...]
+    cell_ref[...] = unit
     norm_ref[...] = jnp.broadcast_to(norms, norm_ref.shape)
 
 
@@ -166,7 +173,7 @@
 
 
 def each_part(length, body):
-    size = math.gcd(length, 768)
+    size = length if length <= 768 else math.gcd(length, 768)
     if size == length:
         body(0, size)
     else:
@@ -181,16 +188,16 @@
         ]
 
 
-def gather_keys(blocks, whole_refs):
-    per_device = blocks[0].shape[0] // 2
+def gather_keys(blocks, whole_ref):
+    per_device = blocks[0].shape[0]
     for i, block in enumerate(blocks):
-        for k, whole_ref in enumerate(whole_refs):
-            whole_ref[i * per_device : (i + 1) * per_device, :] = block[k * per_device : (k + 1) * per_device, :]
+        whole_ref[i * per_device : (i + 1) * per_device, :] = block[...]
 
 
 def stat_kernel(count, qx_ref, qy_ref, *refs):
-    key_ref, query_ref, kx_ref, ky_ref, sums_ref = refs[count:]
-    gather_keys(refs[:count], (kx_ref, ky_ref))
+    key_ref, query_ref, kx_ref, ky_ref, sums_ref = refs[2 * count :]
+    gather_keys(refs[:count], kx_ref)
+    gather_keys(refs[count : 2 * count], ky_ref)
     keys, lanes = kx_ref.shape[0], lanes_of(qx_ref.shape[0])
     query_ref[...] = jnp.zeros_like(query_ref)
 
@@ -221,6 +228,7 @@
                     query_ref[k : k + 1, at] += jnp.sum(value, axis=0, keepdims=True)
 
     each_part(keys, part)
+    key_ref[4:, :] = jnp.zeros_like(key_ref[4:, :])
     for k in range(4):
         for row in range(0, keys, 128):
             at = slice(row, row + 128)
@@ -241,27 +249,28 @@
     )
 
 
-def sum_pair_kernel(size, own_ref, other_ref, out_ref):
-    out_ref[...] = own_ref[...] + reorder(other_ref[...], size, 1)
-
-
-def grad_kernel(count, parts, scale, qx_ref, qy_ref, *refs):
-    blocks, refs = refs[:count], refs[count:]
-    key_sums, query_sums = refs[:count], refs[count : count + parts]
-    outs = refs[count + parts : 2 * count + parts]
-    kx_ref, ky_ref, key_ref, query_ref, total_ref = refs[2 * count + parts :]
-    per_device = blocks[0].shape[0] // 2
-    gather_keys(blocks, (kx_ref, ky_ref))
-
+def sum_kernel(size, flip, own_ref, other_ref, out_ref):
+    out_ref[...] = own_ref[...] + reorder(other_ref[...], size, flip)
+
+
+def grad_kernel(count, chosen, rows, parts, scale, qx_ref, qy_ref, *refs):
+    kx_blocks, ky_blocks, refs = refs[:count], refs[count : 2 * count], refs[2 * count :]
+    key_sums, query_sums, refs = refs[:rows], refs[rows : rows + parts], refs[rows + parts :]
+    outs = refs[:count]
+    kx_ref, ky_ref, key_ref, query_ref, total_ref = refs[count:]
+    per_device = kx_blocks[0].shape[0]
+    gather_keys(kx_blocks, kx_ref)
+    gather_keys(ky_blocks, ky_ref)
     sums = query_sums[0][...]
     for k in range(1, parts):
         sums = sums + reorder(query_sums[k][...], 2 * per_device, k)
     for k, row in enumerate(factors(sums, scale)):
         query_ref[k : k + 1, :] = row
-    sums = key_sums[0][...]
-    for k in range(1, count):
-        sums = sums + reorder(key_sums[k][...], per_device, k)
-    for k, row in enumerate(factors(sums, scale)):
+    sums = key_sums[0][0:4, :]
+    for k in range(1, rows):
+        sums = sums + reorder(key_sums[k][0:4, :], per_device, k)
+    wanted = sums[:, chosen * per_device : (chosen + count) * per_device]
+    for k, row in enumerate(factors(wanted, scale)):
         key_ref[k] = jnp.broadcast_to(row, (128, row.shape[1])).T
 
     lanes = lanes_of(qx_ref.shape[0])
@@ -307,7 +316,7 @@
     gradient = parts[0][...]
     for part in parts[1:]:
         gradient = gradient + part[...].astype(F32)
-    unit = unit_ref[0 : gradient.shape[0], :].astype(F32)
+    unit = unit_ref[...].astype(F32)
     along = jnp.sum(unit * gradient, axis=1, keepdims=True)
     out_ref[...] = (gradient - unit * along) / norm_ref[:, :1]
 
@@ -356,33 +365,36 @@
         (target_index, target_map),
         in_specs=[SMEM, HBM],
         scratch=table_scratch(target_map, per_device),
-        mib=24,
+        mib=FULL - 8,
         nbytes=target_map.size * 2,
     )
+    key_targets = [own_target] + [flip(own_target, "row", k) for k in range(1, row_count)]
     blocks = [sent, flip(sent, "col", 1)]
     for k in range(2, col_count, 2):
         block, own_target = lax.optimization_barrier((flip(sent, "col", k), own_target))
+        if k == 2:
+            for j in (1,2):
+                block, key_targets[j] = lax.optimization_barrier((block, key_targets[j]))
         blocks += [block, flip(block, "col", 1)]
-    query_unit, targets, own_block, own_norm = call(
+    targets, own_unit, own_norm = call(
         functools.partial(pick_kernel, col_count),
         (
-            shape((queries, channels), BF16),
             shape((1, col_count * channels), jnp.int32),
-            shape((2 * per_device, channels), BF16),
+            shape((per_device, channels), BF16),
             shape((per_device, 128), F32),
         ),
-        (me, own_target, *blocks),
-        in_specs=[SMEM] + [VMEM] * (col_count + 1),
+        (me, *blocks),
+        in_specs=[SMEM] + [VMEM] * col_count,
         nbytes=queries * channels * 4,
     )
-    key_blocks = [own_block] + [flip(own_block, "row", k) for k in range(1, row_count)]
-    query_target = call(
-        functools.partial(query_target_kernel, per_device),
-        shape((queries, channels), BF16),
-        (targets, target_map),
-        in_specs=[SMEM, HBM],
+    key_units = [own_unit] + [flip(own_unit, "row", k) for k in range(1, row_count)]
+    query_unit, query_target = call(
+        functools.partial(query_kernel, col_count),
+        [shape((queries, channels), BF16)] * 2,
+        (targets, target_map, *blocks),
+        in_specs=[SMEM, HBM] + [VMEM] * col_count,
         scratch=table_scratch(target_map, queries),
-        mib=24,
+        mib=FULL - 10,
         nbytes=target_map.size * 2,
     )
 
@@ -390,40 +402,59 @@
     key_scratch = [pltpu.VMEM((keys, channels), BF16)] * 2
     key_sums, query_sums = call(
         functools.partial(stat_kernel, row_count),
-        (shape((4, keys), F32), shape((4, queries), F32)),
-        (query_unit, query_target, *key_blocks),
+        (shape((KEY_ROWS, keys), F32), shape((4, queries), F32)),
+        (query_unit, query_target, *key_units, *key_targets),
         scratch=key_scratch + [pltpu.VMEM((4, keys, 128), F32)],
         mib=32,
         flops=2 * flops,
     )
-    key_parts = [key_sums] + [flip(key_sums, "row", k) for k in range(1, row_count)]
-    query_sums = call(
-        functools.partial(sum_pair_kernel, per_device),
-        shape((4, queries), F32),
-        (query_sums, flip(query_sums, "col", 1)),
-    )
-    query_parts = [query_sums] + [
-        flip(query_sums, "col", 2 * k) for k in range(1, col_count // 2)
-    ]
+    for k in range(max(col_count, row_count).bit_length() - 1):
+        if 1 << k < row_count:
+            key_sums = call(
+                functools.partial(sum_kernel, per_device, 1 << k),
+                shape((KEY_ROWS, keys), F32),
+                (key_sums, flip(key_sums, "row", 1 << k)),
+            )
+        if 1 << k < col_count:
+            query_sums = call(
+                functools.partial(sum_kernel, per_device, 1 << k),
+                shape((4, queries), F32),
+                (query_sums, flip(query_sums, "col", 1 << k)),
+            )
+    key_parts, query_parts = [key_sums], [query_sums]
     scale = float(queries * row_count) / math.sqrt(HEAT)
-    partials = call(
-        functools.partial(grad_kernel, row_count, len(query_parts), scale),
-        [shape((per_device, channels), F32 if k == 0 else BF16) for k in range(row_count)],
-        (query_unit, query_target, *key_blocks, *key_parts, *query_parts),
-        scratch=key_scratch
-        + [
-            pltpu.VMEM((3, keys, 128), F32),
-            pltpu.VMEM((3, queries), F32),
-            pltpu.VMEM((keys, channels), F32),
-        ],
-        mib=32,
-        flops=3 * flops,
-    )
-    partials = [partials[0]] + [flip(partials[k], "row", k) for k in range(1, row_count)]
+
+    def gradient(chosen, count, dtype, query_unit):
+        return call(
+            functools.partial(grad_kernel, count, chosen, 1, 1, scale),
+            [shape((per_device, channels), dtype)] * count,
+            (
+                query_unit,
+                query_target,
+                *key_units[chosen : chosen + count],
+                *key_targets[chosen : chosen + count],
+                *key_parts,
+                *query_parts,
+            ),
+            scratch=[pltpu.VMEM((count * per_device, channels), BF16)] * 2
+            + [
+                pltpu.VMEM((3, count * per_device, 128), F32),
+                pltpu.VMEM((3, queries), F32),
+                pltpu.VMEM((count * per_device, channels), F32),
+            ],
+            mib=32,
+            flops=3 * flops * count // row_count,
+        )
+
+    partials, query_unit = lax.optimization_barrier(
+        (gradient(1, row_count - 1, BF16, query_unit), query_unit)
+    )
+    (own_part,) = gradient(0, 1, F32, query_unit)
+    partials = [own_part] + [flip(part, "row", k + 1) for k, part in enumerate(partials)]
     return call(
         last_kernel,
         shape((per_device, channels), F32),
-        (own_block, own_norm, *partials),
+        (own_unit, own_norm, *partials),
     )
 
 

time: 56.3 us -> 53.4 us (0.948)
  local copies, waits for them, and re-layouts: 5.06 us -> 0.69 us
  waiting for transfers between devices: 14 us -> 10.3 us
  Pallas kernels: 15 us -> 18.1 us
  starting transfers between devices: 22 us -> 23.9 us
    unnamed x8 -> x4, local copies, waits for them, and re-layouts: 5.06 us -> 0.69 us
    ppermute x20 -> x21, waiting for transfers between devices: 14 us -> 10.3 us  [flip(): return lax.ppermute(values, axis, pairs)]
    pallas_call x8 -> x13, Pallas kernels: 15 us -> 18.1 us  [call(): pl.pallas_call(kernel, out_shape=out_shape, in_specs=in_specs or [VMEM] *...]
    ppermute x20 -> x21, starting transfers between devices: 22 us -> 23.9 us  [flip(): return lax.ppermute(values, axis, pairs)]
  transfers between devices with their start and end apart: 20 -> 21, of which waited for: 10 -> 8; matrix products, arithmetic and copies ran while one was open for 0% -> 0% of each run, Pallas kernels for 11% -> 20%
where the time goes in v4:
time: 53.4 us; the launch traced here: 53.2 us
  starting transfers between devices  23.9 us (45%)
  Pallas kernels  18.1 us (34%)
  waiting for transfers between devices  10.3 us (19%)
  local copies, waits for them, and re-layouts  0.69 us (1%)
    ppermute x21, starting transfers between devices, flip(): return lax.ppermute(values, axis, pairs)  23.9 us
    pallas_call x13, Pallas kernels, call(): pl.pallas_call(kernel, out_shape=out_shape, in_specs=in_specs or [VMEM] *...  18.1 us
    ppermute x21, waiting for transfers between devices, flip(): return lax.ppermute(values, axis, pairs)  10.3 us
  transfers between devices with their start and end apart: 21, of which 8 were waited for; matrix products, arithmetic and copies ran while one was open for 0% of the time, Pallas kernels for 20%

profile of v4, /device:TPU:0, one launch (start us, length us, event | category | flops | bytes accessed | tf_op | source)
XLA Modules:
  0.0 53.2 jit_solution(9863660789687418557)
XLA Ops:
  0.0 1.6 %shard_map.46.refs_0_ = bf16[208,256]{1,0:T(8,128)(2,1)} custom-call(s32[1]{0:T(128)} %bitcast.1.row_ref, bf16[192,256]{1,0:T(8,128)(2,1)} %feat_ref.1, s32[1,192]{1,0:T(1,128)} %bitcast.5, s32[1,192]{1,0:T(1,128)} %bitcast.4), custom_call_target="tpu_custom_call" | custom-call | tf_op jit(solution)/shard_map/pallas_call | solution.py:326
  1.6 3.1 %collective-permute-start.1 = (bf16[208,256]{1,0:T(8,128)(2,1)}, bf16[208,256]{1,0:T(8,128)(2,1)S(1)}, u32[]{:S(2)}, u32[]{:S(2)}) collective-permute-start(bf16[208,256]{1,0:T(8,128)(2,1)} %shard_map.46.refs_0_), channel_id=1, source_target_pairs={{0,2},{1,3},{2,0},{3,1},{4,6},{5,7},{6,4},{7,5},{8,10},{9,11},{10,... | collective-permute-start | bytes 319496 | tf_op jit(solution)/shard_map/ppermute | solution.py:346
  4.7 2.6 %collective-permute-start.5 = (bf16[208,256]{1,0:T(8,128)(2,1)}, bf16[208,256]{1,0:T(8,128)(2,1)S(1)}, u32[]{:S(2)}, u32[]{:S(2)}) collective-permute-start(bf16[208,256]{1,0:T(8,128)(2,1)} %shard_map.46.refs_0_), channel_id=1, source_target_pairs={{0,4},{1,5},{2,6},{3,7},{4,0},{5,1},{6,2},{7,3},{8,12},{9,13},{10,... | collective-permute-start | bytes 319496 | tf_op jit(solution)/shard_map/ppermute | solution.py:346
  8.0 3.2 %shard_map.47.refs_4_.refs_1_ = bf16[192,256]{1,0:T(8,128)(2,1)S(1)} custom-call(s32[192]{0:T(256)S(1)} %copy-done.1, bf16[8192,256]{1,0:T(8,128)(2,1)} %table_ref.3), custom_call_target="tpu_custom_call" | custom-call | bytes 4194304 | tf_op jit(solution)/shard_map/pallas_call | solution.py:326
  11.2 1.8 %collective-permute-start.2 = (bf16[192,256]{1,0:T(8,128)(2,1)S(1)}, bf16[192,256]{1,0:T(8,128)(2,1)S(1)}, u32[]{:S(2)}, u32[]{:S(2)}) collective-permute-start(bf16[192,256]{1,0:T(8,128)(2,1)S(1)} %shard_map.47.refs_4_.refs_1_), channel_id=1, source_target_pairs={{0,8},{8,0},{16,24},{24,16},{1,9},{9,1},{17,25},{25,17},{2,10},{10... | collective-permute-start | bytes 294920 | tf_op jit(solution)/shard_map/ppermute | solution.py:346
  13.0 1.5 %collective-permute-start.3 = (bf16[192,256]{1,0:T(8,128)(2,1)S(1)}, bf16[192,256]{1,0:T(8,128)(2,1)S(1)}, u32[]{:S(2)}, u32[]{:S(2)}) collective-permute-start(bf16[192,256]{1,0:T(8,128)(2,1)S(1)} %shard_map.47.refs_4_.refs_1_), channel_id=1, source_target_pairs={{0,16},{8,24},{16,0},{24,8},{1,17},{9,25},{17,1},{25,9},{2,18},{10... | collective-permute-start | bytes 294920 | tf_op jit(solution)/shard_map/ppermute | solution.py:346
  14.5 1.4 %collective-permute-done.2.refs_5_.refs_3_ = bf16[192,256]{1,0:T(8,128)(2,1)S(1)} collective-permute-done((bf16[192,256]{1,0:T(8,128)(2,1)S(1)}, bf16[192,256]{1,0:T(8,128)(2,1)S(1)}, u32[]{:S(2)}, u32[]{:S(2)}) %collective-permute-start.2) | collective-permute-done | bytes 98336 | tf_op jit(solution)/shard_map/ppermute | solution.py:346
  15.9 1.7 %collective-permute-done.3.refs_6_.refs_4_ = bf16[192,256]{1,0:T(8,128)(2,1)S(1)} collective-permute-done((bf16[192,256]{1,0:T(8,128)(2,1)S(1)}, bf16[192,256]{1,0:T(8,128)(2,1)S(1)}, u32[]{:S(2)}, u32[]{:S(2)}) %collective-permute-start.3) | collective-permute-done | bytes 98336 | tf_op jit(solution)/shard_map/ppermute | solution.py:346
  18.2 1.5 %collective-permute-start.12 = (bf16[192,256]{1,0:T(8,128)(2,1)S(1)}, bf16[192,256]{1,0:T(8,128)(2,1)S(1)}, u32[]{:S(2)}, u32[]{:S(2)}) collective-permute-start(bf16[192,256]{1,0:T(8,128)(2,1)S(1)} %shard_map.47.refs_4_.refs_1_), channel_id=1, source_target_pairs={{0,24},{8,16},{16,8},{24,0},{1,25},{9,17},{17,9},{25,1},{2,26},{10... | collective-permute-start | bytes 294920 | tf_op jit(solution)/shard_map/ppermute | solution.py:346
  20.3 1.6 %collective-permute-start.9 = (bf16[192,256]{1,0:T(8,128)(2,1)S(1)}, bf16[192,256]{1,0:T(8,128)(2,1)S(1)}, u32[]{:S(2)}, u32[]{:S(2)}) collective-permute-start(bf16[192,256]{1,0:T(8,128)(2,1)S(1)} %get-tuple-element.27.refs_0_.unit_ref), channel_id=1, source_target_pairs={{0,8},{8,0},{16,24},{24,16},{1,9},{9,1},{17,25},{25,17},{2,10},{10... | collective-permute-start | bytes 294920 | tf_op jit(solution)/shard_map/ppermute | solution.py:346
  22.4 1.5 %collective-permute-start.11 = (bf16[192,256]{1,0:T(8,128)(2,1)S(1)}, bf16[192,256]{1,0:T(8,128)(2,1)S(1)}, u32[]{:S(2)}, u32[]{:S(2)}) collective-permute-start(bf16[192,256]{1,0:T(8,128)(2,1)S(1)} %get-tuple-element.27.refs_0_.unit_ref), channel_id=1, source_target_pairs={{0,24},{8,16},{16,8},{24,0},{1,25},{9,17},{17,9},{25,1},{2,26},{10... | collective-permute-start | bytes 294920 | tf_op jit(solution)/shard_map/ppermute | solution.py:346
  23.9 5.6 %shard_map.49 = (bf16[1536,256]{1,0:T(8,128)(2,1)S(1)}, bf16[1536,256]{1,0:T(8,128)(2,1)S(1)}) custom-call(s32[1,2048]{1,0:T(1,128)S(1)} %get-tuple-element.29.target_ref, bf16[8192,256]{1,0:T(8,128)(2,1)} %table_ref.3, bf16[208,256]{1,0:T(8,128)(2,1)S(1)} %copy-done, bf16[208,256]{1,0:T(8,128)(2,1)S(1)} %collective-permute-done.refs_1_, ...), custom_call_target="tpu_custom_call" | custom-call | bytes 4194304 | tf_op jit(solution)/shard_map/pallas_call | solution.py:326
  29.5 2.6 %shard_map.50 = (f32[8,768]{1,0:T(8,128)S(1)}, f32[4,1536]{1,0:T(4,128)S(1)}) custom-call(bf16[1536,256]{1,0:T(8,128)(2,1)S(1)} %get-tuple-element.39.qx_ref, bf16[1536,256]{1,0:T(8,128)(2,1)S(1)} %get-tuple-element.31.qy_ref, bf16[192,256]{1,0:T(8,128)(2,1)S(1)} %get-tuple-element.27.refs_0_.unit_ref, ...), custom_call_target="tpu_custom_call" | custom-call | flops 1207959552 | tf_op jit(solution)/shard_map/pallas_call | solution.py:326
  32.2 1.6 %collective-permute-start.13 = (f32[8,768]{1,0:T(8,128)S(1)}, f32[8,768]{1,0:T(8,128)S(1)}, u32[]{:S(2)}, u32[]{:S(2)}) collective-permute-start(f32[8,768]{1,0:T(8,128)S(1)} %get-tuple-element.34.own_ref), channel_id=1, source_target_pairs={{0,8},{8,0},{16,24},{24,16},{1,9},{9,1},{17,25},{25,17},{2,10},{10... | collective-permute-start | bytes 73736 | tf_op jit(solution)/shard_map/ppermute | solution.py:346
  34.6 1.5 %collective-permute-done.13.other_ref = f32[8,768]{1,0:T(8,128)S(1)} collective-permute-done((f32[8,768]{1,0:T(8,128)S(1)}, f32[8,768]{1,0:T(8,128)S(1)}, u32[]{:S(2)}, u32[]{:S(2)}) %collective-permute-start.13) | collective-permute-done | bytes 24608 | tf_op jit(solution)/shard_map/ppermute | solution.py:346
  36.2 1.3 %collective-permute-start.14 = (f32[8,768]{1,0:T(8,128)S(1)}, f32[8,768]{1,0:T(8,128)S(1)}, u32[]{:S(2)}, u32[]{:S(2)}) collective-permute-start(f32[8,768]{1,0:T(8,128)S(1)} %shard_map.51.own_ref), channel_id=1, source_target_pairs={{0,16},{8,24},{16,0},{24,8},{1,17},{9,25},{17,1},{25,9},{2,18},{10... | collective-permute-start | bytes 73736 | tf_op jit(solution)/shard_map/ppermute | solution.py:346
  37.7 2.1 %collective-permute-start.17 = (f32[4,1536]{1,0:T(4,128)S(1)}, f32[4,1536]{1,0:T(4,128)S(1)}, u32[]{:S(2)}, u32[]{:S(2)}) collective-permute-start(f32[4,1536]{1,0:T(4,128)S(1)} %shard_map.54.own_ref), channel_id=1, source_target_pairs={{0,4},{1,5},{2,6},{3,7},{4,0},{5,1},{6,2},{7,3},{8,12},{9,13},{10,... | collective-permute-start | bytes 73736 | tf_op jit(solution)/shard_map/ppermute | solution.py:346
  40.0 2.5 %collective-permute-done.17.other_ref = f32[4,1536]{1,0:T(4,128)S(1)} collective-permute-done((f32[4,1536]{1,0:T(4,128)S(1)}, f32[4,1536]{1,0:T(4,128)S(1)}, u32[]{:S(2)}, u32[]{:S(2)}) %collective-permute-start.17) | collective-permute-done | bytes 24608 | tf_op jit(solution)/shard_map/ppermute | solution.py:346
  42.5 2.3 %shard_map.56 = (bf16[192,256]{1,0:T(8,128)(2,1)S(1)}, bf16[192,256]{1,0:T(8,128)(2,1)S(1)}, bf16[192,256]{1,0:T(8,128)(2,1)S(1)}) custom-call(bf16[1536,256]{1,0:T(8,128)(2,1)S(1)} %get-tuple-element.39.qx_ref, bf16[1536,256]{1,0:T(8,128)(2,1)S(1)} %get-tuple-element.31.qy_ref, bf16[192,256]{1,0:T(8,128)(2,1)S(1)} %collective-permute-done.9.refs_1_.refs_0_, ...), custom_call_target="tpu_custom_call" | custom-call | flops 1358954496 | tf_op jit(solution)/shard_map/pallas_call | solution.py:326
  44.8 1.2 %collective-permute-start.18 = (bf16[192,256]{1,0:T(8,128)(2,1)S(1)}, bf16[192,256]{1,0:T(8,128)(2,1)S(1)}, u32[]{:S(2)}, u32[]{:S(2)}) collective-permute-start(bf16[192,256]{1,0:T(8,128)(2,1)S(1)} %get-tuple-element.40), channel_id=1, source_target_pairs={{0,8},{8,0},{16,24},{24,16},{1,9},{9,1},{17,25},{25,17},{2,10},{10... | collective-permute-start | bytes 294920 | tf_op jit(solution)/shard_map/ppermute | solution.py:346
  46.8 1.5 %collective-permute-start.20 = (bf16[192,256]{1,0:T(8,128)(2,1)S(1)}, bf16[192,256]{1,0:T(8,128)(2,1)S(1)}, u32[]{:S(2)}, u32[]{:S(2)}) collective-permute-start(bf16[192,256]{1,0:T(8,128)(2,1)S(1)} %get-tuple-element.42), channel_id=1, source_target_pairs={{0,24},{8,16},{16,8},{24,0},{1,25},{9,17},{17,9},{25,1},{2,26},{10... | collective-permute-start | bytes 294920 | tf_op jit(solution)/shard_map/ppermute | solution.py:346
  48.3 1.2 %shard_map.57.refs_0_ = f32[192,256]{1,0:T(8,128)S(1)} custom-call(bf16[1536,256]{1,0:T(8,128)(2,1)S(1)} %get-tuple-element.39.qx_ref, bf16[1536,256]{1,0:T(8,128)(2,1)S(1)} %get-tuple-element.31.qy_ref, bf16[192,256]{1,0:T(8,128)(2,1)S(1)} %get-tuple-element.27.refs_0_.unit_ref, bf16[192,256]{1,0:T(8,128)(2,1)S(1)} %shard_map.47.refs_4_.refs_1_, ...), custom_call_target="tpu_custom_call" | custom-call | flops 452984832 | tf_op jit(solution)/shard_map/pallas_call | solution.py:326
  49.5 1.0 %collective-permute-done.19.refs_2_ = bf16[192,256]{1,0:T(8,128)(2,1)S(1)} collective-permute-done((bf16[192,256]{1,0:T(8,128)(2,1)S(1)}, bf16[192,256]{1,0:T(8,128)(2,1)S(1)}, u32[]{:S(2)}, u32[]{:S(2)}) %collective-permute-start.19) | collective-permute-done | bytes 98336 | tf_op jit(solution)/shard_map/ppermute | solution.py:346
  50.5 1.8 %collective-permute-done.20.refs_3_ = bf16[192,256]{1,0:T(8,128)(2,1)S(1)} collective-permute-done((bf16[192,256]{1,0:T(8,128)(2,1)S(1)}, bf16[192,256]{1,0:T(8,128)(2,1)S(1)}, u32[]{:S(2)}, u32[]{:S(2)}) %collective-permute-start.20) | collective-permute-done | bytes 98336 | tf_op jit(solution)/shard_map/ppermute | solution.py:346
  (35 shorter events, 5.6 us)
Async XLA Ops:
  1.6 12.9 %copy-start = (bf16[208,256]{1,0:T(8,128)(2,1)S(1)}, bf16[208,256]{1,0:T(8,128)(2,1)}, u32[]{:S(2)}) copy-start(bf16[208,256]{1,0:T(8,128)(2,1)} %shard_map.46.refs_0_) | copy-start | bytes 319492
  1.6 12.9 %collective-permute-start.1 = (bf16[208,256]{1,0:T(8,128)(2,1)}, bf16[208,256]{1,0:T(8,128)(2,1)S(1)}, u32[]{:S(2)}, u32[]{:S(2)}) collective-permute-start(bf16[208,256]{1,0:T(8,128)(2,1)} %shard_map.46.refs_0_), channel_id=1, source_target_pairs={{0,2},{1,3},{2,0},{3,1},{4,6},{5,7},{6,4},{7,5},{8,10},{9,11},{10,... | collective-permute-start | bytes 319496 | tf_op jit(solution)/shard_map/ppermute | solution.py:346
  4.7 12.9 %collective-permute-start.5 = (bf16[208,256]{1,0:T(8,128)(2,1)}, bf16[208,256]{1,0:T(8,128)(2,1)S(1)}, u32[]{:S(2)}, u32[]{:S(2)}) collective-permute-start(bf16[208,256]{1,0:T(8,128)(2,1)} %shard_map.46.refs_0_), channel_id=1, source_target_pairs={{0,4},{1,5},{2,6},{3,7},{4,0},{5,1},{6,2},{7,3},{8,12},{9,13},{10,... | collective-permute-start | bytes 319496 | tf_op jit(solution)/shard_map/ppermute | solution.py:346
  7.3 10.8 %collective-permute-start.7 = (bf16[208,256]{1,0:T(8,128)(2,1)}, bf16[208,256]{1,0:T(8,128)(2,1)S(1)}, u32[]{:S(2)}, u32[]{:S(2)}) collective-permute-start(bf16[208,256]{1,0:T(8,128)(2,1)} %shard_map.46.refs_0_), channel_id=1, source_target_pairs={{0,6},{1,7},{2,4},{3,5},{4,2},{5,3},{6,0},{7,1},{8,14},{9,15},{10,... | collective-permute-start | bytes 319496 | tf_op jit(solution)/shard_map/ppermute | solution.py:346
  7.3 0.7 %copy-start.1 = (s32[192]{0:T(256)S(1)}, s32[192]{0:T(256)}, u32[]{:S(2)}) copy-start(s32[192]{0:T(256)} %index_ref.1) | copy-start | bytes 2308
  11.2 4.7 %collective-permute-start.2 = (bf16[192,256]{1,0:T(8,128)(2,1)S(1)}, bf16[192,256]{1,0:T(8,128)(2,1)S(1)}, u32[]{:S(2)}, u32[]{:S(2)}) collective-permute-start(bf16[192,256]{1,0:T(8,128)(2,1)S(1)} %shard_map.47.refs_4_.refs_1_), channel_id=1, source_target_pairs={{0,8},{8,0},{16,24},{24,16},{1,9},{9,1},{17,25},{25,17},{2,10},{10... | collective-permute-start | bytes 294920 | tf_op jit(solution)/shard_map/ppermute | solution.py:346
  13.0 4.6 %collective-permute-start.3 = (bf16[192,256]{1,0:T(8,128)(2,1)S(1)}, bf16[192,256]{1,0:T(8,128)(2,1)S(1)}, u32[]{:S(2)}, u32[]{:S(2)}) collective-permute-start(bf16[192,256]{1,0:T(8,128)(2,1)S(1)} %shard_map.47.refs_4_.refs_1_), channel_id=1, source_target_pairs={{0,16},{8,24},{16,0},{24,8},{1,17},{9,25},{17,1},{25,9},{2,18},{10... | collective-permute-start | bytes 294920 | tf_op jit(solution)/shard_map/ppermute | solution.py:346
  14.5 5.2 %collective-permute-start = (bf16[208,256]{1,0:T(8,128)(2,1)S(1)}, bf16[208,256]{1,0:T(8,128)(2,1)S(1)}, u32[]{:S(2)}, u32[]{:S(2)}) collective-permute-start(bf16[208,256]{1,0:T(8,128)(2,1)S(1)} %copy-done), channel_id=1, source_target_pairs={{0,1},{1,0},{2,3},{3,2},{4,5},{5,4},{6,7},{7,6},{8,9},{9,8},{10,11... | collective-permute-start | bytes 319496 | tf_op jit(solution)/shard_map/ppermute | solution.py:346
  17.6 2.1 %collective-permute-start.4 = (bf16[208,256]{1,0:T(8,128)(2,1)S(1)}, bf16[208,256]{1,0:T(8,128)(2,1)S(1)}, u32[]{:S(2)}, u32[]{:S(2)}) collective-permute-start(bf16[208,256]{1,0:T(8,128)(2,1)S(1)} %collective-permute-done.1.refs_2_), channel_id=1, source_target_pairs={{0,1},{1,0},{2,3},{3,2},{4,5},{5,4},{6,7},{7,6},{8,9},{9,8},{10,11... | collective-permute-start | bytes 319496 | tf_op jit(solution)/shard_map/ppermute | solution.py:346
  17.6 2.1 %collective-permute-start.6 = (bf16[208,256]{1,0:T(8,128)(2,1)S(1)}, bf16[208,256]{1,0:T(8,128)(2,1)S(1)}, u32[]{:S(2)}, u32[]{:S(2)}) collective-permute-start(bf16[208,256]{1,0:T(8,128)(2,1)S(1)} %collective-permute-done.5.refs_4_), channel_id=1, source_target_pairs={{0,1},{1,0},{2,3},{3,2},{4,5},{5,4},{6,7},{7,6},{8,9},{9,8},{10,11... | collective-permute-start | bytes 319496 | tf_op jit(solution)/shard_map/ppermute | solution.py:346
  18.1 1.6 %collective-permute-start.8 = (bf16[208,256]{1,0:T(8,128)(2,1)S(1)}, bf16[208,256]{1,0:T(8,128)(2,1)S(1)}, u32[]{:S(2)}, u32[]{:S(2)}) collective-permute-start(bf16[208,256]{1,0:T(8,128)(2,1)S(1)} %collective-permute-done.7.refs_6_), channel_id=1, source_target_pairs={{0,1},{1,0},{2,3},{3,2},{4,5},{5,4},{6,7},{7,6},{8,9},{9,8},{10,11... | collective-permute-start | bytes 319496 | tf_op jit(solution)/shard_map/ppermute | solution.py:346
  18.2 11.3 %collective-permute-start.12 = (bf16[192,256]{1,0:T(8,128)(2,1)S(1)}, bf16[192,256]{1,0:T(8,128)(2,1)S(1)}, u32[]{:S(2)}, u32[]{:S(2)}) collective-permute-start(bf16[192,256]{1,0:T(8,128)(2,1)S(1)} %shard_map.47.refs_4_.refs_1_), channel_id=1, source_target_pairs={{0,24},{8,16},{16,8},{24,0},{1,25},{9,17},{17,9},{25,1},{2,26},{10... | collective-permute-start | bytes 294920 | tf_op jit(solution)/shard_map/ppermute | solution.py:346
  20.3 9.2 %collective-permute-start.9 = (bf16[192,256]{1,0:T(8,128)(2,1)S(1)}, bf16[192,256]{1,0:T(8,128)(2,1)S(1)}, u32[]{:S(2)}, u32[]{:S(2)}) collective-permute-start(bf16[192,256]{1,0:T(8,128)(2,1)S(1)} %get-tuple-element.27.refs_0_.unit_ref), channel_id=1, source_target_pairs={{0,8},{8,0},{16,24},{24,16},{1,9},{9,1},{17,25},{25,17},{2,10},{10... | collective-permute-start | bytes 294920 | tf_op jit(solution)/shard_map/ppermute | solution.py:346
  21.9 7.6 %collective-permute-start.10 = (bf16[192,256]{1,0:T(8,128)(2,1)S(1)}, bf16[192,256]{1,0:T(8,128)(2,1)S(1)}, u32[]{:S(2)}, u32[]{:S(2)}) collective-permute-start(bf16[192,256]{1,0:T(8,128)(2,1)S(1)} %get-tuple-element.27.refs_0_.unit_ref), channel_id=1, source_target_pairs={{0,16},{8,24},{16,0},{24,8},{1,17},{9,25},{17,1},{25,9},{2,18},{10... | collective-permute-start | bytes 294920 | tf_op jit(solution)/shard_map/ppermute | solution.py:346
  22.4 7.1 %collective-permute-start.11 = (bf16[192,256]{1,0:T(8,128)(2,1)S(1)}, bf16[192,256]{1,0:T(8,128)(2,1)S(1)}, u32[]{:S(2)}, u32[]{:S(2)}) collective-permute-start(bf16[192,256]{1,0:T(8,128)(2,1)S(1)} %get-tuple-element.27.refs_0_.unit_ref), channel_id=1, source_target_pairs={{0,24},{8,16},{16,8},{24,0},{1,25},{9,17},{17,9},{25,1},{2,26},{10... | collective-permute-start | bytes 294920 | tf_op jit(solution)/shard_map/ppermute | solution.py:346
  32.1 1.6 %collective-permute-start.15 = (f32[4,1536]{1,0:T(4,128)S(1)}, f32[4,1536]{1,0:T(4,128)S(1)}, u32[]{:S(2)}, u32[]{:S(2)}) collective-permute-start(f32[4,1536]{1,0:T(4,128)S(1)} %get-tuple-element.35.own_ref), channel_id=1, source_target_pairs={{0,1},{1,0},{2,3},{3,2},{4,5},{5,4},{6,7},{7,6},{8,9},{9,8},{10,11... | collective-permute-start | bytes 73736 | tf_op jit(solution)/shard_map/ppermute | solution.py:346
  32.2 3.9 %collective-permute-start.13 = (f32[8,768]{1,0:T(8,128)S(1)}, f32[8,768]{1,0:T(8,128)S(1)}, u32[]{:S(2)}, u32[]{:S(2)}) collective-permute-start(f32[8,768]{1,0:T(8,128)S(1)} %get-tuple-element.34.own_ref), channel_id=1, source_target_pairs={{0,8},{8,0},{16,24},{24,16},{1,9},{9,1},{17,25},{25,17},{2,10},{10... | collective-permute-start | bytes 73736 | tf_op jit(solution)/shard_map/ppermute | solution.py:346
  33.8 3.9 %collective-permute-start.16 = (f32[4,1536]{1,0:T(4,128)S(1)}, f32[4,1536]{1,0:T(4,128)S(1)}, u32[]{:S(2)}, u32[]{:S(2)}) collective-permute-start(f32[4,1536]{1,0:T(4,128)S(1)} %shard_map.53.own_ref), channel_id=1, source_target_pairs={{0,2},{1,3},{2,0},{3,1},{4,6},{5,7},{6,4},{7,5},{8,10},{9,11},{10,... | collective-permute-start | bytes 73736 | tf_op jit(solution)/shard_map/ppermute | solution.py:346
  36.2 3.8 %collective-permute-start.14 = (f32[8,768]{1,0:T(8,128)S(1)}, f32[8,768]{1,0:T(8,128)S(1)}, u32[]{:S(2)}, u32[]{:S(2)}) collective-permute-start(f32[8,768]{1,0:T(8,128)S(1)} %shard_map.51.own_ref), channel_id=1, source_target_pairs={{0,16},{8,24},{16,0},{24,8},{1,17},{9,25},{17,1},{25,9},{2,18},{10... | collective-permute-start | bytes 73736 | tf_op jit(solution)/shard_map/ppermute | solution.py:346
  37.7 4.7 %collective-permute-start.17 = (f32[4,1536]{1,0:T(4,128)S(1)}, f32[4,1536]{1,0:T(4,128)S(1)}, u32[]{:S(2)}, u32[]{:S(2)}) collective-permute-start(f32[4,1536]{1,0:T(4,128)S(1)} %shard_map.54.own_ref), channel_id=1, source_target_pairs={{0,4},{1,5},{2,6},{3,7},{4,0},{5,1},{6,2},{7,3},{8,12},{9,13},{10,... | collective-permute-start | bytes 73736 | tf_op jit(solution)/shard_map/ppermute | solution.py:346
  44.8 4.8 %collective-permute-start.18 = (bf16[192,256]{1,0:T(8,128)(2,1)S(1)}, bf16[192,256]{1,0:T(8,128)(2,1)S(1)}, u32[]{:S(2)}, u32[]{:S(2)}) collective-permute-start(bf16[192,256]{1,0:T(8,128)(2,1)S(1)} %get-tuple-element.40), channel_id=1, source_target_pairs={{0,8},{8,0},{16,24},{24,16},{1,9},{9,1},{17,25},{25,17},{2,10},{10... | collective-permute-start | bytes 294920 | tf_op jit(solution)/shard_map/ppermute | solution.py:346
  45.9 4.6 %collective-permute-start.19 = (bf16[192,256]{1,0:T(8,128)(2,1)S(1)}, bf16[192,256]{1,0:T(8,128)(2,1)S(1)}, u32[]{:S(2)}, u32[]{:S(2)}) collective-permute-start(bf16[192,256]{1,0:T(8,128)(2,1)S(1)} %get-tuple-element.41), channel_id=1, source_target_pairs={{0,16},{8,24},{16,0},{24,8},{1,17},{9,25},{17,1},{25,9},{2,18},{10... | collective-permute-start | bytes 294920 | tf_op jit(solution)/shard_map/ppermute | solution.py:346
  46.8 5.5 %collective-permute-start.20 = (bf16[192,256]{1,0:T(8,128)(2,1)S(1)}, bf16[192,256]{1,0:T(8,128)(2,1)S(1)}, u32[]{:S(2)}, u32[]{:S(2)}) collective-permute-start(bf16[192,256]{1,0:T(8,128)(2,1)S(1)} %get-tuple-element.42), channel_id=1, source_target_pairs={{0,24},{8,16},{16,8},{24,0},{1,25},{9,17},{17,9},{25,1},{2,26},{10... | collective-permute-start | bytes 294920 | tf_op jit(solution)/shard_map/ppermute | solution.py:346

commit v5 on v4

--- a/solution.py
+++ b/solution.py
@@ -43,6 +43,10 @@
     ]
 
 
+def index_scratch(length):
+    return [pltpu.SMEM((1, length), jnp.int32), pltpu.SemaphoreType.DMA(())]
+
+
 def load_table(table_ref, narrow_ref, wide_ref, sems, meanwhile=lambda: None):
     size = table_ref.shape[0] // PIECES
     half = table_ref.shape[1] // 2
@@ -88,15 +92,18 @@
         out_ref[start : start + step, half:] = (right * inverse).astype(BF16)
 
 
-def own_target_kernel(index_ref, table_ref, out_ref, narrow_ref, wide_ref, rows_ref, sems):
+def own_target_kernel(list_ref, table_ref, out_ref, narrow_ref, wide_ref, rows_ref, sems, index_ref, sem):
+    copy = pltpu.make_async_copy(list_ref, index_ref, sem)
+    copy.start()
     load_table(table_ref, narrow_ref, wide_ref, sems)
-    take_rows(lambda i: index_ref[i], 0, out_ref.shape[0], wide_ref, rows_ref)
+    copy.wait()
+    take_rows(lambda i: index_ref[0, i], 0, out_ref.shape[0], wide_ref, rows_ref)
     unit_taken(rows_ref, out_ref)
 
 
-def query_kernel(count, target_ref, table_ref, *refs):
+def query_kernel(count, list_ref, table_ref, *refs):
     blocks = refs[:count]
-    unit_ref, out_ref, narrow_ref, wide_ref, rows_ref, sems = refs[count:]
+    unit_ref, out_ref, narrow_ref, wide_ref, rows_ref, sems, target_ref, sem = refs[count:]
     per_device = out_ref.shape[0] // count
     stride = table_ref.shape[1]
 
@@ -104,14 +111,17 @@
         for i, block in enumerate(blocks):
             unit_ref[i * per_device : (i + 1) * per_device, :] = unit_rows(block[:per_device, :])[0]
 
+    copy = pltpu.make_async_copy(list_ref, target_ref, sem)
+    copy.start()
     load_table(table_ref, narrow_ref, wide_ref, sems, meanwhile)
+    copy.wait()
     for i in range(count):
         start = i * stride
         take_rows(lambda j: target_ref[0, start + j], i * per_device, per_device, wide_ref, rows_ref)
     unit_taken(rows_ref, out_ref)
 
 
-def send_kernel(columns, row_ref, feat_ref, pos_ref, index_ref, out_ref, pos_own, index_own, sems):
+def send_kernel(columns, row_ref, feat_ref, pos_ref, index_ref, out_ref, list_ref, pos_own, index_own, sems):
     per_device, channels = feat_ref.shape
     copies = [
         pltpu.make_async_copy(pos_ref, pos_own, sems.at[0]),
@@ -126,6 +136,8 @@
     cell = jnp.zeros_like(pos)
     for k in range(1, columns):
         cell = cell + (pos >= k * per_device).astype(jnp.int32)
+    list_ref[...] = jnp.zeros_like(list_ref)
+    list_ref[:, :per_device] = index
     rows = [cell, pos - cell * per_device, index >> BASE_BITS, index & (BASE - 1)]
     digits = jnp.concatenate(rows + [jnp.zeros((EXTRA - 4, per_device), jnp.int32)], axis=0)
     pad = jnp.zeros((EXTRA, channels - per_device), jnp.int32)
@@ -140,6 +152,7 @@
     per_device, channels = cell_ref.shape
     me = col_ref[0]
     slot = lax.broadcasted_iota(jnp.int32, (per_device, per_device), 0)
+    target_ref[...] = jnp.zeros_like(target_ref)
     cell = jnp.zeros((per_device, channels), F32)
     digits = [block[per_device : per_device + EXTRA, :] for block in blocks]
     table = jnp.concatenate([d[2:4, :per_device].astype(F32) for d in digits], axis=0).astype(BF16)
@@ -346,9 +359,9 @@
         return lax.ppermute(values, axis, pairs)
 
     me = lax.axis_index("col").astype(jnp.int32).reshape(1)
-    sent = call(
+    sent, own_list = call(
         functools.partial(send_kernel, col_count),
-        shape((per_device + EXTRA, channels), BF16),
+        (shape((per_device + EXTRA, channels), BF16), shape((1, channels), jnp.int32)),
         (
             lax.axis_index("row").astype(jnp.int32).reshape(1),
             ray_feat,
@@ -362,9 +375,9 @@
     own_target = call(
         own_target_kernel,
         shape((per_device, channels), BF16),
-        (target_index, target_map),
-        in_specs=[SMEM, HBM],
-        scratch=table_scratch(target_map, per_device),
+        (own_list, target_map),
+        in_specs=[VMEM, HBM],
+        scratch=table_scratch(target_map, per_device) + index_scratch(channels),
         mib=FULL - 8,
         nbytes=target_map.size * 2,
     )
@@ -372,8 +385,8 @@
     blocks = [sent, flip(sent, "col", 1)]
     for k in range(2, col_count, 2):
         block, own_target = lax.optimization_barrier((flip(sent, "col", k), own_target))
-        if k == 2:
-            for j in (1,2):
+        if k == col_count - 2:
+            for j in range(1, min(row_count, 3)):
                 block, key_targets[j] = lax.optimization_barrier((block, key_targets[j]))
         blocks += [block, flip(block, "col", 1)]
     targets, own_unit, own_norm = call(
@@ -392,8 +405,8 @@
         functools.partial(query_kernel, col_count),
         [shape((queries, channels), BF16)] * 2,
         (targets, target_map, *blocks),
-        in_specs=[SMEM, HBM] + [VMEM] * col_count,
-        scratch=table_scratch(target_map, queries),
+        in_specs=[VMEM, HBM] + [VMEM] * col_count,
+        scratch=table_scratch(target_map, queries) + index_scratch(col_count * channels),
         mib=FULL - 10,
         nbytes=target_map.size * 2,
     )
@@ -416,10 +429,11 @@
                 (key_sums, flip(key_sums, "row", 1 << k)),
             )
         if 1 << k < col_count:
+            other = (2 << k) if (2 << k) < col_count else 1
             query_sums = call(
-                functools.partial(sum_kernel, per_device, 1 << k),
+                functools.partial(sum_kernel, per_device, other),
                 shape((4, queries), F32),
-                (query_sums, flip(query_sums, "col", 1 << k)),
+                (query_sums, flip(query_sums, "col", other)),
             )
     key_parts, query_parts = [key_sums], [query_sums]
     scale = float(queries * row_count) / math.sqrt(HEAT)

time: 53.4 us -> 52 us (0.974)
  Pallas kernels: 18.1 us -> 17 us
    pallas_call x13, Pallas kernels: 18.1 us -> 17 us  [call(): pl.pallas_call(kernel, out_shape=out_shape, in_specs=in_specs or [VMEM] *...]
  transfers between devices with their start and end apart: 21 -> 21, of which waited for: 8 -> 7; matrix products, arithmetic and copies ran while one was open for 0% -> 0% of each run, Pallas kernels for 20% -> 18%
where the time goes in v5:
time: 52 us; the launch traced here: 51.8 us
  starting transfers between devices  23.9 us (46%)
  Pallas kernels  17 us (33%)
  waiting for transfers between devices  10 us (19%)
  local copies, waits for them, and re-layouts  0.68 us (1%)
    ppermute x21, starting transfers between devices, flip(): return lax.ppermute(values, axis, pairs)  23.9 us
    pallas_call x13, Pallas kernels, call(): pl.pallas_call(kernel, out_shape=out_shape, in_specs=in_specs or [VMEM] *...  17 us
    ppermute x21, waiting for transfers between devices, flip(): return lax.ppermute(values, axis, pairs)  10 us
  transfers between devices with their start and end apart: 21, of which 7 were waited for; matrix products, arithmetic and copies ran while one was open for 0% of the time, Pallas kernels for 18%

profile of v5, /device:TPU:0, one launch (start us, length us, event | category | flops | bytes accessed | tf_op | source)
XLA Modules:
  0.0 51.8 jit_solution(16494221125140214035)
XLA Ops:
  0.0 1.6 %shard_map.46 = (bf16[208,256]{1,0:T(8,128)(2,1)}, s32[1,256]{1,0:T(1,128)}) custom-call(s32[1]{0:T(128)} %bitcast.1.row_ref, bf16[192,256]{1,0:T(8,128)(2,1)} %feat_ref.1, s32[1,192]{1,0:T(1,128)} %bitcast.4, s32[1,192]{1,0:T(1,128)} %bitcast.5), custom_call_target="tpu_custom_call" | custom-call | tf_op jit(solution)/shard_map/pallas_call | solution.py:339
  1.6 3.1 %collective-permute-start.1 = (bf16[208,256]{1,0:T(8,128)(2,1)}, bf16[208,256]{1,0:T(8,128)(2,1)S(1)}, u32[]{:S(2)}, u32[]{:S(2)}) collective-permute-start(bf16[208,256]{1,0:T(8,128)(2,1)} %get-tuple-element.26.refs_0_), channel_id=1, source_target_pairs={{0,2},{1,3},{2,0},{3,1},{4,6},{5,7},{6,4},{7,5},{8,10},{9,11},{10,... | collective-permute-start | bytes 319496 | tf_op jit(solution)/shard_map/ppermute | solution.py:359
  4.7 2.6 %collective-permute-start.3 = (bf16[208,256]{1,0:T(8,128)(2,1)}, bf16[208,256]{1,0:T(8,128)(2,1)S(1)}, u32[]{:S(2)}, u32[]{:S(2)}) collective-permute-start(bf16[208,256]{1,0:T(8,128)(2,1)} %get-tuple-element.26.refs_0_), channel_id=1, source_target_pairs={{0,4},{1,5},{2,6},{3,7},{4,0},{5,1},{6,2},{7,3},{8,12},{9,13},{10,... | collective-permute-start | bytes 319496 | tf_op jit(solution)/shard_map/ppermute | solution.py:359
  8.0 2.7 %shard_map.47.refs_4_.refs_1_ = bf16[192,256]{1,0:T(8,128)(2,1)S(1)} custom-call(s32[1,256]{1,0:T(1,128)S(1)} %copy-done.1, bf16[8192,256]{1,0:T(8,128)(2,1)} %table_ref.3), custom_call_target="tpu_custom_call" | custom-call | bytes 4194304 | tf_op jit(solution)/shard_map/pallas_call | solution.py:339
  10.7 1.8 %collective-permute-start.6 = (bf16[192,256]{1,0:T(8,128)(2,1)S(1)}, bf16[192,256]{1,0:T(8,128)(2,1)S(1)}, u32[]{:S(2)}, u32[]{:S(2)}) collective-permute-start(bf16[192,256]{1,0:T(8,128)(2,1)S(1)} %shard_map.47.refs_4_.refs_1_), channel_id=1, source_target_pairs={{0,8},{8,0},{16,24},{24,16},{1,9},{9,1},{17,25},{25,17},{2,10},{10... | collective-permute-start | bytes 294920 | tf_op jit(solution)/shard_map/ppermute | solution.py:359
  12.4 1.5 %collective-permute-start.7 = (bf16[192,256]{1,0:T(8,128)(2,1)S(1)}, bf16[192,256]{1,0:T(8,128)(2,1)S(1)}, u32[]{:S(2)}, u32[]{:S(2)}) collective-permute-start(bf16[192,256]{1,0:T(8,128)(2,1)S(1)} %shard_map.47.refs_4_.refs_1_), channel_id=1, source_target_pairs={{0,16},{8,24},{16,0},{24,8},{1,17},{9,25},{17,1},{25,9},{2,18},{10... | collective-permute-start | bytes 294920 | tf_op jit(solution)/shard_map/ppermute | solution.py:359
  14.0 2.0 %collective-permute-done.3.refs_4_ = bf16[208,256]{1,0:T(8,128)(2,1)S(1)} collective-permute-done((bf16[208,256]{1,0:T(8,128)(2,1)}, bf16[208,256]{1,0:T(8,128)(2,1)S(1)}, u32[]{:S(2)}, u32[]{:S(2)}) %collective-permute-start.3) | collective-permute-done | bytes 106528 | tf_op jit(solution)/shard_map/ppermute | solution.py:359
  17.1 2.0 %collective-permute-start.12 = (bf16[192,256]{1,0:T(8,128)(2,1)S(1)}, bf16[192,256]{1,0:T(8,128)(2,1)S(1)}, u32[]{:S(2)}, u32[]{:S(2)}) collective-permute-start(bf16[192,256]{1,0:T(8,128)(2,1)S(1)} %shard_map.47.refs_4_.refs_1_), channel_id=1, source_target_pairs={{0,24},{8,16},{16,8},{24,0},{1,25},{9,17},{17,9},{25,1},{2,26},{10... | collective-permute-start | bytes 294920 | tf_op jit(solution)/shard_map/ppermute | solution.py:359
  19.7 1.1 %collective-permute-start.9 = (bf16[192,256]{1,0:T(8,128)(2,1)S(1)}, bf16[192,256]{1,0:T(8,128)(2,1)S(1)}, u32[]{:S(2)}, u32[]{:S(2)}) collective-permute-start(bf16[192,256]{1,0:T(8,128)(2,1)S(1)} %get-tuple-element.31.refs_0_.unit_ref), channel_id=1, source_target_pairs={{0,8},{8,0},{16,24},{24,16},{1,9},{9,1},{17,25},{25,17},{2,10},{10... | collective-permute-start | bytes 294920 | tf_op jit(solution)/shard_map/ppermute | solution.py:359
  20.7 0.8 %collective-permute-start.10 = (bf16[192,256]{1,0:T(8,128)(2,1)S(1)}, bf16[192,256]{1,0:T(8,128)(2,1)S(1)}, u32[]{:S(2)}, u32[]{:S(2)}) collective-permute-start(bf16[192,256]{1,0:T(8,128)(2,1)S(1)} %get-tuple-element.31.refs_0_.unit_ref), channel_id=1, source_target_pairs={{0,16},{8,24},{16,0},{24,8},{1,17},{9,25},{17,1},{25,9},{2,18},{10... | collective-permute-start | bytes 294920 | tf_op jit(solution)/shard_map/ppermute | solution.py:359
  21.5 1.7 %collective-permute-start.11 = (bf16[192,256]{1,0:T(8,128)(2,1)S(1)}, bf16[192,256]{1,0:T(8,128)(2,1)S(1)}, u32[]{:S(2)}, u32[]{:S(2)}) collective-permute-start(bf16[192,256]{1,0:T(8,128)(2,1)S(1)} %get-tuple-element.31.refs_0_.unit_ref), channel_id=1, source_target_pairs={{0,24},{8,16},{16,8},{24,0},{1,25},{9,17},{17,9},{25,1},{2,26},{10... | collective-permute-start | bytes 294920 | tf_op jit(solution)/shard_map/ppermute | solution.py:359
  23.2 4.9 %shard_map.49 = (bf16[1536,256]{1,0:T(8,128)(2,1)S(1)}, bf16[1536,256]{1,0:T(8,128)(2,1)S(1)}) custom-call(s32[1,2048]{1,0:T(1,128)S(1)} %get-tuple-element.33.list_ref, bf16[8192,256]{1,0:T(8,128)(2,1)} %table_ref.3, bf16[208,256]{1,0:T(8,128)(2,1)S(1)} %copy-done, bf16[208,256]{1,0:T(8,128)(2,1)S(1)} %collective-permute-done.refs_1_, ...), custom_call_target="tpu_custom_call" | custom-call | bytes 4194304 | tf_op jit(solution)/shard_map/pallas_call | solution.py:339
  28.2 2.6 %shard_map.50 = (f32[8,768]{1,0:T(8,128)S(1)}, f32[4,1536]{1,0:T(4,128)S(1)}) custom-call(bf16[1536,256]{1,0:T(8,128)(2,1)S(1)} %get-tuple-element.43.qx_ref, bf16[1536,256]{1,0:T(8,128)(2,1)S(1)} %get-tuple-element.35.qy_ref, bf16[192,256]{1,0:T(8,128)(2,1)S(1)} %get-tuple-element.31.refs_0_.unit_ref, ...), custom_call_target="tpu_custom_call" | custom-call | flops 1207959552 | tf_op jit(solution)/shard_map/pallas_call | solution.py:339
  30.8 1.7 %collective-permute-start.15 = (f32[4,1536]{1,0:T(4,128)S(1)}, f32[4,1536]{1,0:T(4,128)S(1)}, u32[]{:S(2)}, u32[]{:S(2)}) collective-permute-start(f32[4,1536]{1,0:T(4,128)S(1)} %get-tuple-element.39.own_ref), channel_id=1, source_target_pairs={{0,2},{1,3},{2,0},{3,1},{4,6},{5,7},{6,4},{7,5},{8,10},{9,11},{10,... | collective-permute-start | bytes 73736 | tf_op jit(solution)/shard_map/ppermute | solution.py:359
  33.0 1.7 %collective-permute-done.15.other_ref = f32[4,1536]{1,0:T(4,128)S(1)} collective-permute-done((f32[4,1536]{1,0:T(4,128)S(1)}, f32[4,1536]{1,0:T(4,128)S(1)}, u32[]{:S(2)}, u32[]{:S(2)}) %collective-permute-start.15) | collective-permute-done | bytes 24608 | tf_op jit(solution)/shard_map/ppermute | solution.py:359
  34.7 2.6 %collective-permute-start.16 = (f32[4,1536]{1,0:T(4,128)S(1)}, f32[4,1536]{1,0:T(4,128)S(1)}, u32[]{:S(2)}, u32[]{:S(2)}) collective-permute-start(f32[4,1536]{1,0:T(4,128)S(1)} %shard_map.53.own_ref), channel_id=1, source_target_pairs={{0,4},{1,5},{2,6},{3,7},{4,0},{5,1},{6,2},{7,3},{8,12},{9,13},{10,... | collective-permute-start | bytes 73736 | tf_op jit(solution)/shard_map/ppermute | solution.py:359
  37.9 1.5 %collective-permute-done.16.other_ref = f32[4,1536]{1,0:T(4,128)S(1)} collective-permute-done((f32[4,1536]{1,0:T(4,128)S(1)}, f32[4,1536]{1,0:T(4,128)S(1)}, u32[]{:S(2)}, u32[]{:S(2)}) %collective-permute-start.16) | collective-permute-done | bytes 24608 | tf_op jit(solution)/shard_map/ppermute | solution.py:359
  39.4 1.8 %collective-permute-done.14.other_ref = f32[8,768]{1,0:T(8,128)S(1)} collective-permute-done((f32[8,768]{1,0:T(8,128)S(1)}, f32[8,768]{1,0:T(8,128)S(1)}, u32[]{:S(2)}, u32[]{:S(2)}) %collective-permute-start.14) | collective-permute-done | bytes 24608 | tf_op jit(solution)/shard_map/ppermute | solution.py:359
  41.3 2.3 %shard_map.56 = (bf16[192,256]{1,0:T(8,128)(2,1)S(1)}, bf16[192,256]{1,0:T(8,128)(2,1)S(1)}, bf16[192,256]{1,0:T(8,128)(2,1)S(1)}) custom-call(bf16[1536,256]{1,0:T(8,128)(2,1)S(1)} %get-tuple-element.43.qx_ref, bf16[1536,256]{1,0:T(8,128)(2,1)S(1)} %get-tuple-element.35.qy_ref, bf16[192,256]{1,0:T(8,128)(2,1)S(1)} %collective-permute-done.9.refs_1_.refs_0_, ...), custom_call_target="tpu_custom_call" | custom-call | flops 1358954496 | tf_op jit(solution)/shard_map/pallas_call | solution.py:339
  44.2 1.0 %collective-permute-start.19 = (bf16[192,256]{1,0:T(8,128)(2,1)S(1)}, bf16[192,256]{1,0:T(8,128)(2,1)S(1)}, u32[]{:S(2)}, u32[]{:S(2)}) collective-permute-start(bf16[192,256]{1,0:T(8,128)(2,1)S(1)} %get-tuple-element.45), channel_id=1, source_target_pairs={{0,16},{8,24},{16,0},{24,8},{1,17},{9,25},{17,1},{25,9},{2,18},{10... | collective-permute-start | bytes 294920 | tf_op jit(solution)/shard_map/ppermute | solution.py:359
  45.2 2.0 %collective-permute-start.20 = (bf16[192,256]{1,0:T(8,128)(2,1)S(1)}, bf16[192,256]{1,0:T(8,128)(2,1)S(1)}, u32[]{:S(2)}, u32[]{:S(2)}) collective-permute-start(bf16[192,256]{1,0:T(8,128)(2,1)S(1)} %get-tuple-element.46), channel_id=1, source_target_pairs={{0,24},{8,16},{16,8},{24,0},{1,25},{9,17},{17,9},{25,1},{2,26},{10... | collective-permute-start | bytes 294920 | tf_op jit(solution)/shard_map/ppermute | solution.py:359
  47.2 1.3 %shard_map.57.refs_0_ = f32[192,256]{1,0:T(8,128)S(1)} custom-call(bf16[1536,256]{1,0:T(8,128)(2,1)S(1)} %get-tuple-element.43.qx_ref, bf16[1536,256]{1,0:T(8,128)(2,1)S(1)} %get-tuple-element.35.qy_ref, bf16[192,256]{1,0:T(8,128)(2,1)S(1)} %get-tuple-element.31.refs_0_.unit_ref, bf16[192,256]{1,0:T(8,128)(2,1)S(1)} %shard_map.47.refs_4_.refs_1_, ...), custom_call_target="tpu_custom_call" | custom-call | flops 452984832 | tf_op jit(solution)/shard_map/pallas_call | solution.py:339
  48.9 2.0 %collective-permute-done.19.refs_2_ = bf16[192,256]{1,0:T(8,128)(2,1)S(1)} collective-permute-done((bf16[192,256]{1,0:T(8,128)(2,1)S(1)}, bf16[192,256]{1,0:T(8,128)(2,1)S(1)}, u32[]{:S(2)}, u32[]{:S(2)}) %collective-permute-start.19) | collective-permute-done | bytes 98336 | tf_op jit(solution)/shard_map/ppermute | solution.py:359
  50.9 0.9 %shard_map.58 = f32[192,256]{1,0:T(8,128)} custom-call(bf16[192,256]{1,0:T(8,128)(2,1)S(1)} %get-tuple-element.31.refs_0_.unit_ref, f32[192,128]{1,0:T(8,128)S(1)} %get-tuple-element.32.norm_ref, f32[192,256]{1,0:T(8,128)S(1)} %shard_map.57.refs_0_, bf16[192,256]{1,0:T(8,128)(2,1)S(1)} %collective-permute-done.18.refs_1_, ...), custom_call_target="tpu_custom_call" | custom-call | tf_op jit(solution)/shard_map/pallas_call | solution.py:339
  (35 shorter events, 4.7 us)
Async XLA Ops:
  1.6 12.4 %copy-start = (bf16[208,256]{1,0:T(8,128)(2,1)S(1)}, bf16[208,256]{1,0:T(8,128)(2,1)}, u32[]{:S(2)}) copy-start(bf16[208,256]{1,0:T(8,128)(2,1)} %get-tuple-element.26.refs_0_) | copy-start | bytes 319492
  1.6 12.3 %collective-permute-start.1 = (bf16[208,256]{1,0:T(8,128)(2,1)}, bf16[208,256]{1,0:T(8,128)(2,1)S(1)}, u32[]{:S(2)}, u32[]{:S(2)}) collective-permute-start(bf16[208,256]{1,0:T(8,128)(2,1)} %get-tuple-element.26.refs_0_), channel_id=1, source_target_pairs={{0,2},{1,3},{2,0},{3,1},{4,6},{5,7},{6,4},{7,5},{8,10},{9,11},{10,... | collective-permute-start | bytes 319496 | tf_op jit(solution)/shard_map/ppermute | solution.py:359
  4.7 11.3 %collective-permute-start.3 = (bf16[208,256]{1,0:T(8,128)(2,1)}, bf16[208,256]{1,0:T(8,128)(2,1)S(1)}, u32[]{:S(2)}, u32[]{:S(2)}) collective-permute-start(bf16[208,256]{1,0:T(8,128)(2,1)} %get-tuple-element.26.refs_0_), channel_id=1, source_target_pairs={{0,4},{1,5},{2,6},{3,7},{4,0},{5,1},{6,2},{7,3},{8,12},{9,13},{10,... | collective-permute-start | bytes 319496 | tf_op jit(solution)/shard_map/ppermute | solution.py:359
  7.3 8.7 %collective-permute-start.5 = (bf16[208,256]{1,0:T(8,128)(2,1)}, bf16[208,256]{1,0:T(8,128)(2,1)S(1)}, u32[]{:S(2)}, u32[]{:S(2)}) collective-permute-start(bf16[208,256]{1,0:T(8,128)(2,1)} %get-tuple-element.26.refs_0_), channel_id=1, source_target_pairs={{0,6},{1,7},{2,4},{3,5},{4,2},{5,3},{6,0},{7,1},{8,14},{9,15},{10,... | collective-permute-start | bytes 319496 | tf_op jit(solution)/shard_map/ppermute | solution.py:359
  7.3 0.7 %copy-start.1 = (s32[1,256]{1,0:T(1,128)S(1)}, s32[1,256]{1,0:T(1,128)}, u32[]{:S(2)}) copy-start(s32[1,256]{1,0:T(1,128)} %get-tuple-element.27.list_ref) | copy-start | bytes 3076
  10.7 5.8 %collective-permute-start.6 = (bf16[192,256]{1,0:T(8,128)(2,1)S(1)}, bf16[192,256]{1,0:T(8,128)(2,1)S(1)}, u32[]{:S(2)}, u32[]{:S(2)}) collective-permute-start(bf16[192,256]{1,0:T(8,128)(2,1)S(1)} %shard_map.47.refs_4_.refs_1_), channel_id=1, source_target_pairs={{0,8},{8,0},{16,24},{24,16},{1,9},{9,1},{17,25},{25,17},{2,10},{10... | collective-permute-start | bytes 294920 | tf_op jit(solution)/shard_map/ppermute | solution.py:359
  12.4 4.6 %collective-permute-start.7 = (bf16[192,256]{1,0:T(8,128)(2,1)S(1)}, bf16[192,256]{1,0:T(8,128)(2,1)S(1)}, u32[]{:S(2)}, u32[]{:S(2)}) collective-permute-start(bf16[192,256]{1,0:T(8,128)(2,1)S(1)} %shard_map.47.refs_4_.refs_1_), channel_id=1, source_target_pairs={{0,16},{8,24},{16,0},{24,8},{1,17},{9,25},{17,1},{25,9},{2,18},{10... | collective-permute-start | bytes 294920 | tf_op jit(solution)/shard_map/ppermute | solution.py:359
  14.0 5.1 %collective-permute-start = (bf16[208,256]{1,0:T(8,128)(2,1)S(1)}, bf16[208,256]{1,0:T(8,128)(2,1)S(1)}, u32[]{:S(2)}, u32[]{:S(2)}) collective-permute-start(bf16[208,256]{1,0:T(8,128)(2,1)S(1)} %copy-done), channel_id=1, source_target_pairs={{0,1},{1,0},{2,3},{3,2},{4,5},{5,4},{6,7},{7,6},{8,9},{9,8},{10,11... | collective-permute-start | bytes 319496 | tf_op jit(solution)/shard_map/ppermute | solution.py:359
  16.0 3.1 %collective-permute-start.2 = (bf16[208,256]{1,0:T(8,128)(2,1)S(1)}, bf16[208,256]{1,0:T(8,128)(2,1)S(1)}, u32[]{:S(2)}, u32[]{:S(2)}) collective-permute-start(bf16[208,256]{1,0:T(8,128)(2,1)S(1)} %collective-permute-done.1.refs_2_), channel_id=1, source_target_pairs={{0,1},{1,0},{2,3},{3,2},{4,5},{5,4},{6,7},{7,6},{8,9},{9,8},{10,11... | collective-permute-start | bytes 319496 | tf_op jit(solution)/shard_map/ppermute | solution.py:359
  16.0 3.0 %collective-permute-start.4 = (bf16[208,256]{1,0:T(8,128)(2,1)S(1)}, bf16[208,256]{1,0:T(8,128)(2,1)S(1)}, u32[]{:S(2)}, u32[]{:S(2)}) collective-permute-start(bf16[208,256]{1,0:T(8,128)(2,1)S(1)} %collective-permute-done.3.refs_4_), channel_id=1, source_target_pairs={{0,1},{1,0},{2,3},{3,2},{4,5},{5,4},{6,7},{7,6},{8,9},{9,8},{10,11... | collective-permute-start | bytes 319496 | tf_op jit(solution)/shard_map/ppermute | solution.py:359
  17.0 2.0 %collective-permute-start.8 = (bf16[208,256]{1,0:T(8,128)(2,1)S(1)}, bf16[208,256]{1,0:T(8,128)(2,1)S(1)}, u32[]{:S(2)}, u32[]{:S(2)}) collective-permute-start(bf16[208,256]{1,0:T(8,128)(2,1)S(1)} %collective-permute-done.5.refs_6_), channel_id=1, source_target_pairs={{0,1},{1,0},{2,3},{3,2},{4,5},{5,4},{6,7},{7,6},{8,9},{9,8},{10,11... | collective-permute-start | bytes 319496 | tf_op jit(solution)/shard_map/ppermute | solution.py:359
  17.1 11.1 %collective-permute-start.12 = (bf16[192,256]{1,0:T(8,128)(2,1)S(1)}, bf16[192,256]{1,0:T(8,128)(2,1)S(1)}, u32[]{:S(2)}, u32[]{:S(2)}) collective-permute-start(bf16[192,256]{1,0:T(8,128)(2,1)S(1)} %shard_map.47.refs_4_.refs_1_), channel_id=1, source_target_pairs={{0,24},{8,16},{16,8},{24,0},{1,25},{9,17},{17,9},{25,1},{2,26},{10... | collective-permute-start | bytes 294920 | tf_op jit(solution)/shard_map/ppermute | solution.py:359
  19.7 8.5 %collective-permute-start.9 = (bf16[192,256]{1,0:T(8,128)(2,1)S(1)}, bf16[192,256]{1,0:T(8,128)(2,1)S(1)}, u32[]{:S(2)}, u32[]{:S(2)}) collective-permute-start(bf16[192,256]{1,0:T(8,128)(2,1)S(1)} %get-tuple-element.31.refs_0_.unit_ref), channel_id=1, source_target_pairs={{0,8},{8,0},{16,24},{24,16},{1,9},{9,1},{17,25},{25,17},{2,10},{10... | collective-permute-start | bytes 294920 | tf_op jit(solution)/shard_map/ppermute | solution.py:359
  20.7 7.4 %collective-permute-start.10 = (bf16[192,256]{1,0:T(8,128)(2,1)S(1)}, bf16[192,256]{1,0:T(8,128)(2,1)S(1)}, u32[]{:S(2)}, u32[]{:S(2)}) collective-permute-start(bf16[192,256]{1,0:T(8,128)(2,1)S(1)} %get-tuple-element.31.refs_0_.unit_ref), channel_id=1, source_target_pairs={{0,16},{8,24},{16,0},{24,8},{1,17},{9,25},{17,1},{25,9},{2,18},{10... | collective-permute-start | bytes 294920 | tf_op jit(solution)/shard_map/ppermute | solution.py:359
  21.5 6.7 %collective-permute-start.11 = (bf16[192,256]{1,0:T(8,128)(2,1)S(1)}, bf16[192,256]{1,0:T(8,128)(2,1)S(1)}, u32[]{:S(2)}, u32[]{:S(2)}) collective-permute-start(bf16[192,256]{1,0:T(8,128)(2,1)S(1)} %get-tuple-element.31.refs_0_.unit_ref), channel_id=1, source_target_pairs={{0,24},{8,16},{16,8},{24,0},{1,25},{9,17},{17,9},{25,1},{2,26},{10... | collective-permute-start | bytes 294920 | tf_op jit(solution)/shard_map/ppermute | solution.py:359
  30.8 3.9 %collective-permute-start.15 = (f32[4,1536]{1,0:T(4,128)S(1)}, f32[4,1536]{1,0:T(4,128)S(1)}, u32[]{:S(2)}, u32[]{:S(2)}) collective-permute-start(f32[4,1536]{1,0:T(4,128)S(1)} %get-tuple-element.39.own_ref), channel_id=1, source_target_pairs={{0,2},{1,3},{2,0},{3,1},{4,6},{5,7},{6,4},{7,5},{8,10},{9,11},{10,... | collective-permute-start | bytes 73736 | tf_op jit(solution)/shard_map/ppermute | solution.py:359
  32.5 4.9 %collective-permute-start.13 = (f32[8,768]{1,0:T(8,128)S(1)}, f32[8,768]{1,0:T(8,128)S(1)}, u32[]{:S(2)}, u32[]{:S(2)}) collective-permute-start(f32[8,768]{1,0:T(8,128)S(1)} %get-tuple-element.38.own_ref), channel_id=1, source_target_pairs={{0,8},{8,0},{16,24},{24,16},{1,9},{9,1},{17,25},{25,17},{2,10},{10... | collective-permute-start | bytes 73736 | tf_op jit(solution)/shard_map/ppermute | solution.py:359
  34.7 4.7 %collective-permute-start.16 = (f32[4,1536]{1,0:T(4,128)S(1)}, f32[4,1536]{1,0:T(4,128)S(1)}, u32[]{:S(2)}, u32[]{:S(2)}) collective-permute-start(f32[4,1536]{1,0:T(4,128)S(1)} %shard_map.53.own_ref), channel_id=1, source_target_pairs={{0,4},{1,5},{2,6},{3,7},{4,0},{5,1},{6,2},{7,3},{8,12},{9,13},{10,... | collective-permute-start | bytes 73736 | tf_op jit(solution)/shard_map/ppermute | solution.py:359
  37.4 3.8 %collective-permute-start.14 = (f32[8,768]{1,0:T(8,128)S(1)}, f32[8,768]{1,0:T(8,128)S(1)}, u32[]{:S(2)}, u32[]{:S(2)}) collective-permute-start(f32[8,768]{1,0:T(8,128)S(1)} %shard_map.51.own_ref), channel_id=1, source_target_pairs={{0,16},{8,24},{16,0},{24,8},{1,17},{9,25},{17,1},{25,9},{2,18},{10... | collective-permute-start | bytes 73736 | tf_op jit(solution)/shard_map/ppermute | solution.py:359
  39.4 1.8 %collective-permute-start.17 = (f32[4,1536]{1,0:T(4,128)S(1)}, f32[4,1536]{1,0:T(4,128)S(1)}, u32[]{:S(2)}, u32[]{:S(2)}) collective-permute-start(f32[4,1536]{1,0:T(4,128)S(1)} %shard_map.54.own_ref), channel_id=1, source_target_pairs={{0,1},{1,0},{2,3},{3,2},{4,5},{5,4},{6,7},{7,6},{8,9},{9,8},{10,11... | collective-permute-start | bytes 73736 | tf_op jit(solution)/shard_map/ppermute | solution.py:359
  43.6 5.3 %collective-permute-start.18 = (bf16[192,256]{1,0:T(8,128)(2,1)S(1)}, bf16[192,256]{1,0:T(8,128)(2,1)S(1)}, u32[]{:S(2)}, u32[]{:S(2)}) collective-permute-start(bf16[192,256]{1,0:T(8,128)(2,1)S(1)} %get-tuple-element.44), channel_id=1, source_target_pairs={{0,8},{8,0},{16,24},{24,16},{1,9},{9,1},{17,25},{25,17},{2,10},{10... | collective-permute-start | bytes 294920 | tf_op jit(solution)/shard_map/ppermute | solution.py:359
  44.2 6.7 %collective-permute-start.19 = (bf16[192,256]{1,0:T(8,128)(2,1)S(1)}, bf16[192,256]{1,0:T(8,128)(2,1)S(1)}, u32[]{:S(2)}, u32[]{:S(2)}) collective-permute-start(bf16[192,256]{1,0:T(8,128)(2,1)S(1)} %get-tuple-element.45), channel_id=1, source_target_pairs={{0,16},{8,24},{16,0},{24,8},{1,17},{9,25},{17,1},{25,9},{2,18},{10... | collective-permute-start | bytes 294920 | tf_op jit(solution)/shard_map/ppermute | solution.py:359
  45.2 5.8 %collective-permute-start.20 = (bf16[192,256]{1,0:T(8,128)(2,1)S(1)}, bf16[192,256]{1,0:T(8,128)(2,1)S(1)}, u32[]{:S(2)}, u32[]{:S(2)}) collective-permute-start(bf16[192,256]{1,0:T(8,128)(2,1)S(1)} %get-tuple-element.46), channel_id=1, source_target_pairs={{0,24},{8,16},{16,8},{24,0},{1,25},{9,17},{17,9},{25,1},{2,26},{10... | collective-permute-start | bytes 294920 | tf_op jit(solution)/shard_map/ppermute | solution.py:359

commit v6 on v5

--- a/solution.py
+++ b/solution.py
@@ -361,7 +361,10 @@
     me = lax.axis_index("col").astype(jnp.int32).reshape(1)
     sent, own_list = call(
         functools.partial(send_kernel, col_count),
-        (shape((per_device + EXTRA, channels), BF16), shape((1, channels), jnp.int32)),
+        (
+            pltpu.VMEM((per_device + EXTRA, channels), BF16),
+            pltpu.VMEM((1, channels), jnp.int32),
+        ),
         (
             lax.axis_index("row").astype(jnp.int32).reshape(1),
             ray_feat,

time: 52 us -> 51.1 us (0.983)
  local copies, waits for them, and re-layouts: 0.68 us -> 0 us
  Pallas kernels: 17 us -> 16.4 us
    unnamed x4 -> x0, local copies, waits for them, and re-layouts: 0.68 us -> none
    pallas_call x13, Pallas kernels: 17 us -> 16.4 us  [call(): pl.pallas_call(kernel, out_shape=out_shape, in_specs=in_specs or [VMEM] *...]
  transfers between devices with their start and end apart: 21 -> 21, of which waited for: 7 -> 7; matrix products, arithmetic and copies ran while one was open for 0% -> 0% of each run, Pallas kernels for 18% -> 19%
where the time goes in v6:
time: 51.1 us; the launch traced here: 50.9 us
  starting transfers between devices  24.4 us (48%)
  Pallas kernels  16.4 us (32%)
  waiting for transfers between devices  10.1 us (20%)
    ppermute x21, starting transfers between devices, flip(): return lax.ppermute(values, axis, pairs)  24.4 us
    pallas_call x13, Pallas kernels, call(): pl.pallas_call(kernel, out_shape=out_shape, in_specs=in_specs or [VMEM] *...  16.4 us
    ppermute x21, waiting for transfers between devices, flip(): return lax.ppermute(values, axis, pairs)  10.1 us
  transfers between devices with their start and end apart: 21, of which 7 were waited for; matrix products, arithmetic and copies ran while one was open for 0% of the time, Pallas kernels for 19%

profile of v6, /device:TPU:0, one launch (start us, length us, event | category | flops | bytes accessed | tf_op | source)
XLA Modules:
  0.0 50.9 jit_solution(15347971554358723100)
XLA Ops:
  0.0 0.9 %shard_map.46 = (bf16[208,256]{1,0:T(8,128)(2,1)S(1)}, s32[1,256]{1,0:T(1,128)S(1)}) custom-call(s32[1]{0:T(128)} %bitcast.1.row_ref, bf16[192,256]{1,0:T(8,128)(2,1)} %feat_ref.1, s32[1,192]{1,0:T(1,128)} %bitcast.4, s32[1,192]{1,0:T(1,128)} %bitcast.5), custom_call_target="tpu_custom_call" | custom-call | tf_op jit(solution)/shard_map/pallas_call | solution.py:339
  1.0 3.1 %collective-permute-start.1 = (bf16[208,256]{1,0:T(8,128)(2,1)S(1)}, bf16[208,256]{1,0:T(8,128)(2,1)S(1)}, u32[]{:S(2)}, u32[]{:S(2)}) collective-permute-start(bf16[208,256]{1,0:T(8,128)(2,1)S(1)} %get-tuple-element.26.refs_0_), channel_id=1, source_target_pairs={{0,2},{1,3},{2,0},{3,1},{4,6},{5,7},{6,4},{7,5},{8,10},{9,11},{10,... | collective-permute-start | bytes 319496 | tf_op jit(solution)/shard_map/ppermute | solution.py:359
  4.0 2.6 %collective-permute-start.3 = (bf16[208,256]{1,0:T(8,128)(2,1)S(1)}, bf16[208,256]{1,0:T(8,128)(2,1)S(1)}, u32[]{:S(2)}, u32[]{:S(2)}) collective-permute-start(bf16[208,256]{1,0:T(8,128)(2,1)S(1)} %get-tuple-element.26.refs_0_), channel_id=1, source_target_pairs={{0,4},{1,5},{2,6},{3,7},{4,0},{5,1},{6,2},{7,3},{8,12},{9,13},{10,... | collective-permute-start | bytes 319496 | tf_op jit(solution)/shard_map/ppermute | solution.py:359
  6.6 2.7 %shard_map.47.refs_4_.refs_1_ = bf16[192,256]{1,0:T(8,128)(2,1)S(1)} custom-call(s32[1,256]{1,0:T(1,128)S(1)} %get-tuple-element.27.list_ref, bf16[8192,256]{1,0:T(8,128)(2,1)} %table_ref.3), custom_call_target="tpu_custom_call" | custom-call | bytes 4194304 | tf_op jit(solution)/shard_map/pallas_call | solution.py:339
  9.3 1.8 %collective-permute-start.6 = (bf16[192,256]{1,0:T(8,128)(2,1)S(1)}, bf16[192,256]{1,0:T(8,128)(2,1)S(1)}, u32[]{:S(2)}, u32[]{:S(2)}) collective-permute-start(bf16[192,256]{1,0:T(8,128)(2,1)S(1)} %shard_map.47.refs_4_.refs_1_), channel_id=1, source_target_pairs={{0,8},{8,0},{16,24},{24,16},{1,9},{9,1},{17,25},{25,17},{2,10},{10... | collective-permute-start | bytes 294920 | tf_op jit(solution)/shard_map/ppermute | solution.py:359
  11.1 1.5 %collective-permute-start.7 = (bf16[192,256]{1,0:T(8,128)(2,1)S(1)}, bf16[192,256]{1,0:T(8,128)(2,1)S(1)}, u32[]{:S(2)}, u32[]{:S(2)}) collective-permute-start(bf16[192,256]{1,0:T(8,128)(2,1)S(1)} %shard_map.47.refs_4_.refs_1_), channel_id=1, source_target_pairs={{0,16},{8,24},{16,0},{24,8},{1,17},{9,25},{17,1},{25,9},{2,18},{10... | collective-permute-start | bytes 294920 | tf_op jit(solution)/shard_map/ppermute | solution.py:359
  12.6 2.5 %collective-permute-done.3.refs_4_ = bf16[208,256]{1,0:T(8,128)(2,1)S(1)} collective-permute-done((bf16[208,256]{1,0:T(8,128)(2,1)S(1)}, bf16[208,256]{1,0:T(8,128)(2,1)S(1)}, u32[]{:S(2)}, u32[]{:S(2)}) %collective-permute-start.3) | collective-permute-done | bytes 106528 | tf_op jit(solution)/shard_map/ppermute | solution.py:359
  15.7 2.4 %collective-permute-start.12 = (bf16[192,256]{1,0:T(8,128)(2,1)S(1)}, bf16[192,256]{1,0:T(8,128)(2,1)S(1)}, u32[]{:S(2)}, u32[]{:S(2)}) collective-permute-start(bf16[192,256]{1,0:T(8,128)(2,1)S(1)} %shard_map.47.refs_4_.refs_1_), channel_id=1, source_target_pairs={{0,24},{8,16},{16,8},{24,0},{1,25},{9,17},{17,9},{25,1},{2,26},{10... | collective-permute-start | bytes 294920 | tf_op jit(solution)/shard_map/ppermute | solution.py:359
  19.4 1.2 %collective-permute-start.10 = (bf16[192,256]{1,0:T(8,128)(2,1)S(1)}, bf16[192,256]{1,0:T(8,128)(2,1)S(1)}, u32[]{:S(2)}, u32[]{:S(2)}) collective-permute-start(bf16[192,256]{1,0:T(8,128)(2,1)S(1)} %get-tuple-element.31.refs_0_.unit_ref), channel_id=1, source_target_pairs={{0,16},{8,24},{16,0},{24,8},{1,17},{9,25},{17,1},{25,9},{2,18},{10... | collective-permute-start | bytes 294920 | tf_op jit(solution)/shard_map/ppermute | solution.py:359
  20.6 1.7 %collective-permute-start.11 = (bf16[192,256]{1,0:T(8,128)(2,1)S(1)}, bf16[192,256]{1,0:T(8,128)(2,1)S(1)}, u32[]{:S(2)}, u32[]{:S(2)}) collective-permute-start(bf16[192,256]{1,0:T(8,128)(2,1)S(1)} %get-tuple-element.31.refs_0_.unit_ref), channel_id=1, source_target_pairs={{0,24},{8,16},{16,8},{24,0},{1,25},{9,17},{17,9},{25,1},{2,26},{10... | collective-permute-start | bytes 294920 | tf_op jit(solution)/shard_map/ppermute | solution.py:359
  22.3 4.9 %shard_map.49 = (bf16[1536,256]{1,0:T(8,128)(2,1)S(1)}, bf16[1536,256]{1,0:T(8,128)(2,1)S(1)}) custom-call(s32[1,2048]{1,0:T(1,128)S(1)} %get-tuple-element.33.list_ref, bf16[8192,256]{1,0:T(8,128)(2,1)} %table_ref.3, bf16[208,256]{1,0:T(8,128)(2,1)S(1)} %get-tuple-element.26.refs_0_, bf16[208,256]{1,0:T(8,128)(2,1)S(1)} %collective-permute-done.refs_1_, ...), custom_call_target="tpu_custom_call" | custom-call | bytes 4194304 | tf_op jit(solution)/shard_map/pallas_call | solution.py:339
  27.3 2.6 %shard_map.50 = (f32[8,768]{1,0:T(8,128)S(1)}, f32[4,1536]{1,0:T(4,128)S(1)}) custom-call(bf16[1536,256]{1,0:T(8,128)(2,1)S(1)} %get-tuple-element.43.qx_ref, bf16[1536,256]{1,0:T(8,128)(2,1)S(1)} %get-tuple-element.35.qy_ref, bf16[192,256]{1,0:T(8,128)(2,1)S(1)} %get-tuple-element.31.refs_0_.unit_ref, ...), custom_call_target="tpu_custom_call" | custom-call | flops 1207959552 | tf_op jit(solution)/shard_map/pallas_call | solution.py:339
  29.9 1.7 %collective-permute-start.15 = (f32[4,1536]{1,0:T(4,128)S(1)}, f32[4,1536]{1,0:T(4,128)S(1)}, u32[]{:S(2)}, u32[]{:S(2)}) collective-permute-start(f32[4,1536]{1,0:T(4,128)S(1)} %get-tuple-element.39.own_ref), channel_id=1, source_target_pairs={{0,2},{1,3},{2,0},{3,1},{4,6},{5,7},{6,4},{7,5},{8,10},{9,11},{10,... | collective-permute-start | bytes 73736 | tf_op jit(solution)/shard_map/ppermute | solution.py:359
  32.1 1.7 %collective-permute-done.15.other_ref = f32[4,1536]{1,0:T(4,128)S(1)} collective-permute-done((f32[4,1536]{1,0:T(4,128)S(1)}, f32[4,1536]{1,0:T(4,128)S(1)}, u32[]{:S(2)}, u32[]{:S(2)}) %collective-permute-start.15) | collective-permute-done | bytes 24608 | tf_op jit(solution)/shard_map/ppermute | solution.py:359
  33.8 2.6 %collective-permute-start.16 = (f32[4,1536]{1,0:T(4,128)S(1)}, f32[4,1536]{1,0:T(4,128)S(1)}, u32[]{:S(2)}, u32[]{:S(2)}) collective-permute-start(f32[4,1536]{1,0:T(4,128)S(1)} %shard_map.53.own_ref), channel_id=1, source_target_pairs={{0,4},{1,5},{2,6},{3,7},{4,0},{5,1},{6,2},{7,3},{8,12},{9,13},{10,... | collective-permute-start | bytes 73736 | tf_op jit(solution)/shard_map/ppermute | solution.py:359
  37.0 1.5 %collective-permute-done.16.other_ref = f32[4,1536]{1,0:T(4,128)S(1)} collective-permute-done((f32[4,1536]{1,0:T(4,128)S(1)}, f32[4,1536]{1,0:T(4,128)S(1)}, u32[]{:S(2)}, u32[]{:S(2)}) %collective-permute-start.16) | collective-permute-done | bytes 24608 | tf_op jit(solution)/shard_map/ppermute | solution.py:359
  38.6 1.8 %collective-permute-done.14.other_ref = f32[8,768]{1,0:T(8,128)S(1)} collective-permute-done((f32[8,768]{1,0:T(8,128)S(1)}, f32[8,768]{1,0:T(8,128)S(1)}, u32[]{:S(2)}, u32[]{:S(2)}) %collective-permute-start.14) | collective-permute-done | bytes 24608 | tf_op jit(solution)/shard_map/ppermute | solution.py:359
  40.5 2.3 %shard_map.56 = (bf16[192,256]{1,0:T(8,128)(2,1)S(1)}, bf16[192,256]{1,0:T(8,128)(2,1)S(1)}, bf16[192,256]{1,0:T(8,128)(2,1)S(1)}) custom-call(bf16[1536,256]{1,0:T(8,128)(2,1)S(1)} %get-tuple-element.43.qx_ref, bf16[1536,256]{1,0:T(8,128)(2,1)S(1)} %get-tuple-element.35.qy_ref, bf16[192,256]{1,0:T(8,128)(2,1)S(1)} %collective-permute-done.9.refs_1_.refs_0_, ...), custom_call_target="tpu_custom_call" | custom-call | flops 1358954496 | tf_op jit(solution)/shard_map/pallas_call | solution.py:339
  43.3 1.0 %collective-permute-start.19 = (bf16[192,256]{1,0:T(8,128)(2,1)S(1)}, bf16[192,256]{1,0:T(8,128)(2,1)S(1)}, u32[]{:S(2)}, u32[]{:S(2)}) collective-permute-start(bf16[192,256]{1,0:T(8,128)(2,1)S(1)} %get-tuple-element.45), channel_id=1, source_target_pairs={{0,16},{8,24},{16,0},{24,8},{1,17},{9,25},{17,1},{25,9},{2,18},{10... | collective-permute-start | bytes 294920 | tf_op jit(solution)/shard_map/ppermute | solution.py:359
  44.3 2.0 %collective-permute-start.20 = (bf16[192,256]{1,0:T(8,128)(2,1)S(1)}, bf16[192,256]{1,0:T(8,128)(2,1)S(1)}, u32[]{:S(2)}, u32[]{:S(2)}) collective-permute-start(bf16[192,256]{1,0:T(8,128)(2,1)S(1)} %get-tuple-element.46), channel_id=1, source_target_pairs={{0,24},{8,16},{16,8},{24,0},{1,25},{9,17},{17,9},{25,1},{2,26},{10... | collective-permute-start | bytes 294920 | tf_op jit(solution)/shard_map/ppermute | solution.py:359
  46.3 1.3 %shard_map.57.refs_0_ = f32[192,256]{1,0:T(8,128)S(1)} custom-call(bf16[1536,256]{1,0:T(8,128)(2,1)S(1)} %get-tuple-element.43.qx_ref, bf16[1536,256]{1,0:T(8,128)(2,1)S(1)} %get-tuple-element.35.qy_ref, bf16[192,256]{1,0:T(8,128)(2,1)S(1)} %get-tuple-element.31.refs_0_.unit_ref, bf16[192,256]{1,0:T(8,128)(2,1)S(1)} %shard_map.47.refs_4_.refs_1_, ...), custom_call_target="tpu_custom_call" | custom-call | flops 452984832 | tf_op jit(solution)/shard_map/pallas_call | solution.py:339
  47.6 0.9 %collective-permute-done.18.refs_1_ = bf16[192,256]{1,0:T(8,128)(2,1)S(1)} collective-permute-done((bf16[192,256]{1,0:T(8,128)(2,1)S(1)}, bf16[192,256]{1,0:T(8,128)(2,1)S(1)}, u32[]{:S(2)}, u32[]{:S(2)}) %collective-permute-start.18) | collective-permute-done | bytes 98336 | tf_op jit(solution)/shard_map/ppermute | solution.py:359
  48.4 1.6 %collective-permute-done.19.refs_2_ = bf16[192,256]{1,0:T(8,128)(2,1)S(1)} collective-permute-done((bf16[192,256]{1,0:T(8,128)(2,1)S(1)}, bf16[192,256]{1,0:T(8,128)(2,1)S(1)}, u32[]{:S(2)}, u32[]{:S(2)}) %collective-permute-start.19) | collective-permute-done | bytes 98336 | tf_op jit(solution)/shard_map/ppermute | solution.py:359
  50.1 0.9 %shard_map.58 = f32[192,256]{1,0:T(8,128)} custom-call(bf16[192,256]{1,0:T(8,128)(2,1)S(1)} %get-tuple-element.31.refs_0_.unit_ref, f32[192,128]{1,0:T(8,128)S(1)} %get-tuple-element.32.norm_ref, f32[192,256]{1,0:T(8,128)S(1)} %shard_map.57.refs_0_, bf16[192,256]{1,0:T(8,128)(2,1)S(1)} %collective-permute-done.18.refs_1_, ...), custom_call_target="tpu_custom_call" | custom-call | tf_op jit(solution)/shard_map/pallas_call | solution.py:339
  (31 shorter events, 3.7 us)
Async XLA Ops:
  1.0 11.7 %collective-permute-start.1 = (bf16[208,256]{1,0:T(8,128)(2,1)S(1)}, bf16[208,256]{1,0:T(8,128)(2,1)S(1)}, u32[]{:S(2)}, u32[]{:S(2)}) collective-permute-start(bf16[208,256]{1,0:T(8,128)(2,1)S(1)} %get-tuple-element.26.refs_0_), channel_id=1, source_target_pairs={{0,2},{1,3},{2,0},{3,1},{4,6},{5,7},{6,4},{7,5},{8,10},{9,11},{10,... | collective-permute-start | bytes 319496 | tf_op jit(solution)/shard_map/ppermute | solution.py:359
  4.0 11.0 %collective-permute-start.3 = (bf16[208,256]{1,0:T(8,128)(2,1)S(1)}, bf16[208,256]{1,0:T(8,128)(2,1)S(1)}, u32[]{:S(2)}, u32[]{:S(2)}) collective-permute-start(bf16[208,256]{1,0:T(8,128)(2,1)S(1)} %get-tuple-element.26.refs_0_), channel_id=1, source_target_pairs={{0,4},{1,5},{2,6},{3,7},{4,0},{5,1},{6,2},{7,3},{8,12},{9,13},{10,... | collective-permute-start | bytes 319496 | tf_op jit(solution)/shard_map/ppermute | solution.py:359
  6.6 8.5 %collective-permute-start.5 = (bf16[208,256]{1,0:T(8,128)(2,1)S(1)}, bf16[208,256]{1,0:T(8,128)(2,1)S(1)}, u32[]{:S(2)}, u32[]{:S(2)}) collective-permute-start(bf16[208,256]{1,0:T(8,128)(2,1)S(1)} %get-tuple-element.26.refs_0_), channel_id=1, source_target_pairs={{0,6},{1,7},{2,4},{3,5},{4,2},{5,3},{6,0},{7,1},{8,14},{9,15},{10,... | collective-permute-start | bytes 319496 | tf_op jit(solution)/shard_map/ppermute | solution.py:359
  9.3 6.3 %collective-permute-start.6 = (bf16[192,256]{1,0:T(8,128)(2,1)S(1)}, bf16[192,256]{1,0:T(8,128)(2,1)S(1)}, u32[]{:S(2)}, u32[]{:S(2)}) collective-permute-start(bf16[192,256]{1,0:T(8,128)(2,1)S(1)} %shard_map.47.refs_4_.refs_1_), channel_id=1, source_target_pairs={{0,8},{8,0},{16,24},{24,16},{1,9},{9,1},{17,25},{25,17},{2,10},{10... | collective-permute-start | bytes 294920 | tf_op jit(solution)/shard_map/ppermute | solution.py:359
  11.1 4.6 %collective-permute-start.7 = (bf16[192,256]{1,0:T(8,128)(2,1)S(1)}, bf16[192,256]{1,0:T(8,128)(2,1)S(1)}, u32[]{:S(2)}, u32[]{:S(2)}) collective-permute-start(bf16[192,256]{1,0:T(8,128)(2,1)S(1)} %shard_map.47.refs_4_.refs_1_), channel_id=1, source_target_pairs={{0,16},{8,24},{16,0},{24,8},{1,17},{9,25},{17,1},{25,9},{2,18},{10... | collective-permute-start | bytes 294920 | tf_op jit(solution)/shard_map/ppermute | solution.py:359
  12.6 5.5 %collective-permute-start = (bf16[208,256]{1,0:T(8,128)(2,1)S(1)}, bf16[208,256]{1,0:T(8,128)(2,1)S(1)}, u32[]{:S(2)}, u32[]{:S(2)}) collective-permute-start(bf16[208,256]{1,0:T(8,128)(2,1)S(1)} %get-tuple-element.26.refs_0_), channel_id=1, source_target_pairs={{0,1},{1,0},{2,3},{3,2},{4,5},{5,4},{6,7},{7,6},{8,9},{9,8},{10,11... | collective-permute-start | bytes 319496 | tf_op jit(solution)/shard_map/ppermute | solution.py:359
  15.1 3.1 %collective-permute-start.2 = (bf16[208,256]{1,0:T(8,128)(2,1)S(1)}, bf16[208,256]{1,0:T(8,128)(2,1)S(1)}, u32[]{:S(2)}, u32[]{:S(2)}) collective-permute-start(bf16[208,256]{1,0:T(8,128)(2,1)S(1)} %collective-permute-done.1.refs_2_), channel_id=1, source_target_pairs={{0,1},{1,0},{2,3},{3,2},{4,5},{5,4},{6,7},{7,6},{8,9},{9,8},{10,11... | collective-permute-start | bytes 319496 | tf_op jit(solution)/shard_map/ppermute | solution.py:359
  15.1 3.1 %collective-permute-start.4 = (bf16[208,256]{1,0:T(8,128)(2,1)S(1)}, bf16[208,256]{1,0:T(8,128)(2,1)S(1)}, u32[]{:S(2)}, u32[]{:S(2)}) collective-permute-start(bf16[208,256]{1,0:T(8,128)(2,1)S(1)} %collective-permute-done.3.refs_4_), channel_id=1, source_target_pairs={{0,1},{1,0},{2,3},{3,2},{4,5},{5,4},{6,7},{7,6},{8,9},{9,8},{10,11... | collective-permute-start | bytes 319496 | tf_op jit(solution)/shard_map/ppermute | solution.py:359
  15.7 2.4 %collective-permute-start.8 = (bf16[208,256]{1,0:T(8,128)(2,1)S(1)}, bf16[208,256]{1,0:T(8,128)(2,1)S(1)}, u32[]{:S(2)}, u32[]{:S(2)}) collective-permute-start(bf16[208,256]{1,0:T(8,128)(2,1)S(1)} %collective-permute-done.5.refs_6_), channel_id=1, source_target_pairs={{0,1},{1,0},{2,3},{3,2},{4,5},{5,4},{6,7},{7,6},{8,9},{9,8},{10,11... | collective-permute-start | bytes 319496 | tf_op jit(solution)/shard_map/ppermute | solution.py:359
  15.7 11.5 %collective-permute-start.12 = (bf16[192,256]{1,0:T(8,128)(2,1)S(1)}, bf16[192,256]{1,0:T(8,128)(2,1)S(1)}, u32[]{:S(2)}, u32[]{:S(2)}) collective-permute-start(bf16[192,256]{1,0:T(8,128)(2,1)S(1)} %shard_map.47.refs_4_.refs_1_), channel_id=1, source_target_pairs={{0,24},{8,16},{16,8},{24,0},{1,25},{9,17},{17,9},{25,1},{2,26},{10... | collective-permute-start | bytes 294920 | tf_op jit(solution)/shard_map/ppermute | solution.py:359
  18.8 8.5 %collective-permute-start.9 = (bf16[192,256]{1,0:T(8,128)(2,1)S(1)}, bf16[192,256]{1,0:T(8,128)(2,1)S(1)}, u32[]{:S(2)}, u32[]{:S(2)}) collective-permute-start(bf16[192,256]{1,0:T(8,128)(2,1)S(1)} %get-tuple-element.31.refs_0_.unit_ref), channel_id=1, source_target_pairs={{0,8},{8,0},{16,24},{24,16},{1,9},{9,1},{17,25},{25,17},{2,10},{10... | collective-permute-start | bytes 294920 | tf_op jit(solution)/shard_map/ppermute | solution.py:359
  19.4 7.9 %collective-permute-start.10 = (bf16[192,256]{1,0:T(8,128)(2,1)S(1)}, bf16[192,256]{1,0:T(8,128)(2,1)S(1)}, u32[]{:S(2)}, u32[]{:S(2)}) collective-permute-start(bf16[192,256]{1,0:T(8,128)(2,1)S(1)} %get-tuple-element.31.refs_0_.unit_ref), channel_id=1, source_target_pairs={{0,16},{8,24},{16,0},{24,8},{1,17},{9,25},{17,1},{25,9},{2,18},{10... | collective-permute-start | bytes 294920 | tf_op jit(solution)/shard_map/ppermute | solution.py:359
  20.6 6.7 %collective-permute-start.11 = (bf16[192,256]{1,0:T(8,128)(2,1)S(1)}, bf16[192,256]{1,0:T(8,128)(2,1)S(1)}, u32[]{:S(2)}, u32[]{:S(2)}) collective-permute-start(bf16[192,256]{1,0:T(8,128)(2,1)S(1)} %get-tuple-element.31.refs_0_.unit_ref), channel_id=1, source_target_pairs={{0,24},{8,16},{16,8},{24,0},{1,25},{9,17},{17,9},{25,1},{2,26},{10... | collective-permute-start | bytes 294920 | tf_op jit(solution)/shard_map/ppermute | solution.py:359
  29.9 3.9 %collective-permute-start.15 = (f32[4,1536]{1,0:T(4,128)S(1)}, f32[4,1536]{1,0:T(4,128)S(1)}, u32[]{:S(2)}, u32[]{:S(2)}) collective-permute-start(f32[4,1536]{1,0:T(4,128)S(1)} %get-tuple-element.39.own_ref), channel_id=1, source_target_pairs={{0,2},{1,3},{2,0},{3,1},{4,6},{5,7},{6,4},{7,5},{8,10},{9,11},{10,... | collective-permute-start | bytes 73736 | tf_op jit(solution)/shard_map/ppermute | solution.py:359
  31.6 4.9 %collective-permute-start.13 = (f32[8,768]{1,0:T(8,128)S(1)}, f32[8,768]{1,0:T(8,128)S(1)}, u32[]{:S(2)}, u32[]{:S(2)}) collective-permute-start(f32[8,768]{1,0:T(8,128)S(1)} %get-tuple-element.38.own_ref), channel_id=1, source_target_pairs={{0,8},{8,0},{16,24},{24,16},{1,9},{9,1},{17,25},{25,17},{2,10},{10... | collective-permute-start | bytes 73736 | tf_op jit(solution)/shard_map/ppermute | solution.py:359
  33.8 4.7 %collective-permute-start.16 = (f32[4,1536]{1,0:T(4,128)S(1)}, f32[4,1536]{1,0:T(4,128)S(1)}, u32[]{:S(2)}, u32[]{:S(2)}) collective-permute-start(f32[4,1536]{1,0:T(4,128)S(1)} %shard_map.53.own_ref), channel_id=1, source_target_pairs={{0,4},{1,5},{2,6},{3,7},{4,0},{5,1},{6,2},{7,3},{8,12},{9,13},{10,... | collective-permute-start | bytes 73736 | tf_op jit(solution)/shard_map/ppermute | solution.py:359
  36.5 3.8 %collective-permute-start.14 = (f32[8,768]{1,0:T(8,128)S(1)}, f32[8,768]{1,0:T(8,128)S(1)}, u32[]{:S(2)}, u32[]{:S(2)}) collective-permute-start(f32[8,768]{1,0:T(8,128)S(1)} %shard_map.51.own_ref), channel_id=1, source_target_pairs={{0,16},{8,24},{16,0},{24,8},{1,17},{9,25},{17,1},{25,9},{2,18},{10... | collective-permute-start | bytes 73736 | tf_op jit(solution)/shard_map/ppermute | solution.py:359
  38.5 1.8 %collective-permute-start.17 = (f32[4,1536]{1,0:T(4,128)S(1)}, f32[4,1536]{1,0:T(4,128)S(1)}, u32[]{:S(2)}, u32[]{:S(2)}) collective-permute-start(f32[4,1536]{1,0:T(4,128)S(1)} %shard_map.54.own_ref), channel_id=1, source_target_pairs={{0,1},{1,0},{2,3},{3,2},{4,5},{5,4},{6,7},{7,6},{8,9},{9,8},{10,11... | collective-permute-start | bytes 73736 | tf_op jit(solution)/shard_map/ppermute | solution.py:359
  42.7 5.7 %collective-permute-start.18 = (bf16[192,256]{1,0:T(8,128)(2,1)S(1)}, bf16[192,256]{1,0:T(8,128)(2,1)S(1)}, u32[]{:S(2)}, u32[]{:S(2)}) collective-permute-start(bf16[192,256]{1,0:T(8,128)(2,1)S(1)} %get-tuple-element.44), channel_id=1, source_target_pairs={{0,8},{8,0},{16,24},{24,16},{1,9},{9,1},{17,25},{25,17},{2,10},{10... | collective-permute-start | bytes 294920 | tf_op jit(solution)/shard_map/ppermute | solution.py:359
  43.3 6.7 %collective-permute-start.19 = (bf16[192,256]{1,0:T(8,128)(2,1)S(1)}, bf16[192,256]{1,0:T(8,128)(2,1)S(1)}, u32[]{:S(2)}, u32[]{:S(2)}) collective-permute-start(bf16[192,256]{1,0:T(8,128)(2,1)S(1)} %get-tuple-element.45), channel_id=1, source_target_pairs={{0,16},{8,24},{16,0},{24,8},{1,17},{9,25},{17,1},{25,9},{2,18},{10... | collective-permute-start | bytes 294920 | tf_op jit(solution)/shard_map/ppermute | solution.py:359
  44.3 5.8 %collective-permute-start.20 = (bf16[192,256]{1,0:T(8,128)(2,1)S(1)}, bf16[192,256]{1,0:T(8,128)(2,1)S(1)}, u32[]{:S(2)}, u32[]{:S(2)}) collective-permute-start(bf16[192,256]{1,0:T(8,128)(2,1)S(1)} %get-tuple-element.46), channel_id=1, source_target_pairs={{0,24},{8,16},{16,8},{24,0},{1,25},{9,17},{17,9},{25,1},{2,26},{10... | collective-permute-start | bytes 294920 | tf_op jit(solution)/shard_map/ppermute | solution.py:359

commit v7 on v6

--- a/solution.py
+++ b/solution.py
@@ -325,22 +325,31 @@
 
 
 def last_kernel(unit_ref, norm_ref, *refs):
-    parts, out_ref = refs[:-1], refs[-1]
-    gradient = parts[0][...]
-    for part in parts[1:]:
-        gradient = gradient + part[...].astype(F32)
-    unit = unit_ref[...].astype(F32)
-    along = jnp.sum(unit * gradient, axis=1, keepdims=True)
-    out_ref[...] = (gradient - unit * along) / norm_ref[:, :1]
-
-
-def call(kernel, out_shape, args, in_specs=None, scratch=(), mib=16, flops=0, nbytes=0):
+    parts, (out_ref, held_ref, sems) = refs[:-3], refs[-3:]
+    size = out_ref.shape[0] // sems.shape[0]
+    copies = []
+    for i in range(sems.shape[0]):
+        rows = slice(i * size, (i + 1) * size)
+        gradient = parts[0][rows, :]
+        for part in parts[1:]:
+            gradient = gradient + part[rows, :].astype(F32)
+        unit = unit_ref[rows, :].astype(F32)
+        along = jnp.sum(unit * gradient, axis=1, keepdims=True)
+        held_ref[rows, :] = (gradient - unit * along) / norm_ref[rows, :1]
+        at = pl.ds(i * size, size)
+        copies.append(pltpu.make_async_copy(held_ref.at[at, :], out_ref.at[at, :], sems.at[i]))
+        copies[-1].start()
+    for copy in copies:
+        copy.wait()
+
+
+def call(kernel, out_shape, args, in_specs=None, scratch=(), mib=16, flops=0, nbytes=0, out_spec=VMEM):
     many = isinstance(out_shape, (tuple, list))
     return pl.pallas_call(
         kernel,
         out_shape=out_shape,
         in_specs=in_specs or [VMEM] * len(args),
-        out_specs=[VMEM] * len(out_shape) if many else VMEM,
+        out_specs=[out_spec] * len(out_shape) if many else out_spec,
         scratch_shapes=scratch,
         compiler_params=params(mib),
         cost_estimate=pl.CostEstimate(flops=flops, bytes_accessed=nbytes, transcendentals=0),
@@ -472,6 +481,11 @@
         last_kernel,
         shape((per_device, channels), F32),
         (own_unit, own_norm, *partials),
+        scratch=[
+            pltpu.VMEM((per_device, channels), F32),
+            pltpu.SemaphoreType.DMA((math.gcd(per_device // 16, 3),)),
+        ],
+        out_spec=HBM,
     )
 
 

time: 51.1 us -> 51.1 us (level)
  no operation moved by 1% of the time
where the time goes in v7:
time: 51.1 us; the launch traced here: 50.9 us
  starting transfers between devices  24.4 us (48%)
  Pallas kernels  16.4 us (32%)
  waiting for transfers between devices  10.1 us (20%)
    ppermute x21, starting transfers between devices, flip(): return lax.ppermute(values, axis, pairs)  24.4 us
    pallas_call x13, Pallas kernels, call(): pl.pallas_call(kernel, out_shape=out_shape, in_specs=in_specs or [VMEM] *...  16.4 us
    ppermute x21, waiting for transfers between devices, flip(): return lax.ppermute(values, axis, pairs)  10.1 us
  transfers between devices with their start and end apart: 21, of which 7 were waited for; matrix products, arithmetic and copies ran while one was open for 0% of the time, Pallas kernels for 19%

profile of v7, /device:TPU:0, one launch (start us, length us, event | category | flops | bytes accessed | tf_op | source)
XLA Modules:
  0.0 50.9 jit_solution(5874545248128819870)
XLA Ops:
  0.0 0.9 %shard_map.46 = (bf16[208,256]{1,0:T(8,128)(2,1)S(1)}, s32[1,256]{1,0:T(1,128)S(1)}) custom-call(s32[1]{0:T(128)} %bitcast.1.row_ref, bf16[192,256]{1,0:T(8,128)(2,1)} %feat_ref.1, s32[1,192]{1,0:T(1,128)} %bitcast.4, s32[1,192]{1,0:T(1,128)} %bitcast.5), custom_call_target="tpu_custom_call" | custom-call | tf_op jit(solution)/shard_map/pallas_call | solution.py:348
  1.0 3.1 %collective-permute-start.1 = (bf16[208,256]{1,0:T(8,128)(2,1)S(1)}, bf16[208,256]{1,0:T(8,128)(2,1)S(1)}, u32[]{:S(2)}, u32[]{:S(2)}) collective-permute-start(bf16[208,256]{1,0:T(8,128)(2,1)S(1)} %get-tuple-element.26.refs_0_), channel_id=1, source_target_pairs={{0,2},{1,3},{2,0},{3,1},{4,6},{5,7},{6,4},{7,5},{8,10},{9,11},{10,... | collective-permute-start | bytes 319496 | tf_op jit(solution)/shard_map/ppermute | solution.py:368
  4.0 2.6 %collective-permute-start.3 = (bf16[208,256]{1,0:T(8,128)(2,1)S(1)}, bf16[208,256]{1,0:T(8,128)(2,1)S(1)}, u32[]{:S(2)}, u32[]{:S(2)}) collective-permute-start(bf16[208,256]{1,0:T(8,128)(2,1)S(1)} %get-tuple-element.26.refs_0_), channel_id=1, source_target_pairs={{0,4},{1,5},{2,6},{3,7},{4,0},{5,1},{6,2},{7,3},{8,12},{9,13},{10,... | collective-permute-start | bytes 319496 | tf_op jit(solution)/shard_map/ppermute | solution.py:368
  6.6 2.7 %shard_map.47.refs_4_.refs_1_ = bf16[192,256]{1,0:T(8,128)(2,1)S(1)} custom-call(s32[1,256]{1,0:T(1,128)S(1)} %get-tuple-element.27.list_ref, bf16[8192,256]{1,0:T(8,128)(2,1)} %table_ref.3), custom_call_target="tpu_custom_call" | custom-call | bytes 4194304 | tf_op jit(solution)/shard_map/pallas_call | solution.py:348
  9.3 1.8 %collective-permute-start.6 = (bf16[192,256]{1,0:T(8,128)(2,1)S(1)}, bf16[192,256]{1,0:T(8,128)(2,1)S(1)}, u32[]{:S(2)}, u32[]{:S(2)}) collective-permute-start(bf16[192,256]{1,0:T(8,128)(2,1)S(1)} %shard_map.47.refs_4_.refs_1_), channel_id=1, source_target_pairs={{0,8},{8,0},{16,24},{24,16},{1,9},{9,1},{17,25},{25,17},{2,10},{10... | collective-permute-start | bytes 294920 | tf_op jit(solution)/shard_map/ppermute | solution.py:368
  11.1 1.5 %collective-permute-start.7 = (bf16[192,256]{1,0:T(8,128)(2,1)S(1)}, bf16[192,256]{1,0:T(8,128)(2,1)S(1)}, u32[]{:S(2)}, u32[]{:S(2)}) collective-permute-start(bf16[192,256]{1,0:T(8,128)(2,1)S(1)} %shard_map.47.refs_4_.refs_1_), channel_id=1, source_target_pairs={{0,16},{8,24},{16,0},{24,8},{1,17},{9,25},{17,1},{25,9},{2,18},{10... | collective-permute-start | bytes 294920 | tf_op jit(solution)/shard_map/ppermute | solution.py:368
  12.6 2.5 %collective-permute-done.3.refs_4_ = bf16[208,256]{1,0:T(8,128)(2,1)S(1)} collective-permute-done((bf16[208,256]{1,0:T(8,128)(2,1)S(1)}, bf16[208,256]{1,0:T(8,128)(2,1)S(1)}, u32[]{:S(2)}, u32[]{:S(2)}) %collective-permute-start.3) | collective-permute-done | bytes 106528 | tf_op jit(solution)/shard_map/ppermute | solution.py:368
  15.7 2.4 %collective-permute-start.12 = (bf16[192,256]{1,0:T(8,128)(2,1)S(1)}, bf16[192,256]{1,0:T(8,128)(2,1)S(1)}, u32[]{:S(2)}, u32[]{:S(2)}) collective-permute-start(bf16[192,256]{1,0:T(8,128)(2,1)S(1)} %shard_map.47.refs_4_.refs_1_), channel_id=1, source_target_pairs={{0,24},{8,16},{16,8},{24,0},{1,25},{9,17},{17,9},{25,1},{2,26},{10... | collective-permute-start | bytes 294920 | tf_op jit(solution)/shard_map/ppermute | solution.py:368
  19.4 1.2 %collective-permute-start.10 = (bf16[192,256]{1,0:T(8,128)(2,1)S(1)}, bf16[192,256]{1,0:T(8,128)(2,1)S(1)}, u32[]{:S(2)}, u32[]{:S(2)}) collective-permute-start(bf16[192,256]{1,0:T(8,128)(2,1)S(1)} %get-tuple-element.31.refs_0_.unit_ref), channel_id=1, source_target_pairs={{0,16},{8,24},{16,0},{24,8},{1,17},{9,25},{17,1},{25,9},{2,18},{10... | collective-permute-start | bytes 294920 | tf_op jit(solution)/shard_map/ppermute | solution.py:368
  20.6 1.7 %collective-permute-start.11 = (bf16[192,256]{1,0:T(8,128)(2,1)S(1)}, bf16[192,256]{1,0:T(8,128)(2,1)S(1)}, u32[]{:S(2)}, u32[]{:S(2)}) collective-permute-start(bf16[192,256]{1,0:T(8,128)(2,1)S(1)} %get-tuple-element.31.refs_0_.unit_ref), channel_id=1, source_target_pairs={{0,24},{8,16},{16,8},{24,0},{1,25},{9,17},{17,9},{25,1},{2,26},{10... | collective-permute-start | bytes 294920 | tf_op jit(solution)/shard_map/ppermute | solution.py:368
  22.3 4.9 %shard_map.49 = (bf16[1536,256]{1,0:T(8,128)(2,1)S(1)}, bf16[1536,256]{1,0:T(8,128)(2,1)S(1)}) custom-call(s32[1,2048]{1,0:T(1,128)S(1)} %get-tuple-element.33.list_ref, bf16[8192,256]{1,0:T(8,128)(2,1)} %table_ref.3, bf16[208,256]{1,0:T(8,128)(2,1)S(1)} %get-tuple-element.26.refs_0_, bf16[208,256]{1,0:T(8,128)(2,1)S(1)} %collective-permute-done.refs_1_, ...), custom_call_target="tpu_custom_call" | custom-call | bytes 4194304 | tf_op jit(solution)/shard_map/pallas_call | solution.py:348
  27.3 2.6 %shard_map.50 = (f32[8,768]{1,0:T(8,128)S(1)}, f32[4,1536]{1,0:T(4,128)S(1)}) custom-call(bf16[1536,256]{1,0:T(8,128)(2,1)S(1)} %get-tuple-element.43.qx_ref, bf16[1536,256]{1,0:T(8,128)(2,1)S(1)} %get-tuple-element.35.qy_ref, bf16[192,256]{1,0:T(8,128)(2,1)S(1)} %get-tuple-element.31.refs_0_.unit_ref, ...), custom_call_target="tpu_custom_call" | custom-call | flops 1207959552 | tf_op jit(solution)/shard_map/pallas_call | solution.py:348
  29.9 1.7 %collective-permute-start.15 = (f32[4,1536]{1,0:T(4,128)S(1)}, f32[4,1536]{1,0:T(4,128)S(1)}, u32[]{:S(2)}, u32[]{:S(2)}) collective-permute-start(f32[4,1536]{1,0:T(4,128)S(1)} %get-tuple-element.39.own_ref), channel_id=1, source_target_pairs={{0,2},{1,3},{2,0},{3,1},{4,6},{5,7},{6,4},{7,5},{8,10},{9,11},{10,... | collective-permute-start | bytes 73736 | tf_op jit(solution)/shard_map/ppermute | solution.py:368
  32.1 1.7 %collective-permute-done.15.other_ref = f32[4,1536]{1,0:T(4,128)S(1)} collective-permute-done((f32[4,1536]{1,0:T(4,128)S(1)}, f32[4,1536]{1,0:T(4,128)S(1)}, u32[]{:S(2)}, u32[]{:S(2)}) %collective-permute-start.15) | collective-permute-done | bytes 24608 | tf_op jit(solution)/shard_map/ppermute | solution.py:368
  33.8 2.6 %collective-permute-start.16 = (f32[4,1536]{1,0:T(4,128)S(1)}, f32[4,1536]{1,0:T(4,128)S(1)}, u32[]{:S(2)}, u32[]{:S(2)}) collective-permute-start(f32[4,1536]{1,0:T(4,128)S(1)} %shard_map.53.own_ref), channel_id=1, source_target_pairs={{0,4},{1,5},{2,6},{3,7},{4,0},{5,1},{6,2},{7,3},{8,12},{9,13},{10,... | collective-permute-start | bytes 73736 | tf_op jit(solution)/shard_map/ppermute | solution.py:368
  37.0 1.5 %collective-permute-done.16.other_ref = f32[4,1536]{1,0:T(4,128)S(1)} collective-permute-done((f32[4,1536]{1,0:T(4,128)S(1)}, f32[4,1536]{1,0:T(4,128)S(1)}, u32[]{:S(2)}, u32[]{:S(2)}) %collective-permute-start.16) | collective-permute-done | bytes 24608 | tf_op jit(solution)/shard_map/ppermute | solution.py:368
  38.6 1.8 %collective-permute-done.14.other_ref = f32[8,768]{1,0:T(8,128)S(1)} collective-permute-done((f32[8,768]{1,0:T(8,128)S(1)}, f32[8,768]{1,0:T(8,128)S(1)}, u32[]{:S(2)}, u32[]{:S(2)}) %collective-permute-start.14) | collective-permute-done | bytes 24608 | tf_op jit(solution)/shard_map/ppermute | solution.py:368
  40.5 2.3 %shard_map.56 = (bf16[192,256]{1,0:T(8,128)(2,1)S(1)}, bf16[192,256]{1,0:T(8,128)(2,1)S(1)}, bf16[192,256]{1,0:T(8,128)(2,1)S(1)}) custom-call(bf16[1536,256]{1,0:T(8,128)(2,1)S(1)} %get-tuple-element.43.qx_ref, bf16[1536,256]{1,0:T(8,128)(2,1)S(1)} %get-tuple-element.35.qy_ref, bf16[192,256]{1,0:T(8,128)(2,1)S(1)} %collective-permute-done.9.refs_1_.refs_0_, ...), custom_call_target="tpu_custom_call" | custom-call | flops 1358954496 | tf_op jit(solution)/shard_map/pallas_call | solution.py:348
  43.3 1.0 %collective-permute-start.19 = (bf16[192,256]{1,0:T(8,128)(2,1)S(1)}, bf16[192,256]{1,0:T(8,128)(2,1)S(1)}, u32[]{:S(2)}, u32[]{:S(2)}) collective-permute-start(bf16[192,256]{1,0:T(8,128)(2,1)S(1)} %get-tuple-element.45), channel_id=1, source_target_pairs={{0,16},{8,24},{16,0},{24,8},{1,17},{9,25},{17,1},{25,9},{2,18},{10... | collective-permute-start | bytes 294920 | tf_op jit(solution)/shard_map/ppermute | solution.py:368
  44.3 2.0 %collective-permute-start.20 = (bf16[192,256]{1,0:T(8,128)(2,1)S(1)}, bf16[192,256]{1,0:T(8,128)(2,1)S(1)}, u32[]{:S(2)}, u32[]{:S(2)}) collective-permute-start(bf16[192,256]{1,0:T(8,128)(2,1)S(1)} %get-tuple-element.46), channel_id=1, source_target_pairs={{0,24},{8,16},{16,8},{24,0},{1,25},{9,17},{17,9},{25,1},{2,26},{10... | collective-permute-start | bytes 294920 | tf_op jit(solution)/shard_map/ppermute | solution.py:368
  46.3 1.3 %shard_map.57.refs_0_ = f32[192,256]{1,0:T(8,128)S(1)} custom-call(bf16[1536,256]{1,0:T(8,128)(2,1)S(1)} %get-tuple-element.43.qx_ref, bf16[1536,256]{1,0:T(8,128)(2,1)S(1)} %get-tuple-element.35.qy_ref, bf16[192,256]{1,0:T(8,128)(2,1)S(1)} %get-tuple-element.31.refs_0_.unit_ref, bf16[192,256]{1,0:T(8,128)(2,1)S(1)} %shard_map.47.refs_4_.refs_1_, ...), custom_call_target="tpu_custom_call" | custom-call | flops 452984832 | tf_op jit(solution)/shard_map/pallas_call | solution.py:348
  47.6 0.9 %collective-permute-done.18.refs_1_ = bf16[192,256]{1,0:T(8,128)(2,1)S(1)} collective-permute-done((bf16[192,256]{1,0:T(8,128)(2,1)S(1)}, bf16[192,256]{1,0:T(8,128)(2,1)S(1)}, u32[]{:S(2)}, u32[]{:S(2)}) %collective-permute-start.18) | collective-permute-done | bytes 98336 | tf_op jit(solution)/shard_map/ppermute | solution.py:368
  48.4 1.6 %collective-permute-done.19.refs_2_ = bf16[192,256]{1,0:T(8,128)(2,1)S(1)} collective-permute-done((bf16[192,256]{1,0:T(8,128)(2,1)S(1)}, bf16[192,256]{1,0:T(8,128)(2,1)S(1)}, u32[]{:S(2)}, u32[]{:S(2)}) %collective-permute-start.19) | collective-permute-done | bytes 98336 | tf_op jit(solution)/shard_map/ppermute | solution.py:368
  50.1 0.9 %shard_map.58 = f32[192,256]{1,0:T(8,128)} custom-call(bf16[192,256]{1,0:T(8,128)(2,1)S(1)} %get-tuple-element.31.refs_0_.unit_ref, f32[192,128]{1,0:T(8,128)S(1)} %get-tuple-element.32.norm_ref, f32[192,256]{1,0:T(8,128)S(1)} %shard_map.57.refs_0_, bf16[192,256]{1,0:T(8,128)(2,1)S(1)} %collective-permute-done.18.refs_1_, ...), custom_call_target="tpu_custom_call" | custom-call | tf_op jit(solution)/shard_map/pallas_call | solution.py:348
  (31 shorter events, 3.7 us)
Async XLA Ops:
  1.0 11.7 %collective-permute-start.1 = (bf16[208,256]{1,0:T(8,128)(2,1)S(1)}, bf16[208,256]{1,0:T(8,128)(2,1)S(1)}, u32[]{:S(2)}, u32[]{:S(2)}) collective-permute-start(bf16[208,256]{1,0:T(8,128)(2,1)S(1)} %get-tuple-element.26.refs_0_), channel_id=1, source_target_pairs={{0,2},{1,3},{2,0},{3,1},{4,6},{5,7},{6,4},{7,5},{8,10},{9,11},{10,... | collective-permute-start | bytes 319496 | tf_op jit(solution)/shard_map/ppermute | solution.py:368
  4.0 11.0 %collective-permute-start.3 = (bf16[208,256]{1,0:T(8,128)(2,1)S(1)}, bf16[208,256]{1,0:T(8,128)(2,1)S(1)}, u32[]{:S(2)}, u32[]{:S(2)}) collective-permute-start(bf16[208,256]{1,0:T(8,128)(2,1)S(1)} %get-tuple-element.26.refs_0_), channel_id=1, source_target_pairs={{0,4},{1,5},{2,6},{3,7},{4,0},{5,1},{6,2},{7,3},{8,12},{9,13},{10,... | collective-permute-start | bytes 319496 | tf_op jit(solution)/shard_map/ppermute | solution.py:368
  6.6 8.5 %collective-permute-start.5 = (bf16[208,256]{1,0:T(8,128)(2,1)S(1)}, bf16[208,256]{1,0:T(8,128)(2,1)S(1)}, u32[]{:S(2)}, u32[]{:S(2)}) collective-permute-start(bf16[208,256]{1,0:T(8,128)(2,1)S(1)} %get-tuple-element.26.refs_0_), channel_id=1, source_target_pairs={{0,6},{1,7},{2,4},{3,5},{4,2},{5,3},{6,0},{7,1},{8,14},{9,15},{10,... | collective-permute-start | bytes 319496 | tf_op jit(solution)/shard_map/ppermute | solution.py:368
  9.3 6.3 %collective-permute-start.6 = (bf16[192,256]{1,0:T(8,128)(2,1)S(1)}, bf16[192,256]{1,0:T(8,128)(2,1)S(1)}, u32[]{:S(2)}, u32[]{:S(2)}) collective-permute-start(bf16[192,256]{1,0:T(8,128)(2,1)S(1)} %shard_map.47.refs_4_.refs_1_), channel_id=1, source_target_pairs={{0,8},{8,0},{16,24},{24,16},{1,9},{9,1},{17,25},{25,17},{2,10},{10... | collective-permute-start | bytes 294920 | tf_op jit(solution)/shard_map/ppermute | solution.py:368
  11.1 4.6 %collective-permute-start.7 = (bf16[192,256]{1,0:T(8,128)(2,1)S(1)}, bf16[192,256]{1,0:T(8,128)(2,1)S(1)}, u32[]{:S(2)}, u32[]{:S(2)}) collective-permute-start(bf16[192,256]{1,0:T(8,128)(2,1)S(1)} %shard_map.47.refs_4_.refs_1_), channel_id=1, source_target_pairs={{0,16},{8,24},{16,0},{24,8},{1,17},{9,25},{17,1},{25,9},{2,18},{10... | collective-permute-start | bytes 294920 | tf_op jit(solution)/shard_map/ppermute | solution.py:368
  12.6 5.5 %collective-permute-start = (bf16[208,256]{1,0:T(8,128)(2,1)S(1)}, bf16[208,256]{1,0:T(8,128)(2,1)S(1)}, u32[]{:S(2)}, u32[]{:S(2)}) collective-permute-start(bf16[208,256]{1,0:T(8,128)(2,1)S(1)} %get-tuple-element.26.refs_0_), channel_id=1, source_target_pairs={{0,1},{1,0},{2,3},{3,2},{4,5},{5,4},{6,7},{7,6},{8,9},{9,8},{10,11... | collective-permute-start | bytes 319496 | tf_op jit(solution)/shard_map/ppermute | solution.py:368
  15.1 3.1 %collective-permute-start.2 = (bf16[208,256]{1,0:T(8,128)(2,1)S(1)}, bf16[208,256]{1,0:T(8,128)(2,1)S(1)}, u32[]{:S(2)}, u32[]{:S(2)}) collective-permute-start(bf16[208,256]{1,0:T(8,128)(2,1)S(1)} %collective-permute-done.1.refs_2_), channel_id=1, source_target_pairs={{0,1},{1,0},{2,3},{3,2},{4,5},{5,4},{6,7},{7,6},{8,9},{9,8},{10,11... | collective-permute-start | bytes 319496 | tf_op jit(solution)/shard_map/ppermute | solution.py:368
  15.1 3.1 %collective-permute-start.4 = (bf16[208,256]{1,0:T(8,128)(2,1)S(1)}, bf16[208,256]{1,0:T(8,128)(2,1)S(1)}, u32[]{:S(2)}, u32[]{:S(2)}) collective-permute-start(bf16[208,256]{1,0:T(8,128)(2,1)S(1)} %collective-permute-done.3.refs_4_), channel_id=1, source_target_pairs={{0,1},{1,0},{2,3},{3,2},{4,5},{5,4},{6,7},{7,6},{8,9},{9,8},{10,11... | collective-permute-start | bytes 319496 | tf_op jit(solution)/shard_map/ppermute | solution.py:368
  15.7 2.4 %collective-permute-start.8 = (bf16[208,256]{1,0:T(8,128)(2,1)S(1)}, bf16[208,256]{1,0:T(8,128)(2,1)S(1)}, u32[]{:S(2)}, u32[]{:S(2)}) collective-permute-start(bf16[208,256]{1,0:T(8,128)(2,1)S(1)} %collective-permute-done.5.refs_6_), channel_id=1, source_target_pairs={{0,1},{1,0},{2,3},{3,2},{4,5},{5,4},{6,7},{7,6},{8,9},{9,8},{10,11... | collective-permute-start | bytes 319496 | tf_op jit(solution)/shard_map/ppermute | solution.py:368
  15.7 11.5 %collective-permute-start.12 = (bf16[192,256]{1,0:T(8,128)(2,1)S(1)}, bf16[192,256]{1,0:T(8,128)(2,1)S(1)}, u32[]{:S(2)}, u32[]{:S(2)}) collective-permute-start(bf16[192,256]{1,0:T(8,128)(2,1)S(1)} %shard_map.47.refs_4_.refs_1_), channel_id=1, source_target_pairs={{0,24},{8,16},{16,8},{24,0},{1,25},{9,17},{17,9},{25,1},{2,26},{10... | collective-permute-start | bytes 294920 | tf_op jit(solution)/shard_map/ppermute | solution.py:368
  18.8 8.5 %collective-permute-start.9 = (bf16[192,256]{1,0:T(8,128)(2,1)S(1)}, bf16[192,256]{1,0:T(8,128)(2,1)S(1)}, u32[]{:S(2)}, u32[]{:S(2)}) collective-permute-start(bf16[192,256]{1,0:T(8,128)(2,1)S(1)} %get-tuple-element.31.refs_0_.unit_ref), channel_id=1, source_target_pairs={{0,8},{8,0},{16,24},{24,16},{1,9},{9,1},{17,25},{25,17},{2,10},{10... | collective-permute-start | bytes 294920 | tf_op jit(solution)/shard_map/ppermute | solution.py:368
  19.4 7.9 %collective-permute-start.10 = (bf16[192,256]{1,0:T(8,128)(2,1)S(1)}, bf16[192,256]{1,0:T(8,128)(2,1)S(1)}, u32[]{:S(2)}, u32[]{:S(2)}) collective-permute-start(bf16[192,256]{1,0:T(8,128)(2,1)S(1)} %get-tuple-element.31.refs_0_.unit_ref), channel_id=1, source_target_pairs={{0,16},{8,24},{16,0},{24,8},{1,17},{9,25},{17,1},{25,9},{2,18},{10... | collective-permute-start | bytes 294920 | tf_op jit(solution)/shard_map/ppermute | solution.py:368
  20.6 6.7 %collective-permute-start.11 = (bf16[192,256]{1,0:T(8,128)(2,1)S(1)}, bf16[192,256]{1,0:T(8,128)(2,1)S(1)}, u32[]{:S(2)}, u32[]{:S(2)}) collective-permute-start(bf16[192,256]{1,0:T(8,128)(2,1)S(1)} %get-tuple-element.31.refs_0_.unit_ref), channel_id=1, source_target_pairs={{0,24},{8,16},{16,8},{24,0},{1,25},{9,17},{17,9},{25,1},{2,26},{10... | collective-permute-start | bytes 294920 | tf_op jit(solution)/shard_map/ppermute | solution.py:368
  29.9 3.9 %collective-permute-start.15 = (f32[4,1536]{1,0:T(4,128)S(1)}, f32[4,1536]{1,0:T(4,128)S(1)}, u32[]{:S(2)}, u32[]{:S(2)}) collective-permute-start(f32[4,1536]{1,0:T(4,128)S(1)} %get-tuple-element.39.own_ref), channel_id=1, source_target_pairs={{0,2},{1,3},{2,0},{3,1},{4,6},{5,7},{6,4},{7,5},{8,10},{9,11},{10,... | collective-permute-start | bytes 73736 | tf_op jit(solution)/shard_map/ppermute | solution.py:368
  31.6 4.9 %collective-permute-start.13 = (f32[8,768]{1,0:T(8,128)S(1)}, f32[8,768]{1,0:T(8,128)S(1)}, u32[]{:S(2)}, u32[]{:S(2)}) collective-permute-start(f32[8,768]{1,0:T(8,128)S(1)} %get-tuple-element.38.own_ref), channel_id=1, source_target_pairs={{0,8},{8,0},{16,24},{24,16},{1,9},{9,1},{17,25},{25,17},{2,10},{10... | collective-permute-start | bytes 73736 | tf_op jit(solution)/shard_map/ppermute | solution.py:368
  33.8 4.7 %collective-permute-start.16 = (f32[4,1536]{1,0:T(4,128)S(1)}, f32[4,1536]{1,0:T(4,128)S(1)}, u32[]{:S(2)}, u32[]{:S(2)}) collective-permute-start(f32[4,1536]{1,0:T(4,128)S(1)} %shard_map.53.own_ref), channel_id=1, source_target_pairs={{0,4},{1,5},{2,6},{3,7},{4,0},{5,1},{6,2},{7,3},{8,12},{9,13},{10,... | collective-permute-start | bytes 73736 | tf_op jit(solution)/shard_map/ppermute | solution.py:368
  36.5 3.8 %collective-permute-start.14 = (f32[8,768]{1,0:T(8,128)S(1)}, f32[8,768]{1,0:T(8,128)S(1)}, u32[]{:S(2)}, u32[]{:S(2)}) collective-permute-start(f32[8,768]{1,0:T(8,128)S(1)} %shard_map.51.own_ref), channel_id=1, source_target_pairs={{0,16},{8,24},{16,0},{24,8},{1,17},{9,25},{17,1},{25,9},{2,18},{10... | collective-permute-start | bytes 73736 | tf_op jit(solution)/shard_map/ppermute | solution.py:368
  38.5 1.8 %collective-permute-start.17 = (f32[4,1536]{1,0:T(4,128)S(1)}, f32[4,1536]{1,0:T(4,128)S(1)}, u32[]{:S(2)}, u32[]{:S(2)}) collective-permute-start(f32[4,1536]{1,0:T(4,128)S(1)} %shard_map.54.own_ref), channel_id=1, source_target_pairs={{0,1},{1,0},{2,3},{3,2},{4,5},{5,4},{6,7},{7,6},{8,9},{9,8},{10,11... | collective-permute-start | bytes 73736 | tf_op jit(solution)/shard_map/ppermute | solution.py:368
  42.7 5.7 %collective-permute-start.18 = (bf16[192,256]{1,0:T(8,128)(2,1)S(1)}, bf16[192,256]{1,0:T(8,128)(2,1)S(1)}, u32[]{:S(2)}, u32[]{:S(2)}) collective-permute-start(bf16[192,256]{1,0:T(8,128)(2,1)S(1)} %get-tuple-element.44), channel_id=1, source_target_pairs={{0,8},{8,0},{16,24},{24,16},{1,9},{9,1},{17,25},{25,17},{2,10},{10... | collective-permute-start | bytes 294920 | tf_op jit(solution)/shard_map/ppermute | solution.py:368
  43.3 6.7 %collective-permute-start.19 = (bf16[192,256]{1,0:T(8,128)(2,1)S(1)}, bf16[192,256]{1,0:T(8,128)(2,1)S(1)}, u32[]{:S(2)}, u32[]{:S(2)}) collective-permute-start(bf16[192,256]{1,0:T(8,128)(2,1)S(1)} %get-tuple-element.45), channel_id=1, source_target_pairs={{0,16},{8,24},{16,0},{24,8},{1,17},{9,25},{17,1},{25,9},{2,18},{10... | collective-permute-start | bytes 294920 | tf_op jit(solution)/shard_map/ppermute | solution.py:368
  44.3 5.8 %collective-permute-start.20 = (bf16[192,256]{1,0:T(8,128)(2,1)S(1)}, bf16[192,256]{1,0:T(8,128)(2,1)S(1)}, u32[]{:S(2)}, u32[]{:S(2)}) collective-permute-start(bf16[192,256]{1,0:T(8,128)(2,1)S(1)} %get-tuple-element.46), channel_id=1, source_target_pairs={{0,24},{8,16},{16,8},{24,0},{1,25},{9,17},{17,9},{25,1},{2,26},{10... | collective-permute-start | bytes 294920 | tf_op jit(solution)/shard_map/ppermute | solution.py:368
